TPU v7x, 32 devices: a whole 2x2x4 slice. The times are simulated.
32 devices in a mesh: tok: 8 (over y, x, core), feat: 4 (over z).
Axes of the slice: x: 2, y: 2, z: 4, core: 2. Of those that a mesh axis runs over, the one named last changes fastest.
Arguments:
- inputs: bfloat16 [2048, 2048], P(('tok', 'feat'))
- norm_gain: float32 [2048], replicated, may hold values from 0.1 to 1.9
- w_in: bfloat16 [512, 8192], P('tok', 'feat'), may hold values from -0.25 to 0.25
- w_out: bfloat16 [512, 8192], P('tok', 'feat'), may hold values from -0.125 to 0.125
- block_index: int32 [64, 4], P('feat'), may hold values from 0 to 15, all different within a row
- segment_ids: int32 [2048], P(('tok', 'feat')), may hold values from 0 to 127, never falling along the last dimension, each value on 1 to 24 neighbouring positions
- teacher_scores: float32 [128], replicated, may hold values from -6 to 6
- upstream: bfloat16 [2048, 2048], P(('tok', 'feat')), may hold values from -6 to 6
- readout: float32 [2048], replicated, may hold values from -0.125 to 0.125
Outputs:
- layer_out: bfloat16 [2048, 2048], P(('tok', 'feat'))
- input_grad: bfloat16 [2048, 2048], P(('tok', 'feat'))
- grad_in: float32 [512, 8192], P('tok', 'feat')
- grad_out: float32 [512, 8192], P('tok', 'feat')
Inputs may be any that keep to these rules, and one draw needn't show every extreme that they name: `block_index`: each row names 4 different feature blocks; every feature block is named by some row. `segment_ids`: never falls along the tokens; every segment 0 to 127 holds 1 to 24 tokens.
All inputs are finite; a program needn't handle non-finite values.
Results may differ from a plain program's by a relative error of at most 0.015.
Values may be sent and summed in bfloat16 or wider, within the bound.
No kernel may reach another device: no remote copies, remote signals or barrier semaphores. Data moves between devices by JAX's collectives and lax.ppermute only.
A program may use at most 128 MiB of HBM per device.

v0:
```python
import math

import jax
import jax.numpy as jnp
from jax import lax
from jax.sharding import PartitionSpec as P

BLK = 128


EPS = 1e-06
LOSS_WEIGHT = 8.0


def gelu_tanh(values):
    return jax.nn.gelu(values, approximate=True)


def gelu_back(values, cotangent):
    return jax.vjp(gelu_tanh, values)[1](cotangent)[0]


def on_device(
    inputs, norm_gain, w_in, w_out, block_index, segment_ids, teacher_scores, upstream, readout
):
    local_tokens, model_width = inputs.shape
    blocks_here = w_in.shape[1] // BLK
    feature_blocks = model_width // BLK
    per_hidden = block_index.shape[1]
    total_tokens = local_tokens * lax.axis_size("tok") * lax.axis_size("feat")
    grad_scale = 1.0 / math.sqrt(total_tokens)
    inputs_wide = inputs.astype(jnp.float32)
    mean_square = jnp.mean(inputs_wide * inputs_wide, axis=1, keepdims=True)
    inv_rms = lax.rsqrt(mean_square + EPS)
    normed = (inputs_wide * inv_rms * norm_gain[None, :]).astype(jnp.bfloat16)
    w_in_all, w_out_all = (
        lax.all_gather(w_in, "tok", axis=0, tiled=True),
        lax.all_gather(w_out, "tok", axis=0, tiled=True),
    )
    picked_width = w_in_all.shape[0]
    w_in_blocks = w_in_all.reshape(picked_width, blocks_here, BLK)
    w_out_blocks = w_out_all.reshape(picked_width, blocks_here, BLK)
    normed_rows = lax.all_gather(normed, "feat", axis=0, tiled=True)
    group_rows = normed_rows.shape[0]
    one_hot = block_index[:, :, None] == jnp.arange(feature_blocks, dtype=jnp.int32)[None, None, :]
    sel_half = one_hot.astype(jnp.bfloat16)
    sel_wide = one_hot.astype(jnp.float32)

    def select(rows):
        blocks = rows.reshape(group_rows, feature_blocks, BLK)
        picked = jnp.einsum("rdc,jkd->rjkc", blocks, sel_half, preferred_element_type=jnp.float32)
        return picked.astype(jnp.bfloat16).reshape(group_rows, blocks_here, picked_width)

    def spread(terms):
        grouped = terms.reshape(group_rows, blocks_here, per_hidden, BLK)
        placed = jnp.einsum("rjkc,jkd->rdc", grouped, sel_wide, precision=lax.Precision.HIGHEST)
        return placed.reshape(group_rows, model_width)

    chosen = select(normed_rows)
    pre_act = jnp.einsum("rjm,mjc->rjc", chosen, w_in_blocks, preferred_element_type=jnp.float32)
    activated = gelu_tanh(pre_act).astype(jnp.bfloat16)
    out_terms_fwd = jnp.einsum(
        "rjc,mjc->rjm", activated, w_out_blocks, preferred_element_type=jnp.float32
    )
    branch = lax.psum_scatter(
        spread(out_terms_fwd).astype(jnp.bfloat16), "feat", scatter_dimension=0, tiled=True
    ).astype(jnp.float32)
    layer_out = (inputs_wide + branch).astype(jnp.bfloat16)
    token_score = jnp.dot(layer_out.astype(jnp.float32), readout, precision=lax.Precision.HIGHEST)
    segment_count = teacher_scores.shape[0]
    member = (segment_ids[:, None] == jnp.arange(segment_count, dtype=jnp.int32)[None, :]).astype(
        jnp.float32
    )
    score_sums = jnp.dot(token_score, member, precision=lax.Precision.HIGHEST)
    token_counts = jnp.sum(member, axis=0)
    score_sums, token_counts = lax.psum((score_sums, token_counts), ("tok", "feat"))
    misfit = score_sums / token_counts - teacher_scores
    token_coeff = 2.0 * LOSS_WEIGHT * jnp.sum(member * misfit[None, :], axis=1)
    cotangent_local = (
        upstream.astype(jnp.float32) + token_coeff[:, None] * readout[None, :]
    ).astype(jnp.bfloat16)
    cotangent_rows = lax.all_gather(cotangent_local, "feat", axis=0, tiled=True)
    chosen_grad = select(cotangent_rows)
    upper_grad = jnp.einsum(
        "rjm,mjc->rjc", chosen_grad, w_out_blocks, preferred_element_type=jnp.float32
    )
    pre_grad = gelu_back(pre_act, upper_grad).astype(jnp.bfloat16)

    def arrange(terms):
        return terms.reshape(picked_width, blocks_here * BLK) * grad_scale

    back_terms = jnp.einsum(
        "rjc,mjc->rjm", pre_grad, w_in_blocks, preferred_element_type=jnp.float32
    )
    out_terms = jnp.einsum(
        "rjm,rjc->mjc", chosen_grad, activated, preferred_element_type=jnp.float32
    )
    in_terms = jnp.einsum("rjm,rjc->mjc", chosen, pre_grad, preferred_element_type=jnp.float32)
    grad_out, grad_in = (
        lax.psum_scatter(
            arrange(out_terms).astype(jnp.bfloat16), "tok", scatter_dimension=0, tiled=True
        ).astype(jnp.float32),
        lax.psum_scatter(
            arrange(in_terms).astype(jnp.bfloat16), "tok", scatter_dimension=0, tiled=True
        ).astype(jnp.float32),
    )
    back_sum = lax.psum_scatter(
        spread(back_terms).astype(jnp.bfloat16), "feat", scatter_dimension=0, tiled=True
    ).astype(jnp.float32)
    scaled = back_sum * norm_gain[None, :]
    inner_mean = jnp.mean(scaled * inputs_wide, axis=1, keepdims=True)
    norm_back = inv_rms * scaled - inputs_wide * (inv_rms * inv_rms * inv_rms) * inner_mean
    input_grad = (cotangent_local.astype(jnp.float32) + norm_back).astype(jnp.bfloat16)
    return (layer_out, input_grad, grad_in, grad_out)


def solution(mesh):
    return jax.shard_map(
        on_device,
        mesh=mesh,
        in_specs=(
            P(("tok", "feat"), None),
            P(),
            P("tok", "feat"),
            P("tok", "feat"),
            P("feat", None),
            P(("tok", "feat")),
            P(),
            P(("tok", "feat"), None),
            P(),
        ),
        out_specs=(
            P(("tok", "feat"), None),
            P(("tok", "feat"), None),
            P("tok", "feat"),
            P("tok", "feat"),
        ),
        check_vma=False,
    )
```

profile of v0, /device:TPU:0, one launch (start us, length us, event | category | flops | bytes accessed | tf_op | source)
XLA Modules:
  0.0 400.1 jit_solution(1458768137621977725)
XLA Ops:
  7.2 0.0 all-gather.5.cloned.1.call-start
  7.2 1.1 fusion.19
  8.3 1.8 fusion.21
  10.1 0.0 all-gather.5.cloned.1.call-update
  10.2 0.0 all-gather.7.cloned.1.call-start
  10.2 0.7 all-gather.7.cloned.1.call-update
  10.9 0.0 all-gather.9.cloned.1.call-start
  11.0 0.7 all-gather.9.cloned.1.call-update
  11.6 0.0 reduce-scatter.5.cloned.1.call-start
  11.7 29.2 %all-gather.5.cloned.1.call-done = bf16[256,2048]{1,0:T(8,128)(2,1)} async-done(((bf16[64,2048]{1,0:T(8,128)(2,1)}), bf16[256,2048]{1,0:T(8,128)(2,1)}) %all-gather.5.cloned.1.call-update) | async-done | bytes 1048592 | tf_op jit(solution)/shard_map/all_gather | solution.py:43
  40.9 1.5 copy.99
  42.4 2.8 convert_bitcast_fusion.1
  45.2 7.5 %copy.62 = bf16[256,16,4,128]{0,3,2,1:T(8,128)(2,1)} copy(bf16[256,16,4,128]{3,1,0,2:T(8,128)(2,1)} %convert_bitcast_fusion.1) | data formatting | bytes 8388608 | tf_op jit(solution)/shard_map/convert_element_type | solution.py:52
  52.7 17.5 %all-gather.7.cloned.1.call-done = bf16[512,2048]{1,0:T(8,128)(2,1)} async-done(((bf16[64,2048]{1,0:T(8,128)(2,1)}), bf16[512,2048]{1,0:T(8,128)(2,1)}) %all-gather.7.cloned.1.call-update) | async-done | bytes 2097168 | tf_op jit(solution)/shard_map/all_gather | solution.py:37
  70.3 2.9 copy.63
  73.1 4.9 %fusion.41 = f32[16,256,128]{2,1,0:T(8,128)} fusion(bf16[256,16,512]{0,2,1:T(8,128)(2,1)} %bitcast.106, bf16[512,16,128]{0,2,1:T(8,128)(2,1)S(1)} %bitcast.108), kind=kOutput, calls=%fused_computation.64 | convolution fusion | flops 536870912 | bytes 8388608 | tf_op jit(solution)/shard_map/rjm,mjc->rjc/dot_general | solution.py:60
  78.0 22.1 %all-gather.9.cloned.1.call-done = bf16[512,2048]{1,0:T(8,128)(2,1)} async-done(((bf16[64,2048]{1,0:T(8,128)(2,1)}), bf16[512,2048]{1,0:T(8,128)(2,1)}) %all-gather.9.cloned.1.call-update) | async-done | bytes 2097168 | tf_op jit(solution)/shard_map/all_gather | solution.py:38
  100.1 3.9 copy.66
  104.0 6.7 %convolution_bitcast_fusion.1 = f32[256,16,512]{2,0,1:T(8,128)} fusion(bf16[512,16,128]{0,2,1:T(8,128)(2,1)} %bitcast.111, f32[16,256,128]{2,1,0:T(8,128)} %fusion.41), kind=kOutput, calls=%fused_computation.9 | convolution fusion | flops 541589504 | bytes 12582912 | tf_op jit(solution)/shard_map/rjc,mjc->rjm/dot_general | solution.py:62
  110.7 9.9 %reshape.74 = f32[256,16,4,128]{3,2,0,1:T(4,128)} reshape(f32[256,16,512]{2,0,1:T(8,128)} %convolution_bitcast_fusion.1) | data formatting | bytes 16777216 | tf_op jit(solution)/shard_map/reshape | solution.py:55
  120.6 12.0 %bitcast_convert_fusion.1 = bf16[16,256,128]{2,0,1:T(8,128)(2,1)S(1)} fusion(f32[256,16,4,128]{3,2,0,1:T(4,128)} %reshape.74, s32[16,4]{0,1:T(4,128)S(1)} %copy-done.5), kind=kOutput, calls=%fused_computation.25 | convolution fusion | flops 403178496 | bytes 9437440 | tf_op jit(solution)/shard_map/rjkc,jkd->rdc/dot_general | solution.py:56
  132.6 0.0 copy-start.9
  132.7 0.0 copy-start.8
  132.7 1.2 copy.114
  133.9 0.0 reduce-scatter.5.cloned.1.call-update
  133.9 0.0 all-gather.11.cloned.1.call-start
  134.0 0.1 convert_reduce_fusion
  134.1 27.1 %reduce-scatter.5.cloned.1.call-done = bf16[64,2048]{1,0:T(8,128)(2,1)} async-done(((bf16[256,2048]{1,0:T(8,128)(2,1)}), bf16[64,2048]{1,0:T(8,128)(2,1)}) %reduce-scatter.5.cloned.1.call-update) | async-done | bytes 262160 | tf_op jit(solution)/shard_map/reduce_scatter | solution.py:65
  161.2 1.0 fusion.22
  162.3 0.0 copy-start.4
  162.3 0.7 copy-done.4
  163.0 0.3 convolution_bitcast_fusion.3
  163.3 0.2 convolution_bitcast_fusion.2
  163.5 38.8 %all-reduce = (f32[128]{0:T(128)S(1)}, f32[128]{0:T(128)S(1)}) all-reduce(f32[128]{0:T(128)S(1)} %convolution_bitcast_fusion.2, f32[128]{0:T(128)S(1)} %convert_reduce_fusion), channel_id=1, replica_groups=mesh['tok'=8,'feat'=4] {'tok','feat'}, use_global_device_ids=true, to_apply=%region_2.0 | all-reduce | flops 256 | bytes 2048 | tf_op jit(solution)/shard_map/psum | solution.py:76
  202.3 0.2 select_reduce_fusion
  202.5 0.8 add_convert_fusion
  203.3 0.0 all-gather.11.cloned.1.call-update
  203.4 0.0 reduce-scatter.7.cloned.1.call-start
  203.4 27.8 %all-gather.11.cloned.1.call-done = bf16[256,2048]{1,0:T(8,128)(2,1)} async-done(((bf16[64,2048]{1,0:T(8,128)(2,1)}), bf16[256,2048]{1,0:T(8,128)(2,1)}) %all-gather.11.cloned.1.call-update) | async-done | bytes 1048592 | tf_op jit(solution)/shard_map/all_gather | solution.py:82
  231.2 1.5 copy.101
  232.7 3.0 convert_bitcast_fusion
  235.7 7.5 %copy.70 = bf16[256,16,4,128]{0,3,2,1:T(8,128)(2,1)} copy(bf16[256,16,4,128]{3,1,0,2:T(8,128)(2,1)} %convert_bitcast_fusion) | data formatting | bytes 8388608 | tf_op jit(solution)/shard_map/convert_element_type | solution.py:52
  243.2 5.7 %fusion.10 = bf16[256,16,128]{2,0,1:T(8,128)(2,1)S(1)} fusion(f32[16,256,128]{2,1,0:T(8,128)} %fusion.41, bf16[256,16,512]{0,2,1:T(8,128)(2,1)} %bitcast.115, bf16[512,16,128]{0,2,1:T(8,128)(2,1)} %bitcast.112), kind=kOutput, calls=%fused_computation.18 | convolution fusion | flops 547356672 | bytes 9437184 | tf_op jit(solution)/shard_map/rjm,mjc->rjc/dot_general | solution.py:84
  248.9 4.5 %convolution_bitcast_fusion = f32[256,16,512]{2,0,1:T(8,128)} fusion(bf16[256,16,128]{2,0,1:T(8,128)(2,1)S(1)} %fusion.10, bf16[512,16,128]{0,2,1:T(8,128)(2,1)S(1)} %bitcast.109), kind=kOutput, calls=%fused_computation.8 | convolution fusion | flops 536870912 | bytes 11534336 | tf_op jit(solution)/shard_map/rjc,mjc->rjm/dot_general | solution.py:92
  253.4 9.9 %reshape.77 = f32[256,16,4,128]{3,2,0,1:T(4,128)} reshape(f32[256,16,512]{2,0,1:T(8,128)} %convolution_bitcast_fusion) | data formatting | bytes 16777216 | tf_op jit(solution)/shard_map/reshape | solution.py:55
  263.3 12.0 %bitcast_convert_fusion = bf16[16,256,128]{2,0,1:T(8,128)(2,1)S(1)} fusion(f32[256,16,4,128]{3,2,0,1:T(4,128)} %reshape.77, s32[16,4]{0,1:T(4,128)S(1)} %copy-done.5), kind=kOutput, calls=%fused_computation.19 | convolution fusion | flops 403178496 | bytes 9437440 | tf_op jit(solution)/shard_map/rjkc,jkd->rdc/dot_general | solution.py:56
  275.3 1.3 copy.113
  276.6 0.0 reduce-scatter.7.cloned.1.call-update
  276.6 0.0 reduce-scatter.9.cloned.1.call-start
  276.7 3.7 multiply_convert_fusion.1
  280.4 2.5 copy.77
  282.8 0.0 reduce-scatter.9.cloned.1.call-update
  282.9 0.0 reduce-scatter.11.cloned.1.call-start
  282.9 1.5 copy-done
  284.4 5.0 %multiply_convert_fusion = bf16[16,128,512]{2,1,0:T(8,128)(2,1)} fusion(bf16[256,16,512]{0,2,1:T(8,128)(2,1)} %bitcast.116, f32[16,256,128]{2,1,0:T(8,128)S(1)} %copy-done), kind=kOutput, calls=%fused_computation.4 | convolution fusion | flops 543686656 | bytes 8388608 | tf_op jit(solution)/shard_map/rjm,rjc->mjc/dot_general | solution.py:95
  289.4 4.0 copy.80
  293.4 0.0 reduce-scatter.11.cloned.1.call-update
  293.4 10.0 %reduce-scatter.7.cloned.1.call-done = bf16[64,2048]{1,0:T(8,128)(2,1)} async-done(((bf16[256,2048]{1,0:T(8,128)(2,1)}), bf16[64,2048]{1,0:T(8,128)(2,1)}) %reduce-scatter.7.cloned.1.call-update) | async-done | bytes 262160 | tf_op jit(solution)/shard_map/reduce_scatter | solution.py:107
  303.4 1.1 fusion.27
  304.6 2.0 fusion.26
  306.5 40.0 %reduce-scatter.9.cloned.1.call-done = bf16[64,2048]{1,0:T(8,128)(2,1)} async-done(((bf16[512,2048]{1,0:T(8,128)(2,1)}), bf16[64,2048]{1,0:T(8,128)(2,1)}) %reduce-scatter.9.cloned.1.call-update) | async-done | bytes 262160 | tf_op jit(solution)/shard_map/reduce_scatter | solution.py:103
  346.6 1.8 convert_element_type.118
  348.4 43.1 %reduce-scatter.11.cloned.1.call-done = bf16[64,2048]{1,0:T(8,128)(2,1)} async-done(((bf16[512,2048]{1,0:T(8,128)(2,1)}), bf16[64,2048]{1,0:T(8,128)(2,1)}) %reduce-scatter.11.cloned.1.call-update) | async-done | bytes 262160 | tf_op jit(solution)/shard_map/reduce_scatter | solution.py:100
  391.5 1.8 convert_element_type.122
  (19 shorter events, 0.1 us)
Async XLA Ops:
  7.2 35.2 %copy-start.5 = (s32[16,4]{0,1:T(4,128)S(1)}, s32[16,4]{0,1:T(4,128)}, u32[]{:S(2)}) copy-start(s32[16,4]{0,1:T(4,128)} %param.13) | copy-start | bytes 772
  7.2 33.8 %all-gather.5.cloned.1.call-start = ((), (), s32[]{:S(2)}) async-start(), calls=%async_computation.4 | async-start | bytes 1310720 | tf_op jit(solution)/shard_map/all_gather | solution.py:43
  10.2 60.1 %all-gather.7.cloned.1.call-start = ((), (), s32[]{:S(2)}) async-start(), calls=%async_computation.5 | async-start | bytes 2359296 | tf_op jit(solution)/shard_map/all_gather | solution.py:37
  10.9 89.2 %all-gather.9.cloned.1.call-start = ((), (), s32[]{:S(2)}) async-start(), calls=%async_computation.6 | async-start | bytes 2359296 | tf_op jit(solution)/shard_map/all_gather | solution.py:38
  11.6 149.6 %reduce-scatter.5.cloned.1.call-start = ((), (), s32[]{:S(2)}) async-start(), calls=%async_computation.7 | async-start | bytes 1310720 | tf_op jit(solution)/shard_map/reduce_scatter | solution.py:65
  132.6 1.4 copy-start.9
  132.6 28.6 %copy-start.1 = (bf16[64,2048]{1,0:T(8,128)(2,1)S(1)}, bf16[64,2048]{1,0:T(8,128)(2,1)}, u32[]{:S(2)}) copy-start(bf16[64,2048]{1,0:T(8,128)(2,1)} %param.9) | copy-start | bytes 786436
  132.6 30.3 %copy-start.7 = (f32[2048]{0:T(1024)S(1)}, f32[2048]{0:T(1024)}, u32[]{:S(2)}) copy-start(f32[2048]{0:T(1024)} %param.17) | copy-start | bytes 24580
  132.7 69.6 %copy-start.8 = (f32[128]{0:T(128)S(1)}, f32[128]{0:T(128)}, u32[]{:S(2)}) copy-start(f32[128]{0:T(128)} %param.15) | copy-start | bytes 1540
  132.7 69.8 %copy-start.2 = (bf16[64,2048]{1,0:T(8,128)(2,1)S(1)}, bf16[64,2048]{1,0:T(8,128)(2,1)}, u32[]{:S(2)}) copy-start(bf16[64,2048]{1,0:T(8,128)(2,1)} %param.16) | copy-start | bytes 786436
  133.9 97.3 %all-gather.11.cloned.1.call-start = ((), (), s32[]{:S(2)}) async-start(), calls=%async_computation.8 | async-start | bytes 1310720 | tf_op jit(solution)/shard_map/all_gather | solution.py:82
  162.3 0.7 copy-start.4
  203.4 100.0 %reduce-scatter.7.cloned.1.call-start = ((), (), s32[]{:S(2)}) async-start(), calls=%async_computation.9 | async-start | bytes 1310720 | tf_op jit(solution)/shard_map/reduce_scatter | solution.py:107
  276.6 70.0 %reduce-scatter.9.cloned.1.call-start = ((), (), s32[]{:S(2)}) async-start(), calls=%async_computation.10 | async-start | bytes 2359296 | tf_op jit(solution)/shard_map/reduce_scatter | solution.py:103
  282.8 1.6 copy-start
  282.9 108.6 %reduce-scatter.11.cloned.1.call-start = ((), (), s32[]{:S(2)}) async-start(), calls=%async_computation.11 | async-start | bytes 2359296 | tf_op jit(solution)/shard_map/reduce_scatter | solution.py:100
  293.4 10.0 %copy-start.6 = (f32[2048]{0:T(1024)S(1)}, f32[2048]{0:T(1024)}, u32[]{:S(2)}) copy-start(f32[2048]{0:T(1024)} %param.10) | copy-start | bytes 24580
  293.4 11.1 %copy-start.3 = (bf16[64,2048]{1,0:T(8,128)(2,1)S(1)}, bf16[64,2048]{1,0:T(8,128)(2,1)}, u32[]{:S(2)}) copy-start(bf16[64,2048]{1,0:T(8,128)(2,1)} %param.16) | copy-start | bytes 786436
Sparse Core Ops, SparseCore 0:
  10.3 30.6 all-gather.4
  42.8 27.3 all-gather.6
  72.1 27.8 all-gather.8
  134.1 27.1 reduce-scatter.4
  203.5 27.6 all-gather.10
  276.7 26.6 reduce-scatter.6
  306.7 39.8 reduce-scatter.8
  350.2 41.2 reduce-scatter.10
where the time goes:
time: 402 us; the launch traced here: 400 us
  waiting for transfers between devices  218 us (54%)
  matrix products  60.8 us (15%)
  local copies, waits for them, and re-layouts  55.7 us (14%)
  blocking collectives  38.8 us (10%)
  between operations  14.3 us (4%)
  other arithmetic  11.7 us (3%)
    reduce_scatter x1, waiting for transfers between devices, on_device(): lax.psum_scatter(arrange(out_terms).astype(jnp.bfloat16), 'tok', scatter_...  43.1 us
    reduce_scatter x1, waiting for transfers between devices, on_device(): lax.psum_scatter(arrange(in_terms).astype(jnp.bfloat16), 'tok', scatter_d...  40 us
    psum x1, blocking collectives, on_device(): lax.psum((score_sums, token_counts), ('tok', 'feat'))  38.8 us
    all_gather x1, waiting for transfers between devices, on_device(): normed_rows = lax.all_gather(normed, 'feat', axis=0, tiled=True)  29.2 us
    all_gather x1, waiting for transfers between devices, on_device(): cotangent_rows = lax.all_gather(cotangent_local, 'feat', axis=0, tiled=True)  27.8 us
    reduce_scatter x1, waiting for transfers between devices, on_device(): lax.psum_scatter(spread(out_terms_fwd).astype(jnp.bfloat16), 'feat', scat...  27.1 us
    dot_general x2, matrix products, spread(): jnp.einsum('rjkc,jkd->rdc', grouped, sel_wide, precision=lax.Precision.HI...  24 us
    all_gather x1, waiting for transfers between devices, on_device(): lax.all_gather(w_out, 'tok', axis=0, tiled=True)  22.1 us
  transfers between devices with their start and end apart: 8, of which 8 were waited for; matrix products, arithmetic and copies ran while one was open for 10% of the time, Pallas kernels for 0%

commit v1 on v0

v1 whole, which is shorter than its diff:
```python
import functools
import math

import jax
import jax.numpy as jnp
from jax import lax
from jax.experimental import pallas as pl
from jax.experimental.pallas import tpu as pltpu
from jax.sharding import PartitionSpec as P

BLK = 128
EPS = 1e-06
LOSS_WEIGHT = 8.0
GELU_A = math.sqrt(2.0 / math.pi)
GELU_B = 0.044715
VMEM_BYTES = 48 * 1024 * 1024
BF16 = jnp.bfloat16
F32 = jnp.float32
NT = (((1,), (1,)), ((), ()))
TN = (((0,), (0,)), ((), ()))


def dot(a, b, dims=(((1,), (0,)), ((), ()))):
    return lax.dot_general(a, b, dims, preferred_element_type=F32)


def three_terms(row):
    hi = row.astype(BF16)
    rest = row - hi.astype(F32)
    mid = rest.astype(BF16)
    low = (rest - mid.astype(F32)).astype(BF16)
    pad = jnp.zeros((8 - 3, row.shape[1]), F32).astype(BF16)
    return jnp.concatenate([hi, mid, low, pad], axis=0)


def forward_kernel(masks_in, masks_out, nf, *refs):
    idx, place = refs[0], refs[1]
    refs = refs[2:]
    xs, refs = refs[:nf], refs[nf:]
    gain, readout = refs[:2]
    refs = refs[2:]
    win_parts, refs = refs[: len(masks_in)], refs[len(masks_in):]
    wout_parts, refs = refs[: len(masks_out)], refs[len(masks_out):]
    normed, act, dact, win, wout, score = refs[:6]
    branch, acc = refs[6 : 6 + nf], refs[6 + nf]
    rows = xs[0].shape[0]
    fb = normed.shape[0]
    nj, kb = idx.shape
    for d in range(nf):
        x = xs[d][...].astype(F32)
        inv = lax.rsqrt(jnp.mean(x * x, axis=1, keepdims=True) + EPS)
        n = (x * inv * gain[...]).astype(BF16)
        for b in range(fb):
            normed[b, d * rows : (d + 1) * rows, :] = n[:, b * BLK : (b + 1) * BLK]
    for parts, masks, whole in ((win_parts, masks_in, win), (wout_parts, masks_out, wout)):
        for part, ms in zip(parts, masks):
            depth = part.shape[0] // len(ms)
            for i, m in enumerate(ms):
                at = pl.multiple_of((place[0] ^ m) * depth, depth)
                for j in range(nj):
                    whole[j, pl.ds(at, depth), :] = part[
                        i * depth : (i + 1) * depth, j * BLK : (j + 1) * BLK
                    ]
    acc[...] = jnp.zeros_like(acc)

    @pl.loop(0, nj)
    def _(j):
        which = [idx[j, k] for k in range(kb)]
        picked = jnp.concatenate([normed[w] for w in which], axis=1)
        v = dot(picked, win[j])
        v2 = v * v
        t = jnp.tanh(GELU_A * v * (1.0 + GELU_B * v2))
        half = 0.5 * (1.0 + t)
        a = (v * half).astype(BF16)
        act[j] = a
        dact[j] = half + 0.5 * v * (1.0 - t * t) * (GELU_A * (1.0 + 3.0 * GELU_B * v2))
        terms = dot(a, wout[j], NT)
        for k, w in enumerate(which):
            acc[w] += terms[:, k * BLK : (k + 1) * BLK]

    total = jnp.zeros((8, nf * rows), F32)
    own = jnp.zeros((8, rows), F32)
    for b in range(fb):
        part = acc[b].astype(BF16)
        r = three_terms(readout[:, b * BLK : (b + 1) * BLK])
        total = total + dot(r, part, NT)
        own = own + dot(r, xs[0][:, b * BLK : (b + 1) * BLK], NT)
        for d in range(nf):
            branch[d][:, b * BLK : (b + 1) * BLK] = part[d * rows : (d + 1) * rows]
    own = jnp.sum(own, axis=0, keepdims=True)
    pad = jnp.zeros((1, (nf - 1) * rows), F32)
    score[...] = jnp.sum(total, axis=0, keepdims=True) + jnp.concatenate([own, pad], axis=1)


def backward_kernel(nf, *refs):
    idx = refs[0]
    ups, refs = refs[1 : 1 + nf], refs[1 + nf:]
    score, sleft, sright, ids, ileft, iright, teacher, readout = refs[:8]
    win, wout, dact, cot, pre_grad, own_cot = refs[8:14]
    back, acc = refs[14 : 14 + nf], refs[14 + nf]
    rows = ups[0].shape[0]
    fb = cot.shape[0]
    nj, kb = idx.shape
    tokens = nf * rows
    nseg = teacher.shape[0]
    seg = lax.broadcasted_iota(jnp.int32, (nseg, tokens), 0) + 1
    sums = jnp.zeros((nseg, 1), F32)
    counts = jnp.zeros((nseg, 1), F32)
    for s, i in ((score, ids), (sleft, ileft), (sright, iright)):
        here = i[...] == seg
        sums = sums + jnp.sum(jnp.where(here, s[...], 0.0), axis=1, keepdims=True)
        counts = counts + jnp.sum(jnp.where(here, 1.0, 0.0), axis=1, keepdims=True)
    misfit = sums / jnp.maximum(counts, 1.0) - teacher[...]
    coeff = 2.0 * LOSS_WEIGHT * jnp.sum(
        jnp.where(ids[...] == seg, misfit, 0.0), axis=0, keepdims=True
    )
    column = jnp.transpose(jnp.broadcast_to(coeff, (BLK, tokens)))
    for d in range(nf):
        for b in range(fb):
            c = (
                ups[d][:, b * BLK : (b + 1) * BLK].astype(F32)
                + column[d * rows : (d + 1) * rows] * readout[:, b * BLK : (b + 1) * BLK]
            ).astype(BF16)
            cot[b, d * rows : (d + 1) * rows, :] = c
            if d == 0:
                own_cot[:, b * BLK : (b + 1) * BLK] = c
    acc[...] = jnp.zeros_like(acc)

    @pl.loop(0, nj)
    def _(j):
        which = [idx[j, k] for k in range(kb)]
        picked = jnp.concatenate([cot[w] for w in which], axis=1)
        p = (dot(picked, wout[j]) * dact[j]).astype(BF16)
        pre_grad[j] = p
        terms = dot(p, win[j], NT)
        for k, w in enumerate(which):
            acc[w] += terms[:, k * BLK : (k + 1) * BLK]

    for b in range(fb):
        part = acc[b].astype(BF16)
        for d in range(nf):
            back[d][:, b * BLK : (b + 1) * BLK] = part[d * rows : (d + 1) * rows]


def grads_kernel(orders, scale, idx, place, cot, act, normed, pre_grad, *outs):
    nj, kb = idx.shape
    n = len(orders[0])
    depth = kb * BLK // n
    half = n // 2

    def one(left, right, keep, send, order, j):
        at = [0] * n
        for pos, m in enumerate(order):
            at[m] = pos
        for k in range(kb):
            g = (dot(left[idx[j, k]], right[j], TN) * scale).astype(BF16)
            for part in range(BLK // depth):
                owner = k * (BLK // depth) + part
                m = place[0] ^ owner
                pos = at[n - 1]
                for c in range(n - 1):
                    pos = jnp.where(m == c, at[c], pos)
                piece = g[part * depth : (part + 1) * depth]
                col = pl.ds(pl.multiple_of(j * BLK, BLK), BLK)

                @pl.when(pos < half)
                def _():
                    keep[pl.ds(pl.multiple_of(pos * depth, depth), depth), col] = piece

                @pl.when(pos >= half)
                def _():
                    send[pl.ds(pl.multiple_of((pos - half) * depth, depth), depth), col] = piece

    @pl.loop(0, nj)
    def _(j):
        one(cot, act, outs[0], outs[1], orders[0], j)
        one(normed, pre_grad, outs[2], outs[3], orders[1], j)


def finish_kernel(x_ref, gain, cot, own, *refs):
    others, out = refs[:-1], refs[-1]
    x = x_ref[...].astype(F32)
    inv = lax.rsqrt(jnp.mean(x * x, axis=1, keepdims=True) + EPS)
    total = own[...].astype(F32)
    for o in others:
        total = total + o[...].astype(F32)
    g = total * gain[...]
    inner = jnp.mean(g * x, axis=1, keepdims=True)
    out[...] = (cot[...].astype(F32) + (inv * g - x * (inv * inv * inv) * inner)).astype(BF16)


VM = pl.BlockSpec(memory_space=pltpu.VMEM)
SM = pl.BlockSpec(memory_space=pltpu.SMEM)


def call(body, outs, args, scalars, scratch, flops):
    return pl.pallas_call(
        body,
        out_shape=outs,
        in_specs=[SM] * scalars + [VM] * (len(args) - scalars),
        out_specs=[VM] * len(outs),
        scratch_shapes=scratch,
        compiler_params=pltpu.CompilerParams(vmem_limit_bytes=VMEM_BYTES),
        cost_estimate=pl.CostEstimate(
            flops=flops,
            bytes_accessed=sum(math.prod(o.shape) * o.dtype.itemsize for o in outs),
            transcendentals=0,
        ),
    )(*args)


def xor(n, mask):
    return [(i, i ^ mask) for i in range(n)]


def swap(value, axis, mask):
    return lax.ppermute(value, axis, xor(lax.axis_size(axis), mask))


def bits_of(n):
    return [1 << b for b in range(n.bit_length() - 1)]


def gather_tok(w, bits):
    held, masks = [w], [[0]]
    for bit in bits:
        whole = jnp.concatenate(held, axis=0) if len(held) > 1 else held[0]
        flat = [m for ms in masks for m in ms]
        held, masks = [whole, swap(whole, "tok", bit)], [flat, [m ^ bit for m in flat]]
    other = [swap(h, "tok", 1) for h in held]
    return held + other, masks + [[m ^ 1 for m in ms] for ms in masks]


def order_of(bits):
    order = [0]
    for bit in reversed(bits):
        order = order + [m ^ bit for m in order]
    return order


def scatter_tok(keep, send, bits):
    total = keep.astype(F32) + swap(send, "tok", bits[0]).astype(F32)
    for bit in bits[1:]:
        half = total.shape[0] // 2
        total = total[:half] + swap(total[half:].astype(BF16), "tok", bit).astype(F32)
    return total


def on_device(
    inputs, norm_gain, w_in, w_out, block_index, segment_ids, teacher_scores, upstream, readout
):
    rows, width = inputs.shape
    nt, nf = lax.axis_size("tok"), lax.axis_size("feat")
    nj, kb = block_index.shape
    hidden = w_in.shape[1]
    fb = width // BLK
    tokens = rows * nf
    grad_scale = 1.0 / math.sqrt(tokens * nt)
    tok_bits = bits_of(nt)
    feat_bits = bits_of(nf)
    place = lax.axis_index("tok").astype(jnp.int32).reshape(1)
    gain_row, readout_row = norm_gain.reshape(1, width), readout.reshape(1, width)
    flops = 2 * tokens * hidden * kb * BLK

    win_parts, masks_in = gather_tok(w_in, tok_bits[1:])
    wout_parts, masks_out = gather_tok(w_out, tok_bits[1:][::-1])
    xs = [inputs] + [swap(inputs, "feat", d) for d in range(1, nf)]

    ids = segment_ids + 1
    for bit in feat_bits:
        ids = jnp.concatenate([ids, swap(ids, "feat", bit)])
    up_line = [(i, i + 1) for i in range(nt - 1)]
    down_line = [(i + 1, i) for i in range(nt - 1)]
    ids_left = lax.ppermute(ids, "tok", up_line)
    ids_right = lax.ppermute(ids, "tok", down_line)

    ups = [upstream] + [swap(upstream, "feat", d) for d in range(1, nf)]

    sds = jax.ShapeDtypeStruct
    piece = sds((rows, width), BF16)
    outs = call(
        functools.partial(forward_kernel, masks_in, masks_out, nf),
        [
            sds((fb, tokens, BLK), BF16),
            sds((nj, tokens, BLK), BF16),
            sds((nj, tokens, BLK), F32),
            sds((nj, kb * BLK, BLK), BF16),
            sds((nj, kb * BLK, BLK), BF16),
            sds((1, tokens), F32),
        ]
        + [piece] * nf,
        [block_index, place] + xs + [gain_row, readout_row] + win_parts + wout_parts,
        2,
        [pltpu.VMEM((fb, tokens, BLK), F32)],
        2 * flops,
    )
    normed, act, dact, win, wout, score = outs[:6]
    branch = outs[6:]

    score = score.reshape(nf, rows)
    for bit in feat_bits:
        score = score + jnp.flip(
            swap(score, "feat", bit).reshape(nf // (2 * bit), 2, bit, rows), axis=1
        ).reshape(nf, rows)
    score = score.reshape(1, tokens)
    score_left = lax.ppermute(score, "tok", up_line)
    score_right = lax.ppermute(score, "tok", down_line)

    total = branch[0].astype(F32)
    for d in range(1, nf):
        total = total + swap(branch[d], "feat", d).astype(F32)
    layer_out = (inputs.astype(F32) + total).astype(BF16)

    outs = call(
        functools.partial(backward_kernel, nf),
        [sds((fb, tokens, BLK), BF16), sds((nj, tokens, BLK), BF16), piece] + [piece] * nf,
        [block_index]
        + ups
        + [score, score_left, score_right]
        + [i.reshape(1, tokens) for i in (ids, ids_left, ids_right)]
        + [teacher_scores.reshape(-1, 1), readout_row, win, wout, dact],
        1,
        [pltpu.VMEM((fb, tokens, BLK), F32)],
        2 * flops,
    )
    cot, pre_grad, own_cot = outs[:3]
    back = outs[3:]
    back_others = [swap(back[d], "feat", d) for d in range(1, nf)]

    out_bits = [1] + tok_bits[1:]
    in_bits = [1] + tok_bits[1:][::-1]
    half = sds((kb * BLK // 2, hidden), BF16)
    keep_out, send_out, keep_in, send_in = call(
        functools.partial(grads_kernel, (order_of(out_bits), order_of(in_bits)), grad_scale),
        [half] * 4,
        [block_index, place, cot, act, normed, pre_grad],
        2,
        [],
        2 * flops,
    )
    grad_out = scatter_tok(keep_out, send_out, out_bits)
    grad_in = scatter_tok(keep_in, send_in, in_bits)
    (input_grad,) = call(
        finish_kernel,
        [piece],
        [inputs, gain_row, own_cot, back[0]] + back_others,
        0,
        [],
        rows * width,
    )
    return (layer_out, input_grad, grad_in, grad_out)


def solution(mesh):
    return jax.shard_map(
        on_device,
        mesh=mesh,
        in_specs=(
            P(("tok", "feat"), None),
            P(),
            P("tok", "feat"),
            P("tok", "feat"),
            P("feat", None),
            P(("tok", "feat")),
            P(),
            P(("tok", "feat"), None),
            P(),
        ),
        out_specs=(
            P(("tok", "feat"), None),
            P(("tok", "feat"), None),
            P("tok", "feat"),
            P("tok", "feat"),
        ),
        check_vma=False,
    )
```

time: 402 us -> 200 us (0.50)
  the two profiles are of different devices: /device:TPU:0 before, /device:TPU:10 now
where the time goes in v1:
time: 200 us
  waiting for transfers between devices  86.3 us (43%)
  Pallas kernels  54.6 us (27%)
  starting transfers between devices  42.7 us (21%)
  local copies, waits for them, and re-layouts  11.3 us (6%)
  other arithmetic  4.28 us (2%)
    ppermute x30, waiting for transfers between devices, swap(): return lax.ppermute(value, axis, xor(lax.axis_size(axis), mask))  85.1 us
    pallas_call x4, Pallas kernels, call(): pl.pallas_call(body, out_shape=outs, in_specs=[SM] * scalars + [VM] * (le...  54.6 us
    ppermute x30, starting transfers between devices, swap(): return lax.ppermute(value, axis, xor(lax.axis_size(axis), mask))  33.3 us
    unnamed x43, local copies, waits for them, and re-layouts  10.1 us
  transfers between devices with their start and end apart: 34, of which 15 were waited for; matrix products, arithmetic and copies ran while one was open for 3% of the time, Pallas kernels for 7%

profile of v1, /device:TPU:10, one launch (start us, length us, event | category | flops | bytes accessed | tf_op | source)
XLA Modules:
  0.0 200.1 jit_solution(9942619599711125445)
XLA Ops:
  0.7 1.6 collective-permute-start.7
  2.3 0.5 collective-permute-start.3
  2.8 1.0 constant_dynamic-update-slice_fusion.3
  3.8 1.0 constant_dynamic-update-slice_fusion.1
  4.7 4.3 %collective-permute-done.7 = bf16[64,2048]{1,0:T(8,128)(2,1)S(1)} collective-permute-done((bf16[64,2048]{1,0:T(8,128)(2,1)}, bf16[64,2048]{1,0:T(8,128)(2,1)S(1)}, u32[]{:S(2)}, u32[]{:S(2)}) %collective-permute-start.7) | collective-permute-done | bytes 262176 | tf_op jit(solution)/shard_map/ppermute | solution.py:217
  9.0 0.6 collective-permute-start.8
  9.6 0.6 collective-permute-done.3
  10.3 1.0 collective-permute-start.4
  11.2 0.4 collective-permute-start
  11.7 2.6 %collective-permute-start.1 = (bf16[64,2048]{1,0:T(8,128)(2,1)S(1)}, bf16[64,2048]{1,0:T(8,128)(2,1)S(1)}, u32[]{:S(2)}, u32[]{:S(2)}) collective-permute-start(bf16[64,2048]{1,0:T(8,128)(2,1)S(1)} %copy-done), channel_id=1, source_target_pairs={{0,2},{1,3},{2,0},{3,1},{4,6},{5,7},{6,4},{7,5},{8,10},{9,11},{10,... | collective-permute-start | bytes 786440 | tf_op jit(solution)/shard_map/ppermute | solution.py:217
  14.3 7.0 %collective-permute-done.refs_3_ = bf16[64,2048]{1,0:T(8,128)(2,1)S(1)} collective-permute-done((bf16[64,2048]{1,0:T(8,128)(2,1)S(1)}, bf16[64,2048]{1,0:T(8,128)(2,1)S(1)}, u32[]{:S(2)}, u32[]{:S(2)}) %collective-permute-start) | collective-permute-done | bytes 262176 | tf_op jit(solution)/shard_map/ppermute | solution.py:217
  21.3 0.7 copy-done.4
  22.0 0.5 collective-permute-start.10
  22.5 0.3 collective-permute-done.4.refs_9_
  22.8 1.8 collective-permute-done.1.refs_4_
  24.6 0.7 copy-done.6
  25.3 0.4 collective-permute-start.2
  25.8 12.1 %collective-permute-done.2.refs_5_ = bf16[64,2048]{1,0:T(8,128)(2,1)} collective-permute-done((bf16[64,2048]{1,0:T(8,128)(2,1)S(1)}, bf16[64,2048]{1,0:T(8,128)(2,1)}, u32[]{:S(2)}, u32[]{:S(2)}) %collective-permute-start.2) | collective-permute-done | bytes 262176 | tf_op jit(solution)/shard_map/ppermute | solution.py:217
  38.0 0.9 copy-done.5
  39.0 0.9 copy-done.7
  39.9 12.5 %shard_map.120 = (bf16[16,256,128]{2,1,0:T(8,128)(2,1)}, bf16[16,256,128]{2,1,0:T(8,128)(2,1)}, f32[16,256,128]{2,1,0:T(8,128)}, bf16[16,512,128]{2,1,0:T(8,128)...) custom-call(s32[16,4]{1,0:T(8,128)S(1)} %copy.13.refs_0_.idx, ...), custom_call_target="tpu_custom_call" | custom-call | flops 1073741824 | bytes 9438208 | tf_op jit(solution)/shard_map/pallas_call | solution.py:197
  52.4 0.7 copy-done.2
  53.1 0.7 copy-done.11
  53.8 0.7 copy-done.13
  54.5 0.7 copy-done.15
  55.2 0.5 broadcast.3
  55.7 0.6 reduce.3
  56.5 2.0 %collective-permute-start.17 = (f32[4,64]{1,0:T(4,128)S(1)}, f32[4,64]{1,0:T(4,128)S(1)}, u32[]{:S(2)}, u32[]{:S(2)}) collective-permute-start(f32[4,64]{1,0:T(4,128)S(1)} %reshape.52), channel_id=1, source_target_pairs={{0,1},{1,0},{2,3},{3,2},{4,5},{5,4},{6,7},{7,6},{8,9},{9,8},{10,11... | collective-permute-start | bytes 3080 | tf_op jit(solution)/shard_map/ppermute | solution.py:217
  58.6 1.0 collective-permute-start.22
  59.6 2.0 %collective-permute-start.14 = (bf16[64,2048]{1,0:T(8,128)(2,1)}, bf16[64,2048]{1,0:T(8,128)(2,1)S(1)}, u32[]{:S(2)}, u32[]{:S(2)}) collective-permute-start(bf16[64,2048]{1,0:T(8,128)(2,1)} %refs_1_.1), channel_id=1, source_target_pairs={{0,1},{1,0},{2,3},{3,2},{4,5},{5,4},{6,7},{7,6},{8,9},{9,8},{10,11... | collective-permute-start | bytes 786440 | tf_op jit(solution)/shard_map/ppermute | solution.py:217
  61.7 1.4 collective-permute-start.16
  63.1 2.8 %collective-permute-start.18 = (f32[4,64]{1,0:T(4,128)S(1)}, f32[4,64]{1,0:T(4,128)S(1)}, u32[]{:S(2)}, u32[]{:S(2)}) collective-permute-start(f32[4,64]{1,0:T(4,128)S(1)} %add.51), channel_id=1, source_target_pairs={{0,2},{1,3},{2,0},{3,1},{4,6},{5,7},{6,4},{7,5},{8,10},{9,11},{10,... | collective-permute-start | bytes 3080 | tf_op jit(solution)/shard_map/ppermute | solution.py:217
  66.0 1.9 collective-permute-start.23
  68.0 14.8 %collective-permute-done.18 = f32[4,64]{1,0:T(4,128)S(1)} collective-permute-done((f32[4,64]{1,0:T(4,128)S(1)}, f32[4,64]{1,0:T(4,128)S(1)}, u32[]{:S(2)}, u32[]{:S(2)}) %collective-permute-start.18) | collective-permute-done | bytes 1056 | tf_op jit(solution)/shard_map/ppermute | solution.py:217
  82.8 1.9 collective-permute-start.24
  84.9 2.4 %collective-permute-start.19 = (f32[1,256]{1,0:T(1,128)S(1)}, f32[1,256]{1,0:T(1,128)S(1)}, u32[]{:S(2)}, u32[]{:S(2)}) collective-permute-start(f32[1,256]{1,0:T(1,128)S(1)} %add_add_fusion.refs_5_), channel_id=1, source_target_pairs={{0,4},{4,8},{8,12},{12,16},{16,20},{20,24},{24,28},{1,5},{5,9},{9,... | collective-permute-start | bytes 3080 | tf_op jit(solution)/shard_map/ppermute | solution.py:306
  87.3 3.2 %collective-permute-start.20 = (f32[1,256]{1,0:T(1,128)S(1)}, f32[1,256]{1,0:T(1,128)S(1)}, u32[]{:S(2)}, u32[]{:S(2)}) collective-permute-start(f32[1,256]{1,0:T(1,128)S(1)} %add_add_fusion.refs_5_), channel_id=1, source_target_pairs={{4,0},{8,4},{12,8},{16,12},{20,16},{24,20},{28,24},{5,1},{9,5},{13... | collective-permute-start | bytes 3080 | tf_op jit(solution)/shard_map/ppermute | solution.py:307
  90.5 0.1 copy.15.refs_11_
  90.6 1.2 collective-permute-done.20.refs_7_
  91.8 0.9 copy-done.8
  92.8 10.1 %shard_map.121 = (bf16[16,256,128]{2,1,0:T(8,128)(2,1)S(1)}, bf16[16,256,128]{2,1,0:T(8,128)(2,1)S(1)}, bf16[64,2048]{1,0:T(8,128)(2,1)S(1)}, bf16[64,2048]{1,0:...) custom-call(s32[16,4]{1,0:T(8,128)S(1)} %copy.13.refs_0_.idx, ...), custom_call_target="tpu_custom_call" | custom-call | flops 1073741824 | bytes 3407872 | tf_op jit(solution)/shard_map/pallas_call | solution.py:197
  102.9 1.0 copy-done.1
  103.8 30.9 %shard_map.123 = (bf16[256,2048]{1,0:T(8,128)(2,1)S(1)}, bf16[256,2048]{1,0:T(8,128)(2,1)S(1)}, bf16[256,2048]{1,0:T(8,128)(2,1)S(1)}, bf16[256,2048]{1,0:T(8,128)(2,1)S(1)}) custom-call(s32[16,4]{1,0:T(8,128)S(1)} %copy.13.refs_0_.idx, s32[1]{0:T(128)} %bitcast.refs_1_.place, bf16[16,256,128]{2,1,0:T(8,128)(2,1)S(1)} %get-tuple-element.38.cot, ...), custom_call_target="tpu_custom_call" | custom-call | flops 1073741824 | bytes 4194304 | tf_op jit(solution)/shard_map/pallas_call | solution.py:197
  134.7 3.5 %collective-permute-start.31 = (bf16[256,2048]{1,0:T(8,128)(2,1)S(1)}, bf16[256,2048]{1,0:T(8,128)(2,1)S(1)}, u32[]{:S(2)}, u32[]{:S(2)}) collective-permute-start(bf16[256,2048]{1,0:T(8,128)(2,1)S(1)} %get-tuple-element.45), channel_id=1, source_target_pairs={{0,4},{4,0},{8,12},{12,8},{16,20},{20,16},{24,28},{28,24},{1,5},{5... | collective-permute-start | bytes 3145736 | tf_op jit(solution)/shard_map/ppermute | solution.py:217
  138.3 3.2 %collective-permute-start.11 = (bf16[64,2048]{1,0:T(8,128)(2,1)S(1)}, bf16[64,2048]{1,0:T(8,128)(2,1)S(1)}, u32[]{:S(2)}, u32[]{:S(2)}) collective-permute-start(bf16[64,2048]{1,0:T(8,128)(2,1)S(1)} %copy-done.16), channel_id=1, source_target_pairs={{0,1},{1,0},{2,3},{3,2},{4,5},{5,4},{6,7},{7,6},{8,9},{9,8},{10,11... | collective-permute-start | bytes 786440 | tf_op jit(solution)/shard_map/ppermute | solution.py:217
  141.6 0.1 collective-permute-start.12
  141.7 1.4 collective-permute-start.13
  143.1 2.9 %collective-permute-start.25 = (bf16[64,2048]{1,0:T(8,128)(2,1)S(1)}, bf16[64,2048]{1,0:T(8,128)(2,1)S(1)}, u32[]{:S(2)}, u32[]{:S(2)}) collective-permute-start(bf16[64,2048]{1,0:T(8,128)(2,1)S(1)} %get-tuple-element.35), channel_id=1, source_target_pairs={{0,1},{1,0},{2,3},{3,2},{4,5},{5,4},{6,7},{7,6},{8,9},{9,8},{10,11... | collective-permute-start | bytes 786440 | tf_op jit(solution)/shard_map/ppermute | solution.py:217
  145.9 0.4 convert_add_fusion
  146.5 0.3 convert_add_fusion.1
  146.9 5.7 %collective-permute-done.11 = bf16[64,2048]{1,0:T(8,128)(2,1)S(1)} collective-permute-done((bf16[64,2048]{1,0:T(8,128)(2,1)S(1)}, bf16[64,2048]{1,0:T(8,128)(2,1)S(1)}, u32[]{:S(2)}, u32[]{:S(2)}) %collective-permute-start.11) | collective-permute-done | bytes 262176 | tf_op jit(solution)/shard_map/ppermute | solution.py:217
  152.6 3.3 %collective-permute-start.26 = (bf16[64,2048]{1,0:T(8,128)(2,1)S(1)}, bf16[64,2048]{1,0:T(8,128)(2,1)S(1)}, u32[]{:S(2)}, u32[]{:S(2)}) collective-permute-start(bf16[64,2048]{1,0:T(8,128)(2,1)S(1)} %get-tuple-element.36), channel_id=1, source_target_pairs={{0,2},{1,3},{2,0},{3,1},{4,6},{5,7},{6,4},{7,5},{8,10},{9,11},{10,... | collective-permute-start | bytes 786440 | tf_op jit(solution)/shard_map/ppermute | solution.py:217
  155.9 3.6 %collective-permute-done.12 = bf16[64,2048]{1,0:T(8,128)(2,1)S(1)} collective-permute-done((bf16[64,2048]{1,0:T(8,128)(2,1)S(1)}, bf16[64,2048]{1,0:T(8,128)(2,1)S(1)}, u32[]{:S(2)}, u32[]{:S(2)}) %collective-permute-start.12) | collective-permute-done | bytes 262176 | tf_op jit(solution)/shard_map/ppermute | solution.py:217
  159.5 1.5 collective-permute-start.27
  161.0 17.3 %collective-permute-done.13 = bf16[64,2048]{1,0:T(8,128)(2,1)S(1)} collective-permute-done((bf16[64,2048]{1,0:T(8,128)(2,1)S(1)}, bf16[64,2048]{1,0:T(8,128)(2,1)S(1)}, u32[]{:S(2)}, u32[]{:S(2)}) %collective-permute-start.13) | collective-permute-done | bytes 262176 | tf_op jit(solution)/shard_map/ppermute | solution.py:217
  178.4 0.9 add_convert_fusion
  179.2 2.9 %collective-permute-done.26.refs_1_ = bf16[64,2048]{1,0:T(8,128)(2,1)S(1)} collective-permute-done((bf16[64,2048]{1,0:T(8,128)(2,1)S(1)}, bf16[64,2048]{1,0:T(8,128)(2,1)S(1)}, u32[]{:S(2)}, u32[]{:S(2)}) %collective-permute-start.26) | collective-permute-done | bytes 262176 | tf_op jit(solution)/shard_map/ppermute | solution.py:217
  182.1 7.0 %collective-permute-done.27.refs_2_ = bf16[64,2048]{1,0:T(8,128)(2,1)S(1)} collective-permute-done((bf16[64,2048]{1,0:T(8,128)(2,1)S(1)}, bf16[64,2048]{1,0:T(8,128)(2,1)S(1)}, u32[]{:S(2)}, u32[]{:S(2)}) %collective-permute-start.27) | collective-permute-done | bytes 262176 | tf_op jit(solution)/shard_map/ppermute | solution.py:217
  189.1 1.1 shard_map.122
  190.3 0.1 slice_add_fusion
  190.5 0.9 collective-permute-done.29
  191.6 6.8 %collective-permute-done.33 = bf16[64,2048]{1,0:T(8,128)(2,1)S(1)} collective-permute-done((bf16[64,2048]{1,0:T(8,128)(2,1)S(1)}, bf16[64,2048]{1,0:T(8,128)(2,1)S(1)}, u32[]{:S(2)}, u32[]{:S(2)}) %collective-permute-start.33) | collective-permute-done | bytes 262176 | tf_op jit(solution)/shard_map/ppermute | solution.py:217
  198.4 0.8 slice_add_fusion.2
  199.2 0.9 slice_add_fusion.3
  (77 shorter events, 1.3 us)
Async XLA Ops:
  0.6 10.6 %copy-start = (bf16[64,2048]{1,0:T(8,128)(2,1)S(1)}, bf16[64,2048]{1,0:T(8,128)(2,1)}, u32[]{:S(2)}) copy-start(bf16[64,2048]{1,0:T(8,128)(2,1)} %x_ref.1) | copy-start | bytes 786436
  0.6 25.1 %copy-start.17 = (s32[16,4]{0,1:T(4,128)S(1)}, s32[16,4]{0,1:T(4,128)}, u32[]{:S(2)}) copy-start(s32[16,4]{0,1:T(4,128)} %param.13) | copy-start | bytes 772
  0.7 25.2 %copy-start.19 = (s32[64]{0:T(128)S(1)}, s32[64]{0:T(128)}, u32[]{:S(2)}) copy-start(s32[64]{0:T(128)} %param.14) | copy-start | bytes 772
  0.7 37.3 %copy-start.9 = (f32[2048]{0:T(1024)S(1)}, f32[2048]{0:T(1024)}, u32[]{:S(2)}) copy-start(f32[2048]{0:T(1024)} %param.10) | copy-start | bytes 24580
  0.7 37.3 %copy-start.10 = (f32[2048]{0:T(1024)S(1)}, f32[2048]{0:T(1024)}, u32[]{:S(2)}) copy-start(f32[2048]{0:T(1024)} %param.17) | copy-start | bytes 24580
  0.7 8.3 %collective-permute-start.7 = (bf16[64,2048]{1,0:T(8,128)(2,1)}, bf16[64,2048]{1,0:T(8,128)(2,1)S(1)}, u32[]{:S(2)}, u32[]{:S(2)}) collective-permute-start(bf16[64,2048]{1,0:T(8,128)(2,1)} %param.12), channel_id=1, source_target_pairs={{0,16},{4,20},{8,24},{12,28},{16,0},{20,4},{24,8},{28,12},{1,17},{... | collective-permute-start | bytes 786440 | tf_op jit(solution)/shard_map/ppermute | solution.py:217
  2.3 8.0 %collective-permute-start.3 = (bf16[64,2048]{1,0:T(8,128)(2,1)}, bf16[64,2048]{1,0:T(8,128)(2,1)S(1)}, u32[]{:S(2)}, u32[]{:S(2)}) collective-permute-start(bf16[64,2048]{1,0:T(8,128)(2,1)} %param.11), channel_id=1, source_target_pairs={{0,8},{4,12},{8,0},{12,4},{16,24},{20,28},{24,16},{28,20},{1,9},{5... | collective-permute-start | bytes 786440 | tf_op jit(solution)/shard_map/ppermute | solution.py:217
  9.0 13.0 %collective-permute-start.8 = (bf16[128,2048]{1,0:T(8,128)(2,1)S(1)}, bf16[128,2048]{1,0:T(8,128)(2,1)S(1)}, u32[]{:S(2)}, u32[]{:S(2)}) collective-permute-start(bf16[128,2048]{1,0:T(8,128)(2,1)S(1)} %constant_dynamic-update-slice_fusion.2.refs_12_), channel_id=1, source_target_pairs={{0,8},{4,12},{8,0},{12,4},{16,24},{20,28},{24,16},{28,20},{1,9},{5... | collective-permute-start | bytes 1572872 | tf_op jit(solution)/shard_map/ppermute | solution.py:217
  10.3 12.5 %collective-permute-start.4 = (bf16[128,2048]{1,0:T(8,128)(2,1)S(1)}, bf16[128,2048]{1,0:T(8,128)(2,1)S(1)}, u32[]{:S(2)}, u32[]{:S(2)}) collective-permute-start(bf16[128,2048]{1,0:T(8,128)(2,1)S(1)} %constant_dynamic-update-slice_fusion.refs_8_), channel_id=1, source_target_pairs={{0,16},{4,20},{8,24},{12,28},{16,0},{20,4},{24,8},{28,12},{1,17},{... | collective-permute-start | bytes 1572872 | tf_op jit(solution)/shard_map/ppermute | solution.py:217
  11.2 10.1 %collective-permute-start = (bf16[64,2048]{1,0:T(8,128)(2,1)S(1)}, bf16[64,2048]{1,0:T(8,128)(2,1)S(1)}, u32[]{:S(2)}, u32[]{:S(2)}) collective-permute-start(bf16[64,2048]{1,0:T(8,128)(2,1)S(1)} %copy-done), channel_id=1, source_target_pairs={{0,1},{1,0},{2,3},{3,2},{4,5},{5,4},{6,7},{7,6},{8,9},{9,8},{10,11... | collective-permute-start | bytes 786440 | tf_op jit(solution)/shard_map/ppermute | solution.py:217
  11.7 12.9 %collective-permute-start.1 = (bf16[64,2048]{1,0:T(8,128)(2,1)S(1)}, bf16[64,2048]{1,0:T(8,128)(2,1)S(1)}, u32[]{:S(2)}, u32[]{:S(2)}) collective-permute-start(bf16[64,2048]{1,0:T(8,128)(2,1)S(1)} %copy-done), channel_id=1, source_target_pairs={{0,2},{1,3},{2,0},{3,1},{4,6},{5,7},{6,4},{7,5},{8,10},{9,11},{10,... | collective-permute-start | bytes 786440 | tf_op jit(solution)/shard_map/ppermute | solution.py:217
  14.3 23.7 %collective-permute-start.5 = (bf16[128,2048]{1,0:T(8,128)(2,1)S(1)}, bf16[128,2048]{1,0:T(8,128)(2,1)S(1)}, u32[]{:S(2)}, u32[]{:S(2)}) collective-permute-start(bf16[128,2048]{1,0:T(8,128)(2,1)S(1)} %constant_dynamic-update-slice_fusion.refs_8_), channel_id=1, source_target_pairs={{0,4},{4,0},{8,12},{12,8},{16,20},{20,16},{24,28},{28,24},{1,5},{5... | collective-permute-start | bytes 1572872 | tf_op jit(solution)/shard_map/ppermute | solution.py:217
  21.3 0.7 copy-start.4
  22.0 15.9 %collective-permute-start.9 = (bf16[128,2048]{1,0:T(8,128)(2,1)S(1)}, bf16[128,2048]{1,0:T(8,128)(2,1)S(1)}, u32[]{:S(2)}, u32[]{:S(2)}) collective-permute-start(bf16[128,2048]{1,0:T(8,128)(2,1)S(1)} %constant_dynamic-update-slice_fusion.2.refs_12_), channel_id=1, source_target_pairs={{0,4},{4,0},{8,12},{12,8},{16,20},{20,16},{24,28},{28,24},{1,5},{5... | collective-permute-start | bytes 1572872 | tf_op jit(solution)/shard_map/ppermute | solution.py:217
  22.0 15.9 %collective-permute-start.10 = (bf16[128,2048]{1,0:T(8,128)(2,1)S(1)}, bf16[128,2048]{1,0:T(8,128)(2,1)}, u32[]{:S(2)}, u32[]{:S(2)}) collective-permute-start(bf16[128,2048]{1,0:T(8,128)(2,1)S(1)} %collective-permute-done.8.refs_13_), channel_id=1, source_target_pairs={{0,4},{4,0},{8,12},{12,8},{16,20},{20,16},{24,28},{28,24},{1,5},{5... | collective-permute-start | bytes 1572872 | tf_op jit(solution)/shard_map/ppermute | solution.py:217
  22.8 15.2 %collective-permute-start.6 = (bf16[128,2048]{1,0:T(8,128)(2,1)S(1)}, bf16[128,2048]{1,0:T(8,128)(2,1)}, u32[]{:S(2)}, u32[]{:S(2)}) collective-permute-start(bf16[128,2048]{1,0:T(8,128)(2,1)S(1)} %collective-permute-done.4.refs_9_), channel_id=1, source_target_pairs={{0,4},{4,0},{8,12},{12,8},{16,20},{20,16},{24,28},{28,24},{1,5},{5... | collective-permute-start | bytes 1572872 | tf_op jit(solution)/shard_map/ppermute | solution.py:217
  24.6 0.7 copy-start.6
  25.3 12.7 %collective-permute-start.2 = (bf16[64,2048]{1,0:T(8,128)(2,1)S(1)}, bf16[64,2048]{1,0:T(8,128)(2,1)}, u32[]{:S(2)}, u32[]{:S(2)}) collective-permute-start(bf16[64,2048]{1,0:T(8,128)(2,1)S(1)} %copy-done), channel_id=1, source_target_pairs={{0,3},{1,2},{2,1},{3,0},{4,7},{5,6},{6,5},{7,4},{8,11},{9,10},{10,... | collective-permute-start | bytes 786440 | tf_op jit(solution)/shard_map/ppermute | solution.py:217
  38.0 20.5 %collective-permute-start.21 = (s32[64]{0:T(128)S(1)}, s32[64]{0:T(128)S(1)}, u32[]{:S(2)}, u32[]{:S(2)}) collective-permute-start(s32[64]{0:T(128)S(1)} %broadcast_add_fusion), channel_id=1, source_target_pairs={{0,1},{1,0},{2,3},{3,2},{4,5},{5,4},{6,7},{7,6},{8,9},{9,8},{10,11... | collective-permute-start | bytes 776 | tf_op jit(solution)/shard_map/ppermute | solution.py:217
  38.0 1.0 copy-start.5
  39.0 0.9 copy-start.7
  39.9 50.5 %copy-start.18 = (f32[128]{0:T(128)S(1)}, f32[128]{0:T(128)}, u32[]{:S(2)}) copy-start(f32[128]{0:T(128)} %param.15) | copy-start | bytes 1540
  52.4 0.7 copy-start.2
  53.1 0.7 copy-start.11
  53.8 0.7 copy-start.13
  54.5 0.7 copy-start.15
  56.5 6.6 %collective-permute-start.17 = (f32[4,64]{1,0:T(4,128)S(1)}, f32[4,64]{1,0:T(4,128)S(1)}, u32[]{:S(2)}, u32[]{:S(2)}) collective-permute-start(f32[4,64]{1,0:T(4,128)S(1)} %reshape.52), channel_id=1, source_target_pairs={{0,1},{1,0},{2,3},{3,2},{4,5},{5,4},{6,7},{7,6},{8,9},{9,8},{10,11... | collective-permute-start | bytes 3080 | tf_op jit(solution)/shard_map/ppermute | solution.py:217
  58.6 7.4 %collective-permute-start.22 = (s32[128]{0:T(128)S(1)}, s32[128]{0:T(128)S(1)}, u32[]{:S(2)}, u32[]{:S(2)}) collective-permute-start(s32[128]{0:T(128)S(1)} %pad_add_fusion.1), channel_id=1, source_target_pairs={{0,2},{1,3},{2,0},{3,1},{4,6},{5,7},{6,4},{7,5},{8,10},{9,11},{10,... | collective-permute-start | bytes 1544 | tf_op jit(solution)/shard_map/ppermute | solution.py:217
  59.6 31.0 %collective-permute-start.14 = (bf16[64,2048]{1,0:T(8,128)(2,1)}, bf16[64,2048]{1,0:T(8,128)(2,1)S(1)}, u32[]{:S(2)}, u32[]{:S(2)}) collective-permute-start(bf16[64,2048]{1,0:T(8,128)(2,1)} %refs_1_.1), channel_id=1, source_target_pairs={{0,1},{1,0},{2,3},{3,2},{4,5},{5,4},{6,7},{7,6},{8,9},{9,8},{10,11... | collective-permute-start | bytes 786440 | tf_op jit(solution)/shard_map/ppermute | solution.py:217
  61.6 29.0 %collective-permute-start.15 = (bf16[64,2048]{1,0:T(8,128)(2,1)}, bf16[64,2048]{1,0:T(8,128)(2,1)S(1)}, u32[]{:S(2)}, u32[]{:S(2)}) collective-permute-start(bf16[64,2048]{1,0:T(8,128)(2,1)} %refs_1_.1), channel_id=1, source_target_pairs={{0,2},{1,3},{2,0},{3,1},{4,6},{5,7},{6,4},{7,5},{8,10},{9,11},{10,... | collective-permute-start | bytes 786440 | tf_op jit(solution)/shard_map/ppermute | solution.py:217
  61.7 28.9 %collective-permute-start.16 = (bf16[64,2048]{1,0:T(8,128)(2,1)}, bf16[64,2048]{1,0:T(8,128)(2,1)S(1)}, u32[]{:S(2)}, u32[]{:S(2)}) collective-permute-start(bf16[64,2048]{1,0:T(8,128)(2,1)} %refs_1_.1), channel_id=1, source_target_pairs={{0,3},{1,2},{2,1},{3,0},{4,7},{5,6},{6,5},{7,4},{8,11},{9,10},{10,... | collective-permute-start | bytes 786440 | tf_op jit(solution)/shard_map/ppermute | solution.py:217
  63.1 19.7 %collective-permute-start.18 = (f32[4,64]{1,0:T(4,128)S(1)}, f32[4,64]{1,0:T(4,128)S(1)}, u32[]{:S(2)}, u32[]{:S(2)}) collective-permute-start(f32[4,64]{1,0:T(4,128)S(1)} %add.51), channel_id=1, source_target_pairs={{0,2},{1,3},{2,0},{3,1},{4,6},{5,7},{6,4},{7,5},{8,10},{9,11},{10,... | collective-permute-start | bytes 3080 | tf_op jit(solution)/shard_map/ppermute | solution.py:217
  66.0 18.8 %collective-permute-start.23 = (s32[256]{0:T(256)S(1)}, s32[256]{0:T(256)S(1)}, u32[]{:S(2)}, u32[]{:S(2)}) collective-permute-start(s32[256]{0:T(256)S(1)} %pad_add_fusion), channel_id=1, source_target_pairs={{0,4},{4,8},{8,12},{12,16},{16,20},{20,24},{24,28},{1,5},{5,9},{9,... | collective-permute-start | bytes 3080 | tf_op jit(solution)/shard_map/ppermute | solution.py:274
  82.8 4.4 %collective-permute-start.24 = (s32[256]{0:T(256)S(1)}, s32[256]{0:T(256)S(1)}, u32[]{:S(2)}, u32[]{:S(2)}) collective-permute-start(s32[256]{0:T(256)S(1)} %pad_add_fusion), channel_id=1, source_target_pairs={{4,0},{8,4},{12,8},{16,12},{20,16},{24,20},{28,24},{5,1},{9,5},{13... | collective-permute-start | bytes 3080 | tf_op jit(solution)/shard_map/ppermute | solution.py:275
  84.9 5.7 %collective-permute-start.19 = (f32[1,256]{1,0:T(1,128)S(1)}, f32[1,256]{1,0:T(1,128)S(1)}, u32[]{:S(2)}, u32[]{:S(2)}) collective-permute-start(f32[1,256]{1,0:T(1,128)S(1)} %add_add_fusion.refs_5_), channel_id=1, source_target_pairs={{0,4},{4,8},{8,12},{12,16},{16,20},{20,24},{24,28},{1,5},{5,9},{9,... | collective-permute-start | bytes 3080 | tf_op jit(solution)/shard_map/ppermute | solution.py:306
  87.3 4.5 %collective-permute-start.20 = (f32[1,256]{1,0:T(1,128)S(1)}, f32[1,256]{1,0:T(1,128)S(1)}, u32[]{:S(2)}, u32[]{:S(2)}) collective-permute-start(f32[1,256]{1,0:T(1,128)S(1)} %add_add_fusion.refs_5_), channel_id=1, source_target_pairs={{4,0},{8,4},{12,8},{16,12},{20,16},{24,20},{28,24},{5,1},{9,5},{13... | collective-permute-start | bytes 3080 | tf_op jit(solution)/shard_map/ppermute | solution.py:307
  91.8 1.0 copy-start.8
  102.8 1.0 copy-start.1
  103.8 34.5 %copy-start.16 = (bf16[64,2048]{1,0:T(8,128)(2,1)S(1)}, bf16[64,2048]{1,0:T(8,128)(2,1)}, u32[]{:S(2)}) copy-start(bf16[64,2048]{1,0:T(8,128)(2,1)} %copy-done.15) | copy-start | bytes 786436
  103.8 37.7 %copy-start.14 = (bf16[64,2048]{1,0:T(8,128)(2,1)S(1)}, bf16[64,2048]{1,0:T(8,128)(2,1)}, u32[]{:S(2)}) copy-start(bf16[64,2048]{1,0:T(8,128)(2,1)} %copy-done.13) | copy-start | bytes 786436
  103.8 37.9 %copy-start.12 = (bf16[64,2048]{1,0:T(8,128)(2,1)S(1)}, bf16[64,2048]{1,0:T(8,128)(2,1)}, u32[]{:S(2)}) copy-start(bf16[64,2048]{1,0:T(8,128)(2,1)} %copy-done.11) | copy-start | bytes 786436
  134.7 8.4 %collective-permute-start.31 = (bf16[256,2048]{1,0:T(8,128)(2,1)S(1)}, bf16[256,2048]{1,0:T(8,128)(2,1)S(1)}, u32[]{:S(2)}, u32[]{:S(2)}) collective-permute-start(bf16[256,2048]{1,0:T(8,128)(2,1)S(1)} %get-tuple-element.45), channel_id=1, source_target_pairs={{0,4},{4,0},{8,12},{12,8},{16,20},{20,16},{24,28},{28,24},{1,5},{5... | collective-permute-start | bytes 3145736 | tf_op jit(solution)/shard_map/ppermute | solution.py:217
  138.2 8.1 %collective-permute-start.28 = (bf16[256,2048]{1,0:T(8,128)(2,1)S(1)}, bf16[256,2048]{1,0:T(8,128)(2,1)S(1)}, u32[]{:S(2)}, u32[]{:S(2)}) collective-permute-start(bf16[256,2048]{1,0:T(8,128)(2,1)S(1)} %get-tuple-element.43), channel_id=1, source_target_pairs={{0,4},{4,0},{8,12},{12,8},{16,20},{20,16},{24,28},{28,24},{1,5},{5... | collective-permute-start | bytes 3145736 | tf_op jit(solution)/shard_map/ppermute | solution.py:217
  138.3 14.3 %collective-permute-start.11 = (bf16[64,2048]{1,0:T(8,128)(2,1)S(1)}, bf16[64,2048]{1,0:T(8,128)(2,1)S(1)}, u32[]{:S(2)}, u32[]{:S(2)}) collective-permute-start(bf16[64,2048]{1,0:T(8,128)(2,1)S(1)} %copy-done.16), channel_id=1, source_target_pairs={{0,1},{1,0},{2,3},{3,2},{4,5},{5,4},{6,7},{7,6},{8,9},{9,8},{10,11... | collective-permute-start | bytes 786440 | tf_op jit(solution)/shard_map/ppermute | solution.py:217
  141.6 17.9 %collective-permute-start.12 = (bf16[64,2048]{1,0:T(8,128)(2,1)S(1)}, bf16[64,2048]{1,0:T(8,128)(2,1)S(1)}, u32[]{:S(2)}, u32[]{:S(2)}) collective-permute-start(bf16[64,2048]{1,0:T(8,128)(2,1)S(1)} %copy-done.14), channel_id=1, source_target_pairs={{0,2},{1,3},{2,0},{3,1},{4,6},{5,7},{6,4},{7,5},{8,10},{9,11},{10,... | collective-permute-start | bytes 786440 | tf_op jit(solution)/shard_map/ppermute | solution.py:217
  141.7 36.7 %collective-permute-start.13 = (bf16[64,2048]{1,0:T(8,128)(2,1)S(1)}, bf16[64,2048]{1,0:T(8,128)(2,1)S(1)}, u32[]{:S(2)}, u32[]{:S(2)}) collective-permute-start(bf16[64,2048]{1,0:T(8,128)(2,1)S(1)} %copy-done.12), channel_id=1, source_target_pairs={{0,3},{1,2},{2,1},{3,0},{4,7},{5,6},{6,5},{7,4},{8,11},{9,10},{10,... | collective-permute-start | bytes 786440 | tf_op jit(solution)/shard_map/ppermute | solution.py:217
  143.1 36.1 %collective-permute-start.25 = (bf16[64,2048]{1,0:T(8,128)(2,1)S(1)}, bf16[64,2048]{1,0:T(8,128)(2,1)S(1)}, u32[]{:S(2)}, u32[]{:S(2)}) collective-permute-start(bf16[64,2048]{1,0:T(8,128)(2,1)S(1)} %get-tuple-element.35), channel_id=1, source_target_pairs={{0,1},{1,0},{2,3},{3,2},{4,5},{5,4},{6,7},{7,6},{8,9},{9,8},{10,11... | collective-permute-start | bytes 786440 | tf_op jit(solution)/shard_map/ppermute | solution.py:217
  146.4 43.9 %collective-permute-start.32 = (bf16[128,2048]{1,0:T(8,128)(2,1)S(1)}, bf16[128,2048]{1,0:T(8,128)(2,1)S(1)}, u32[]{:S(2)}, u32[]{:S(2)}) collective-permute-start(bf16[128,2048]{1,0:T(8,128)(2,1)S(1)} %slice.52), channel_id=1, source_target_pairs={{0,8},{4,12},{8,0},{12,4},{16,24},{20,28},{24,16},{28,20},{1,9},{5... | collective-permute-start | bytes 1572872 | tf_op jit(solution)/shard_map/ppermute | solution.py:217
  146.5 31.9 %copy-start.3 = (bf16[64,2048]{1,0:T(8,128)(2,1)S(1)}, bf16[64,2048]{1,0:T(8,128)(2,1)}, u32[]{:S(2)}) copy-start(bf16[64,2048]{1,0:T(8,128)(2,1)} %copy-done.2) | copy-start | bytes 786436
  152.6 29.5 %collective-permute-start.26 = (bf16[64,2048]{1,0:T(8,128)(2,1)S(1)}, bf16[64,2048]{1,0:T(8,128)(2,1)S(1)}, u32[]{:S(2)}, u32[]{:S(2)}) collective-permute-start(bf16[64,2048]{1,0:T(8,128)(2,1)S(1)} %get-tuple-element.36), channel_id=1, source_target_pairs={{0,2},{1,3},{2,0},{3,1},{4,6},{5,7},{6,4},{7,5},{8,10},{9,11},{10,... | collective-permute-start | bytes 786440 | tf_op jit(solution)/shard_map/ppermute | solution.py:217
  159.5 29.6 %collective-permute-start.27 = (bf16[64,2048]{1,0:T(8,128)(2,1)S(1)}, bf16[64,2048]{1,0:T(8,128)(2,1)S(1)}, u32[]{:S(2)}, u32[]{:S(2)}) collective-permute-start(bf16[64,2048]{1,0:T(8,128)(2,1)S(1)} %get-tuple-element.37), channel_id=1, source_target_pairs={{0,3},{1,2},{2,1},{3,0},{4,7},{5,6},{6,5},{7,4},{8,11},{9,10},{10,... | collective-permute-start | bytes 786440 | tf_op jit(solution)/shard_map/ppermute | solution.py:217
  178.3 13.0 %collective-permute-start.29 = (bf16[128,2048]{1,0:T(8,128)(2,1)S(1)}, bf16[128,2048]{1,0:T(8,128)(2,1)S(1)}, u32[]{:S(2)}, u32[]{:S(2)}) collective-permute-start(bf16[128,2048]{1,0:T(8,128)(2,1)S(1)} %slice.53), channel_id=1, source_target_pairs={{0,16},{4,20},{8,24},{12,28},{16,0},{20,4},{24,8},{28,12},{1,17},{... | collective-permute-start | bytes 1572872 | tf_op jit(solution)/shard_map/ppermute | solution.py:217
  190.4 7.9 %collective-permute-start.33 = (bf16[64,2048]{1,0:T(8,128)(2,1)S(1)}, bf16[64,2048]{1,0:T(8,128)(2,1)S(1)}, u32[]{:S(2)}, u32[]{:S(2)}) collective-permute-start(bf16[64,2048]{1,0:T(8,128)(2,1)S(1)} %slice.54), channel_id=1, source_target_pairs={{0,16},{4,20},{8,24},{12,28},{16,0},{20,4},{24,8},{28,12},{1,17},{... | collective-permute-start | bytes 786440 | tf_op jit(solution)/shard_map/ppermute | solution.py:217
  191.5 7.7 %collective-permute-start.30 = (bf16[64,2048]{1,0:T(8,128)(2,1)S(1)}, bf16[64,2048]{1,0:T(8,128)(2,1)S(1)}, u32[]{:S(2)}, u32[]{:S(2)}) collective-permute-start(bf16[64,2048]{1,0:T(8,128)(2,1)S(1)} %slice.55), channel_id=1, source_target_pairs={{0,8},{4,12},{8,0},{12,4},{16,24},{20,28},{24,16},{28,20},{1,9},{5... | collective-permute-start | bytes 786440 | tf_op jit(solution)/shard_map/ppermute | solution.py:217

commit v2 on v0

v2 whole, which is shorter than its diff:
```python
import functools
import math

import jax
import jax.numpy as jnp
from jax import lax
from jax.experimental import pallas as pl
from jax.experimental.pallas import tpu as pltpu
from jax.sharding import PartitionSpec as P

BLK = 128
EPS = 1e-06
LOSS_WEIGHT = 8.0
GELU_A = math.sqrt(2.0 / math.pi)
GELU_B = 0.044715
VMEM_BYTES = 32 * 1024 * 1024
BF16 = jnp.bfloat16
F32 = jnp.float32
NN = (((1,), (0,)), ((), ()))
NT = (((1,), (1,)), ((), ()))
TN = (((0,), (0,)), ((), ()))


def dot(a, b, dims=NN):
    return lax.dot_general(a, b, dims, preferred_element_type=F32)


def block(b):
    return slice(b * BLK, (b + 1) * BLK)


def column(j):
    return pl.ds(pl.multiple_of(j * BLK, BLK), BLK)


def bits_of(n):
    return [1 << b for b in range(n.bit_length() - 1)]


def three_terms(row):
    hi = row.astype(BF16)
    rest = row - hi.astype(F32)
    mid = rest.astype(BF16)
    low = (rest - mid.astype(F32)).astype(BF16)
    pad = jnp.zeros((8 - 3, row.shape[1]), F32).astype(BF16)
    return jnp.concatenate([hi, mid, low, pad], axis=0)


def load_weight(place, parts, masks, which, whole, sem):
    core = place[0] & 1
    for part, ms in zip(parts, masks):
        depth = part.shape[0] // (2 * len(ms))
        for i, (even, odd) in enumerate(ms):
            owner = place[0] ^ jnp.where(core == 0, even, odd)
            at = pl.multiple_of(owner * depth, depth)
            pltpu.make_async_copy(
                part.at[pl.ds((2 * i + which) * depth, depth)], whole.at[pl.ds(at, depth)], sem
            ).start()
    return lambda: pltpu.make_async_copy(whole, whole, sem).wait()


def load(src, dst, sem):
    copy = pltpu.make_async_copy(src, dst, sem)
    copy.start()
    return copy.wait


def loop(nj, unroll=4):
    return pl.loop(0, nj, unroll=math.gcd(nj, unroll))


def spread(acc, outs, rows):
    for b in range(acc.shape[0]):
        part = acc[b].astype(BF16)
        for d, out in enumerate(outs):
            out[:, block(b)] = part[d * rows : (d + 1) * rows]


def forward_kernel(masks, nf, *refs):
    idx, place = refs[:2]
    xs, refs = refs[2 : 2 + nf], refs[2 + nf:]
    gain, readout, ids = refs[:3]
    parts, refs = refs[3 : 3 + len(masks)], refs[3 + len(masks):]
    normed_out, act_out, dact_out, score = refs[:4]
    branch_out, refs = refs[4 : 4 + nf], refs[4 + nf:]
    xbuf, normed, act, dact, win, wout, acc, branch, sems = refs
    rows = ids.shape[1]
    fb = normed.shape[0]
    nj, kb = idx.shape
    waits = [load(xs[d], xbuf.at[d], sems.at[d]) for d in range(nf)]
    win_wait = load_weight(place, parts, masks, 0, win, sems.at[nf])
    wout_wait = load_weight(place, parts, masks, 1, wout, sems.at[nf + 1])
    acc[...] = jnp.zeros_like(acc)
    own = jnp.zeros((8, rows), F32)
    for d in range(nf):
        waits[d]()
        x = xbuf[d].astype(F32)
        inv = lax.rsqrt(jnp.mean(x * x, axis=1, keepdims=True) + EPS)
        n = (x * inv * gain[...]).astype(BF16)
        for b in range(fb):
            normed[b, d * rows : (d + 1) * rows, :] = n[:, block(b)]
            if d == 0:
                own = own + dot(three_terms(readout[:, block(b)]), xbuf[0, :, block(b)], NT)
    normed_wait = load(normed, normed_out, sems.at[nf + 2])
    win_wait()
    wout_wait()

    @loop(nj)
    def _(j):
        which = [idx[j, k] for k in range(kb)]
        picked = jnp.concatenate([normed[w] for w in which], axis=1)
        v = dot(picked, win[:, column(j)])
        v2 = v * v
        t = jnp.tanh(GELU_A * v * (1.0 + GELU_B * v2))
        half = 0.5 * (1.0 + t)
        a = (v * half).astype(BF16)
        act[j] = a
        dact[j] = half + 0.5 * v * (1.0 - t * t) * (GELU_A * (1.0 + 3.0 * GELU_B * v2))
        terms = dot(a, wout[:, column(j)], NT)
        for k, w in enumerate(which):
            acc[w] += terms[:, block(k)]

    act_wait = load(act, act_out, sems.at[nf + 3])
    dact_wait = load(dact, dact_out, sems.at[nf + 4])
    spread(acc, [branch.at[d] for d in range(nf)], rows)
    waits = [load(branch.at[d], branch_out[d], sems.at[d]) for d in range(nf)]
    total = jnp.zeros((8, nf * rows), F32)
    for b in range(fb):
        total = total + dot(three_terms(readout[:, block(b)]), acc[b].astype(BF16), NT)
    own = jnp.sum(own, axis=0, keepdims=True)
    pad = jnp.zeros((1, (nf - 1) * rows), F32)
    row = jnp.sum(total, axis=0, keepdims=True) + jnp.concatenate([own, pad], axis=1)
    score[...] = jnp.concatenate([row, ids[...].astype(F32) + 1.0], axis=1)
    for wait in waits + [normed_wait, act_wait, dact_wait]:
        wait()


def store_grads(idx, place, orders, scale, left, right, keep, send):
    nj, kb = idx.shape
    count = 2 << len(orders[0])
    depth = kb * BLK // count
    per = BLK // depth
    core = place[0] & 1

    def slot(owner, order):
        m = place[0] ^ owner
        pos = 0
        for bit in order:
            pos = 2 * pos + jnp.where((m & bit) != 0, 1, 0)
        return pos * depth

    def slots(own):
        return [
            pl.multiple_of(jnp.where(own == 0, slot(2 * q, orders[0]), slot(2 * q, orders[1])), depth)
            for q in range(count // 2)
        ]

    keep_at, send_at = slots(core), slots(1 - core)

    @loop(nj)
    def _(j):
        for k in range(kb):
            g = (dot(left[idx[j, k]], right[j], TN) * scale).astype(BF16)
            for half in range(per // 2):
                q = k * (per // 2) + half
                even = g[2 * half * depth : (2 * half + 1) * depth]
                odd = g[(2 * half + 1) * depth : (2 * half + 2) * depth]
                keep[pl.ds(keep_at[q], depth), column(j)] = jnp.where(core == 0, even, odd)
                send[pl.ds(send_at[q], depth), column(j)] = jnp.where(core == 0, odd, even)


def upper_kernel(masks, nf, *refs):
    idx, place = refs[:2]
    ups, refs = refs[2 : 2 + nf], refs[2 + nf:]
    readout, refs = refs[0], refs[1:]
    parts, refs = refs[: len(masks)], refs[len(masks):]
    upper_out, turn, pattern, ubuf, up, wout, upper, flat, sems = refs
    nj, kb = idx.shape
    fb = up.shape[0]
    rows = ubuf.shape[1]
    depth = pattern.shape[0]
    waits = [load(ups[d], ubuf.at[d], sems.at[d]) for d in range(nf)]
    wout_wait = load_weight(place, parts, masks, 1, wout, sems.at[nf])
    for d in range(nf):
        waits[d]()
        for b in range(fb):
            up[b, d * rows : (d + 1) * rows, :] = ubuf[d, :, block(b)]
    wout_wait()

    @loop(nj)
    def _(j):
        which = [idx[j, k] for k in range(kb)]
        picked = jnp.concatenate([up[w] for w in which], axis=1)
        upper[j] = dot(picked, wout[:, column(j)])
        pltpu.make_async_copy(upper.at[j], upper_out.at[j], sems.at[nf + 1]).start()
        turned = jnp.concatenate([three_terms(readout[:, column(w)]) for w in which], axis=1)
        turn[:, column(j)] = jnp.sum(dot(turned, wout[:, column(j)]), axis=0, keepdims=True)

    first = place[0] * depth
    for j in range(nj):
        row = readout[:, column(idx[j, first // BLK])]
        flat[...] = jnp.transpose(jnp.broadcast_to(row, (BLK, BLK)))
        pattern[:, block(j)] = flat[pl.ds(pl.multiple_of(first % BLK, depth), depth), :]
    pltpu.make_async_copy(upper, upper_out, sems.at[nf + 1]).wait()


def fixed_grads_kernel(orders, scale, nf, *refs):
    idx, place = refs[:2]
    ups, refs = refs[2 : 2 + nf], refs[2 + nf:]
    act_in, keep, send, ubuf, up, act, sems = refs
    rows = ubuf.shape[1]
    waits = [load(ups[d], ubuf.at[d], sems.at[d]) for d in range(nf)]
    act_wait = load(act_in, act, sems.at[nf])
    for d in range(nf):
        waits[d]()
        for b in range(up.shape[0]):
            up[b, d * rows : (d + 1) * rows, :] = ubuf[d, :, block(b)]
    act_wait()
    store_grads(idx, place, orders, scale, up, act, keep, send)


def backward_kernel(masks, orders, scale, nf, *refs):
    idx, place, here, left, right, teacher, turn, upper_in, dact_in, normed_in, act_in = refs[:11]
    parts, refs = refs[11 : 11 + len(masks)], refs[11 + len(masks):]
    own_coeff, along, keep, send = refs[:4]
    outs, refs = refs[4 : 4 + nf], refs[4 + nf:]
    upper, dact, normed, act, pre_grad, win, acc, sems = refs
    nj, kb = idx.shape
    rows = outs[0].shape[0]
    tokens = nf * rows
    nseg = teacher.shape[0]
    upper_wait = load(upper_in, upper, sems.at[0])
    dact_wait = load(dact_in, dact, sems.at[1])
    win_wait = load_weight(place, parts, masks, 0, win, sems.at[2])
    normed_wait = load(normed_in, normed, sems.at[3])
    act_wait = load(act_in, act, sems.at[4])
    acc[...] = jnp.zeros_like(acc)
    seg = (lax.broadcasted_iota(jnp.int32, (nseg, tokens), 0) + 1).astype(F32)
    sums = jnp.zeros((nseg, 1), F32)
    counts = jnp.zeros((nseg, 1), F32)
    for group in (here, left, right):
        member = group[:, tokens:] == seg
        sums = sums + jnp.sum(jnp.where(member, group[:, :tokens], 0.0), axis=1, keepdims=True)
        counts = counts + jnp.sum(jnp.where(member, 1.0, 0.0), axis=1, keepdims=True)
    misfit = sums / jnp.maximum(counts, 1.0) - teacher[...]
    coeff = 2.0 * LOSS_WEIGHT * jnp.sum(
        jnp.where(here[:, tokens:] == seg, misfit, 0.0), axis=0, keepdims=True
    )
    terms_of = three_terms(coeff * scale)
    across = jnp.transpose(jnp.broadcast_to(coeff, (BLK, tokens)))
    own_coeff[...] = across[:rows]
    upper_wait()
    dact_wait()
    win_wait()

    @loop(nj)
    def _(j):
        p = ((upper[j] + across * turn[:, column(j)]) * dact[j]).astype(BF16)
        pre_grad[j] = p
        terms = dot(p, win[:, column(j)], NT)
        for k in range(kb):
            acc[idx[j, k]] += terms[:, block(k)]

    spread(acc, outs, rows)
    normed_wait()
    store_grads(idx, place, orders, scale, normed, pre_grad, keep, send)
    act_wait()
    for j in range(nj):
        along[:, block(j)] = jnp.sum(dot(terms_of, act[j]), axis=0, keepdims=True)


def finish_kernel(x_ref, gain, upstream, readout, own_coeff, own, other, out):
    x = x_ref[...].astype(F32)
    inv = lax.rsqrt(jnp.mean(x * x, axis=1, keepdims=True) + EPS)
    g = (own[...] + other[...].astype(F32)) * gain[...]
    inner = jnp.mean(g * x, axis=1, keepdims=True)
    back = inv * g - x * (inv * inv * inv) * inner
    for b in range(x.shape[1] // BLK):
        cot = upstream[:, block(b)].astype(F32) + own_coeff[...] * readout[:, block(b)]
        out[:, block(b)] = (cot.astype(BF16).astype(F32) + back[:, block(b)]).astype(BF16)


VM = pl.BlockSpec(memory_space=pltpu.VMEM)
SM = pl.BlockSpec(memory_space=pltpu.SMEM)
HBM = pl.BlockSpec(memory_space=pltpu.HBM)


def call(body, outs, args, scratch, flops):
    return pl.pallas_call(
        body,
        out_shape=[pltpu.HBM(o.shape, o.dtype) if m is HBM else o for m, o in outs],
        in_specs=[m for m, _ in args],
        out_specs=[m for m, _ in outs],
        scratch_shapes=scratch,
        compiler_params=pltpu.CompilerParams(vmem_limit_bytes=VMEM_BYTES),
        cost_estimate=pl.CostEstimate(
            flops=flops,
            bytes_accessed=sum(math.prod(o.shape) * o.dtype.itemsize for _, o in outs),
            transcendentals=0,
        ),
    )(*[pltpu.with_memory_space_constraint(a, pltpu.HBM) if m is HBM else a for m, a in args])


def swap(value, axis, mask):
    n = lax.axis_size(axis)
    return lax.ppermute(value, axis, [(i, i ^ mask) for i in range(n)])


def swap_tok(value, even, odd):
    n = lax.axis_size("tok")
    return lax.ppermute(value, "tok", [(i, i ^ (odd if i & 1 else even)) for i in range(n)])


def after(value, *others):
    return lax.optimization_barrier((value, *others))[0]


def gather_tok(w_in, w_out, bits, ties):
    held, masks = [w_in, w_out], [[(0, 0)]]
    for step, (even, odd) in enumerate(zip(bits, bits[::-1])):
        whole = jnp.concatenate(held, axis=0)
        if step == len(bits) - 1:
            whole = after(whole, *ties[0])
        flat = [m for ms in masks for m in ms]
        held = [whole, swap_tok(whole, even, odd)]
        masks = [flat, [(a ^ even, b ^ odd) for a, b in flat]]
    other = [swap(after(h, *ties[1]), "tok", 1) for h in held]
    return held + other, masks + [[(b ^ 1, a ^ 1) for a, b in ms] for ms in masks]


def gather_feat(own, bits, far=None):
    held = {0: own}
    for bit in bits[::-1]:
        if bit == bits[-1] and far is not None:
            held[bit] = far
        else:
            held.update({
                m ^ bit: swap(held[m] if far is None else after(held[m], far), "feat", bit)
                for m in sorted(held)
            })
    return [held[d] for d in range(2 * bits[-1])]


def scatter_near(parts):
    held = {}
    for d in range(len(parts) - 2, 0, -2):
        held[d] = parts[d].astype(F32) + swap(parts[d + 1], "feat", 1).astype(F32)
    return held


def scatter_far(parts, held, bits, tie):
    firsts = [held[d] for d in sorted(held)]
    held = dict(held)
    held[0] = parts[0].astype(F32) + swap(after(parts[1], *firsts), "feat", 1).astype(F32)
    for bit in bits[1:]:
        stay = [d for d in held if not d & bit]
        for d in sorted(stay, reverse=True):
            got = swap(after(held[d | bit].astype(BF16), tie), "feat", bit)
            if d == 0 and bit == bits[-1]:
                return held[0], got
            held[d] = held[d] + got.astype(F32)
        held = {d: held[d] for d in stay}


def on_device(
    inputs, norm_gain, w_in, w_out, block_index, segment_ids, teacher_scores, upstream, readout
):
    rows, width = inputs.shape
    nt, nf = lax.axis_size("tok"), lax.axis_size("feat")
    nj, kb = block_index.shape
    hidden = w_in.shape[1]
    fb = width // BLK
    depth = w_in.shape[0]
    tokens = rows * nf
    grad_scale = 1.0 / math.sqrt(tokens * nt)
    bits = bits_of(nt)[1:]
    orders = (bits, bits[::-1])
    feat_bits = bits_of(nf)
    place = lax.axis_index("tok").astype(jnp.int32).reshape(1)
    gain_row, readout_row = norm_gain.reshape(1, width), readout.reshape(1, width)
    flops = 2 * tokens * hidden * kb * BLK
    sds = jax.ShapeDtypeStruct
    scalars = [(SM, block_index), (SM, place)]

    xs = gather_feat(inputs, feat_bits)
    near, far = xs[1], xs[feat_bits[-1]]
    upstream_far = swap(after(upstream, near, far), "feat", feat_bits[-1])
    ups = gather_feat(upstream, feat_bits, upstream_far)
    parts, masks = gather_tok(
        w_in, w_out, bits, ((near, far), xs[2:] + [upstream_far])
    )
    parts = [(HBM, p) for p in parts]

    by_feature = pltpu.VMEM((fb, tokens, BLK), BF16)
    by_hidden = pltpu.VMEM((nj, tokens, BLK), BF16)
    by_hidden_wide = pltpu.VMEM((nj, tokens, BLK), F32)
    weight = pltpu.VMEM((kb * BLK, hidden), BF16)
    summed = pltpu.VMEM((fb, tokens, BLK), F32)
    piece = sds((rows, width), BF16)
    half_grad = sds((kb * BLK // 2, hidden), BF16)

    outs = call(
        functools.partial(forward_kernel, masks, nf),
        [
            (HBM, sds((fb, tokens, BLK), BF16)),
            (HBM, sds((nj, tokens, BLK), BF16)),
            (HBM, sds((nj, tokens, BLK), F32)),
            (VM, sds((1, tokens + rows), F32)),
        ]
        + [(HBM, piece)] * nf,
        scalars
        + [(HBM, x) for x in xs]
        + [(VM, gain_row), (VM, readout_row), (VM, segment_ids.reshape(1, rows))]
        + parts,
        [
            pltpu.VMEM((nf, rows, width), BF16),
            by_feature,
            by_hidden,
            by_hidden_wide,
            weight,
            weight,
            summed,
            pltpu.VMEM((nf, rows, width), BF16),
            pltpu.SemaphoreType.DMA((nf + 5,)),
        ],
        2 * flops,
    )
    normed, act, dact, here = outs[:4]
    branch = outs[4:]

    upper, turn, pattern = call(
        functools.partial(upper_kernel, masks, nf),
        [
            (HBM, sds((nj, tokens, BLK), F32)),
            (VM, sds((1, hidden), F32)),
            (VM, sds((depth, hidden), F32)),
        ],
        scalars + [(HBM, u) for u in ups] + [(VM, readout_row)] + parts,
        [
            pltpu.VMEM((nf, rows, width), BF16),
            by_feature,
            weight,
            by_hidden_wide,
            pltpu.VMEM((BLK, BLK), F32),
            pltpu.SemaphoreType.DMA((nf + 2,)),
        ],
        flops,
    )
    keep_out, send_out = call(
        functools.partial(fixed_grads_kernel, orders, grad_scale, nf),
        [(VM, half_grad), (VM, half_grad)],
        scalars + [(HBM, u) for u in ups] + [(HBM, act)],
        [
            pltpu.VMEM((nf, rows, width), BF16),
            by_feature,
            by_hidden,
            pltpu.SemaphoreType.DMA((nf + 1,)),
        ],
        flops,
    )
    branch_near = scatter_near(branch)
    firsts = [branch_near[d] for d in sorted(branch_near)]
    for step, bit in enumerate(feat_bits):
        ties = ups[1:] if step == 0 else [keep_out, turn] + firsts
        there = swap(after(here, *ties), "feat", bit)
        turned = jnp.flip(there[:, :tokens].reshape(nf // (2 * bit), 2, bit * rows), axis=1)
        here = jnp.concatenate(
            [here[:, :tokens] + turned.reshape(1, tokens), here[:, tokens:], there[:, tokens:]],
            axis=1,
        )
    left = lax.ppermute(here, "tok", [(i, i + 1) for i in range(nt - 1)])
    right = lax.ppermute(here, "tok", [(i + 1, i) for i in range(nt - 1)])

    own, got = scatter_far(branch, branch_near, feat_bits, here)
    branch_sum = own + got.astype(F32)
    layer_out = (inputs.astype(F32) + branch_sum).astype(BF16)
    total_out = keep_out.astype(F32) + swap(send_out, "tok", 1).astype(F32)
    even, odd = bits[0], bits[-1]
    half = total_out.shape[0] // 2
    total_out = total_out[:half] + swap_tok(total_out[half:].astype(BF16), even, odd).astype(F32)

    outs = call(
        functools.partial(backward_kernel, masks, orders, grad_scale, nf),
        [
            (VM, sds((rows, BLK), F32)),
            (VM, sds((1, hidden), F32)),
            (VM, half_grad),
            (VM, half_grad),
        ]
        + [(VM, piece)] * nf,
        scalars
        + [(VM, here), (VM, left), (VM, right), (VM, teacher_scores.reshape(-1, 1)), (VM, turn)]
        + [(HBM, upper), (HBM, dact), (HBM, normed), (HBM, act)]
        + parts,
        [
            by_hidden_wide,
            by_hidden_wide,
            by_feature,
            by_hidden,
            by_hidden,
            weight,
            summed,
            pltpu.SemaphoreType.DMA((5,)),
        ],
        2 * flops,
    )
    own_coeff, along, keep_in, send_in = outs[:4]
    back = outs[4:]
    back_near = scatter_near(back)
    own, got = scatter_far(back, back_near, feat_bits, layer_out)

    send_in = after(send_in, layer_out, total_out)
    total = keep_in.astype(F32) + swap(send_in, "tok", 1).astype(F32)
    along = along + swap(along, "tok", 1)
    rest = list(zip(bits, bits[::-1]))
    for step, (even, odd) in enumerate(rest):
        half = total.shape[0] // 2
        away = after(total[half:].astype(BF16), along, total_out)
        along = along + swap_tok(after(along, total), even, odd)
        if step + 1 < len(rest):
            cut = total_out.shape[0] // 2
            got_out = swap_tok(after(total_out[cut:], total).astype(BF16), *rest[step + 1])
            total_out = total_out[:cut] + got_out.astype(F32)
        total = total[:half] + swap_tok(away, even, odd).astype(F32)
    grad_in = total
    grad_out = total_out + pattern * along
    (input_grad,) = call(
        finish_kernel,
        [(VM, piece)],
        [
            (VM, a)
            for a in (inputs, gain_row, upstream, readout_row, own_coeff, own, got)
        ],
        [],
        rows * width,
    )
    return (layer_out, input_grad, grad_in, grad_out)


def solution(mesh):
    return jax.shard_map(
        on_device,
        mesh=mesh,
        in_specs=(
            P(("tok", "feat"), None),
            P(),
            P("tok", "feat"),
            P("tok", "feat"),
            P("feat", None),
            P(("tok", "feat")),
            P(),
            P(("tok", "feat"), None),
            P(),
        ),
        out_specs=(
            P(("tok", "feat"), None),
            P(("tok", "feat"), None),
            P("tok", "feat"),
            P("tok", "feat"),
        ),
        check_vma=False,
    )
```

time: 402 us -> 120 us (0.30)
  waiting for transfers between devices: 218 us -> 44.2 us
  matrix products: 60.8 us -> 0 us
  local copies, waits for them, and re-layouts: 55.7 us -> 1.46 us
  blocking collectives: 38.8 us -> 0 us
  starting transfers between devices: 0.32 us -> 35.6 us
  Pallas kernels: 0 us -> 29.3 us
  between operations: 14.3 us -> 1.01 us
    reduce_scatter x4 -> x0, waiting for transfers between devices: 120 us -> none  [the longest x1 43.1 us: on_device(): lax.psum_scatter(arrange(out_terms).astype(jnp.bfloat16), 'tok', scatter_...]
    all_gather x4 -> x0, waiting for transfers between devices: 96.6 us -> none  [the longest x1 29.2 us: on_device(): normed_rows = lax.all_gather(normed, 'feat', axis=0, tiled=True)]
    dot_general x12 -> x0, matrix products: 60.8 us -> none  [the longest x2 24 us: spread(): jnp.einsum('rjkc,jkd->rdc', grouped, sel_wide, precision=lax.Precision.HI...]
    ppermute x0 -> x29, waiting for transfers between devices: none -> 44.2 us  [the longest x19 32.3 us: swap(): return lax.ppermute(value, axis, [(i, i ^ mask) for i in range(n)])]
    psum x1 -> x0, blocking collectives: 38.8 us -> none  [on_device(): lax.psum((score_sums, token_counts), ('tok', 'feat'))]
    ppermute x0 -> x29, starting transfers between devices: none -> 35.6 us  [the longest x19 19.7 us: swap(): return lax.ppermute(value, axis, [(i, i ^ mask) for i in range(n)])]
    pallas_call x0 -> x5, Pallas kernels: none -> 29.3 us  [call(): pl.pallas_call(body, out_shape=[pltpu.HBM(o.shape, o.dtype) if m is HBM e...]
    convert_element_type x4 -> x0, local copies, waits for them, and re-layouts: 21.5 us -> none  [the longest x2 15 us: select(): picked.astype(jnp.bfloat16).reshape(group_rows, blocks_here, picked_width)]
  transfers between devices with their start and end apart: 8 -> 29, of which waited for: 8 -> 13; matrix products, arithmetic and copies ran while one was open for 10% -> 5% of each run, Pallas kernels for 0% -> 21%
where the time goes in v2:
time: 120 us
  waiting for transfers between devices  44.2 us (37%)
  starting transfers between devices  35.6 us (30%)
  Pallas kernels  29.3 us (24%)
  other arithmetic  8.36 us (7%)
  local copies, waits for them, and re-layouts  1.46 us (1%)
    ppermute x19, waiting for transfers between devices, swap(): return lax.ppermute(value, axis, [(i, i ^ mask) for i in range(n)])  32.3 us
    pallas_call x5, Pallas kernels, call(): pl.pallas_call(body, out_shape=[pltpu.HBM(o.shape, o.dtype) if m is HBM e...  29.3 us
    ppermute x19, starting transfers between devices, swap(): return lax.ppermute(value, axis, [(i, i ^ mask) for i in range(n)])  19.7 us
    ppermute x8, starting transfers between devices, swap_tok(): lax.ppermute(value, 'tok', [(i, i ^ (odd if i & 1 else even)) for i in ra...  13.2 us
    ppermute x8, waiting for transfers between devices, swap_tok(): lax.ppermute(value, 'tok', [(i, i ^ (odd if i & 1 else even)) for i in ra...  11.9 us
  transfers between devices with their start and end apart: 29, of which 13 were waited for; matrix products, arithmetic and copies ran while one was open for 5% of the time, Pallas kernels for 21%

profile of v2, /device:TPU:0, one launch (start us, length us, event | category | flops | bytes accessed | tf_op | source)
XLA Modules:
  0.0 119.9 jit_solution(8420946546421344995)
XLA Ops:
  0.7 1.2 pad_maximum_fusion.1
  1.9 3.0 %collective-permute-start.3 = (bf16[128,2048]{1,0:T(8,128)(2,1)S(1)}, bf16[128,2048]{1,0:T(8,128)(2,1)S(1)}, u32[]{:S(2)}, u32[]{:S(2)}) collective-permute-start(bf16[128,2048]{1,0:T(8,128)(2,1)S(1)} %pad_maximum_fusion.1), channel_id=1, source_target_pairs={{0,8},{4,20},{8,0},{12,28},{16,24},{20,4},{24,16},{28,12},{1,9},{5... | collective-permute-start | bytes 1572872 | tf_op jit(solution)/shard_map/ppermute | solution.py:311
  4.9 2.6 %collective-permute-start.1 = (bf16[64,2048]{1,0:T(8,128)(2,1)}, bf16[64,2048]{1,0:T(8,128)(2,1)S(1)}, u32[]{:S(2)}, u32[]{:S(2)}) collective-permute-start(bf16[64,2048]{1,0:T(8,128)(2,1)} %x_ref.1), channel_id=1, source_target_pairs={{0,2},{1,3},{2,0},{3,1},{4,6},{5,7},{6,4},{7,5},{8,10},{9,11},{10,... | collective-permute-start | bytes 786440 | tf_op jit(solution)/shard_map/ppermute | solution.py:306
  7.5 1.6 %collective-permute-start = (bf16[64,2048]{1,0:T(8,128)(2,1)}, bf16[64,2048]{1,0:T(8,128)(2,1)S(1)}, u32[]{:S(2)}, u32[]{:S(2)}) collective-permute-start(bf16[64,2048]{1,0:T(8,128)(2,1)} %x_ref.1), channel_id=1, source_target_pairs={{0,1},{1,0},{2,3},{3,2},{4,5},{5,4},{6,7},{7,6},{8,9},{9,8},{10,11... | collective-permute-start | bytes 786440 | tf_op jit(solution)/shard_map/ppermute | solution.py:306
  9.0 3.0 %collective-permute-done.3 = bf16[128,2048]{1,0:T(8,128)(2,1)S(1)} collective-permute-done((bf16[128,2048]{1,0:T(8,128)(2,1)S(1)}, bf16[128,2048]{1,0:T(8,128)(2,1)S(1)}, u32[]{:S(2)}, u32[]{:S(2)}) %collective-permute-start.3) | collective-permute-done | bytes 524320 | tf_op jit(solution)/shard_map/ppermute | solution.py:311
  12.0 1.1 pad_maximum_fusion.refs_9_.refs_7_.refs_11_
  13.1 6.4 %collective-permute-done.1.refs_4_ = bf16[64,2048]{1,0:T(8,128)(2,1)S(1)} collective-permute-done((bf16[64,2048]{1,0:T(8,128)(2,1)}, bf16[64,2048]{1,0:T(8,128)(2,1)S(1)}, u32[]{:S(2)}, u32[]{:S(2)}) %collective-permute-start.1) | collective-permute-done | bytes 262176 | tf_op jit(solution)/shard_map/ppermute | solution.py:306
  19.5 0.2 collective-permute-done.refs_3_
  19.7 0.5 collective-permute-start.4
  20.1 1.4 %collective-permute-start.5 = (bf16[64,2048]{1,0:T(8,128)(2,1)S(1)}, bf16[64,2048]{1,0:T(8,128)(2,1)S(1)}, u32[]{:S(2)}, u32[]{:S(2)}) collective-permute-start(bf16[64,2048]{1,0:T(8,128)(2,1)S(1)} %copy-done.1), channel_id=1, source_target_pairs={{0,2},{1,3},{2,0},{3,1},{4,6},{5,7},{6,4},{7,5},{8,10},{9,11},{10,... | collective-permute-start | bytes 786440 | tf_op jit(solution)/shard_map/ppermute | solution.py:306
  21.5 2.5 %collective-permute-start.2 = (bf16[64,2048]{1,0:T(8,128)(2,1)S(1)}, bf16[64,2048]{1,0:T(8,128)(2,1)S(1)}, u32[]{:S(2)}, u32[]{:S(2)}) collective-permute-start(bf16[64,2048]{1,0:T(8,128)(2,1)S(1)} %collective-permute-done.1.refs_4_), channel_id=1, source_target_pairs={{0,1},{1,0},{2,3},{3,2},{4,5},{5,4},{6,7},{7,6},{8,9},{9,8},{10,11... | collective-permute-start | bytes 786440 | tf_op jit(solution)/shard_map/ppermute | solution.py:306
  24.0 11.5 %collective-permute-done.5.refs_4_ = bf16[64,2048]{1,0:T(8,128)(2,1)S(1)} collective-permute-done((bf16[64,2048]{1,0:T(8,128)(2,1)S(1)}, bf16[64,2048]{1,0:T(8,128)(2,1)S(1)}, u32[]{:S(2)}, u32[]{:S(2)}) %collective-permute-start.5) | collective-permute-done | bytes 262176 | tf_op jit(solution)/shard_map/ppermute | solution.py:306
  35.6 0.1 collective-permute-done.2.refs_5_
  35.7 0.5 collective-permute-start.7
  36.2 0.2 collective-permute-start.10
  36.4 1.8 %collective-permute-start.11 = (bf16[64,2048]{1,0:T(8,128)(2,1)S(1)}, bf16[64,2048]{1,0:T(8,128)(2,1)S(1)}, u32[]{:S(2)}, u32[]{:S(2)}) collective-permute-start(bf16[64,2048]{1,0:T(8,128)(2,1)S(1)} %collective-permute-done.5.refs_4_), channel_id=1, source_target_pairs={{0,1},{1,0},{2,3},{3,2},{4,5},{5,4},{6,7},{7,6},{8,9},{9,8},{10,11... | collective-permute-start | bytes 786440 | tf_op jit(solution)/shard_map/ppermute | solution.py:306
  38.2 0.1 copy.13.refs_0_
  38.3 0.1 copy.17.refs_5_
  38.4 1.5 %collective-permute-done.7.refs_12_.refs_10_.refs_14_ = bf16[256,2048]{1,0:T(8,128)(2,1)} collective-permute-done((bf16[256,2048]{1,0:T(8,128)(2,1)S(1)}, bf16[256,2048]{1,0:T(8,128)(2,1)}, u32[]{:S(2)}, u32[]{:S(2)}) %collective-permute-start.7) | collective-permute-done | bytes 1048608 | tf_op jit(solution)/shard_map/ppermute | solution.py:306
  40.0 10.5 %shard_map.120 = (bf16[16,256,128]{2,1,0:T(8,128)(2,1)}, bf16[16,256,128]{2,1,0:T(8,128)(2,1)}, f32[16,256,128]{2,1,0:T(8,128)}, f32[1,320]{1,0:T(1,128)S(1)}, b...) custom-call(s32[16,4]{1,0:T(8,128)S(1)} %copy.13.refs_0_, ...), custom_call_target="tpu_custom_call" | custom-call | flops 1073741824 | bytes 5244160 | tf_op jit(solution)/shard_map/pallas_call | solution.py:289
  50.5 0.7 copy-done.9
  51.1 0.1 copy-done.10
  51.2 4.2 %shard_map.121 = (bf16[256,2048]{1,0:T(8,128)(2,1)S(1)}, bf16[256,2048]{1,0:T(8,128)(2,1)S(1)}) custom-call(s32[16,4]{1,0:T(8,128)S(1)} %copy.13.refs_0_, s32[1]{0:T(128)} %bitcast.refs_1_, bf16[64,2048]{1,0:T(8,128)(2,1)} %upstream.1, bf16[64,2048]{1,0:T(8,128)(2,1)} %copy-done.9, bf16[64,2048]{1,0:T(8,128)(2,1)} %copy-done.8, bf16[64,2048]{1,0:T(8,128)(2,1)} %copy-done.10, ...), custom_call_target="tpu_custom_call" | custom-call | flops 536870912 | bytes 2097152 | tf_op jit(solution)/shard_map/pallas_call | solution.py:289
  55.4 0.2 collective-permute-start.20
  55.6 0.2 collective-permute-start.8
  55.9 1.8 %collective-permute-start.12 = (f32[1,320]{1,0:T(1,128)S(1)}, f32[1,320]{1,0:T(1,128)S(1)}, u32[]{:S(2)}, u32[]{:S(2)}) collective-permute-start(f32[1,320]{1,0:T(1,128)S(1)} %get-tuple-element.55), channel_id=1, source_target_pairs={{0,1},{1,0},{2,3},{3,2},{4,5},{5,4},{6,7},{7,6},{8,9},{9,8},{10,11... | collective-permute-start | bytes 3848 | tf_op jit(solution)/shard_map/ppermute | solution.py:306
  57.7 5.5 %shard_map.122 = (f32[16,256,128]{2,1,0:T(8,128)}, f32[1,2048]{1,0:T(1,128)S(1)}, f32[64,2048]{1,0:T(8,128)S(1)}) custom-call(s32[16,4]{1,0:T(8,128)S(1)} %copy.13.refs_0_, s32[1]{0:T(128)} %bitcast.refs_1_, bf16[64,2048]{1,0:T(8,128)(2,1)} %upstream.1, bf16[64,2048]{1,0:T(8,128)(2,1)} %copy-done.9, bf16[64,2048]{1,0:T(8,128)(2,1)} %copy-done.8, ...), custom_call_target="tpu_custom_call" | custom-call | flops 536870912 | bytes 2629632 | tf_op jit(solution)/shard_map/pallas_call | solution.py:289
  63.2 1.4 %collective-permute-done.12 = f32[1,320]{1,0:T(1,128)S(1)} collective-permute-done((f32[1,320]{1,0:T(1,128)S(1)}, f32[1,320]{1,0:T(1,128)S(1)}, u32[]{:S(2)}, u32[]{:S(2)}) %collective-permute-start.12) | collective-permute-done | bytes 1312 | tf_op jit(solution)/shard_map/ppermute | solution.py:306
  64.6 0.1 reshape.39
  64.7 0.1 reshape.40
  64.8 0.1 pad_maximum_fusion.3
  64.9 1.3 %collective-permute-start.13 = (f32[1,384]{1,0:T(1,128)S(1)}, f32[1,384]{1,0:T(1,128)S(1)}, u32[]{:S(2)}, u32[]{:S(2)}) collective-permute-start(f32[1,384]{1,0:T(1,128)S(1)} %pad_maximum_fusion.3), channel_id=1, source_target_pairs={{0,2},{1,3},{2,0},{3,1},{4,6},{5,7},{6,4},{7,5},{8,10},{9,11},{10,... | collective-permute-start | bytes 4616 | tf_op jit(solution)/shard_map/ppermute | solution.py:306
  66.2 1.7 %collective-permute-start.9 = (bf16[64,2048]{1,0:T(8,128)(2,1)}, bf16[64,2048]{1,0:T(8,128)(2,1)S(1)}, u32[]{:S(2)}, u32[]{:S(2)}) collective-permute-start(bf16[64,2048]{1,0:T(8,128)(2,1)} %get-tuple-element.51), channel_id=1, source_target_pairs={{0,1},{1,0},{2,3},{3,2},{4,5},{5,4},{6,7},{7,6},{8,9},{9,8},{10,11... | collective-permute-start | bytes 786440 | tf_op jit(solution)/shard_map/ppermute | solution.py:306
  67.9 1.0 fusion
  68.9 0.6 collective-permute-done.13
  69.5 0.1 pad_maximum_fusion.2.refs_2_
  69.6 1.3 %collective-permute-start.15 = (f32[1,512]{1,0:T(1,128)S(1)}, f32[1,512]{1,0:T(1,128)S(1)}, u32[]{:S(2)}, u32[]{:S(2)}) collective-permute-start(f32[1,512]{1,0:T(1,128)S(1)} %pad_maximum_fusion.2.refs_2_), channel_id=1, source_target_pairs={{0,4},{4,8},{8,12},{12,16},{16,20},{20,24},{24,28},{1,5},{5,9},{9,... | collective-permute-start | bytes 6152 | tf_op jit(solution)/shard_map/ppermute | solution.py:471
  70.9 1.3 %collective-permute-start.16 = (f32[1,512]{1,0:T(1,128)S(1)}, f32[1,512]{1,0:T(1,128)S(1)}, u32[]{:S(2)}, u32[]{:S(2)}) collective-permute-start(f32[1,512]{1,0:T(1,128)S(1)} %pad_maximum_fusion.2.refs_2_), channel_id=1, source_target_pairs={{4,0},{8,4},{12,8},{16,12},{20,16},{24,20},{28,24},{5,1},{9,5},{13... | collective-permute-start | bytes 6152 | tf_op jit(solution)/shard_map/ppermute | solution.py:472
  72.2 1.3 %collective-permute-start.14 = (bf16[64,2048]{1,0:T(8,128)(2,1)S(1)}, bf16[64,2048]{1,0:T(8,128)(2,1)S(1)}, u32[]{:S(2)}, u32[]{:S(2)}) collective-permute-start(bf16[64,2048]{1,0:T(8,128)(2,1)S(1)} %fusion), channel_id=1, source_target_pairs={{0,2},{1,3},{2,0},{3,1},{4,6},{5,7},{6,4},{7,5},{8,10},{9,11},{10,... | collective-permute-start | bytes 786440 | tf_op jit(solution)/shard_map/ppermute | solution.py:306
  73.4 1.6 %convert_add_fusion.1 = f32[256,2048]{1,0:T(8,128)S(1)} fusion(bf16[256,2048]{1,0:T(8,128)(2,1)} %collective-permute-done.20, bf16[256,2048]{1,0:T(8,128)(2,1)S(1)} %get-tuple-element.57), kind=kLoop, calls=%fused_computation.1 | loop fusion | flops 1572864 | bytes 4194304 | tf_op jit(solution)/shard_map/add | solution.py:477
  75.1 3.6 %collective-permute-start.21 = (bf16[128,2048]{1,0:T(8,128)(2,1)S(1)}, bf16[128,2048]{1,0:T(8,128)(2,1)S(1)}, u32[]{:S(2)}, u32[]{:S(2)}) collective-permute-start(bf16[128,2048]{1,0:T(8,128)(2,1)S(1)} %slice.83), channel_id=1, source_target_pairs={{0,8},{4,20},{8,0},{12,28},{16,24},{20,4},{24,16},{28,12},{1,9},{5... | collective-permute-start | bytes 1572872 | tf_op jit(solution)/shard_map/ppermute | solution.py:311
  78.7 8.1 %shard_map.123 = (f32[64,128]{1,0:T(8,128)S(1)}, f32[1,2048]{1,0:T(1,128)S(1)}, bf16[256,2048]{1,0:T(8,128)(2,1)S(1)}, bf16[256,2048]{1,0:T(8,128)(2,1)S(1)}, bf...) custom-call(s32[16,4]{1,0:T(8,128)S(1)} %copy.13.refs_0_, ...), custom_call_target="tpu_custom_call" | custom-call | flops 1073741824 | bytes 3186688 | tf_op jit(solution)/shard_map/pallas_call | solution.py:289
  86.9 0.6 collective-permute-done.14
  87.5 0.8 add_convert_fusion
  88.3 0.1 slice_add_fusion.1
  88.4 0.2 collective-permute-start.22
  88.6 0.4 collective-permute-start.23
  89.0 2.2 %collective-permute-done.23 = f32[1,2048]{1,0:T(1,128)S(1)} collective-permute-done((f32[1,2048]{1,0:T(1,128)S(1)}, f32[1,2048]{1,0:T(1,128)S(1)}, u32[]{:S(2)}, u32[]{:S(2)}) %collective-permute-start.23) | collective-permute-done | bytes 8224 | tf_op jit(solution)/shard_map/ppermute | solution.py:306
  91.2 0.3 convert_add_fusion
  91.6 2.3 %collective-permute-start.24 = (bf16[128,2048]{1,0:T(8,128)(2,1)S(1)}, bf16[128,2048]{1,0:T(8,128)(2,1)S(1)}, u32[]{:S(2)}, u32[]{:S(2)}) collective-permute-start(bf16[128,2048]{1,0:T(8,128)(2,1)S(1)} %slice.82), channel_id=1, source_target_pairs={{0,8},{4,20},{8,0},{12,28},{16,24},{20,4},{24,16},{28,12},{1,9},{5... | collective-permute-start | bytes 1572872 | tf_op jit(solution)/shard_map/ppermute | solution.py:311
  93.9 0.1 collective-permute-start.25
  94.0 1.0 collective-permute-start.17
  95.0 1.0 collective-permute-start.18
  96.0 1.2 %collective-permute-start.26 = (bf16[64,2048]{1,0:T(8,128)(2,1)S(1)}, bf16[64,2048]{1,0:T(8,128)(2,1)S(1)}, u32[]{:S(2)}, u32[]{:S(2)}) collective-permute-start(bf16[64,2048]{1,0:T(8,128)(2,1)S(1)} %slice.72), channel_id=1, source_target_pairs={{0,16},{4,12},{8,24},{12,4},{16,0},{20,28},{24,8},{28,20},{1,17},{... | collective-permute-start | bytes 786440 | tf_op jit(solution)/shard_map/ppermute | solution.py:311
  97.3 6.7 %collective-permute-done.25 = f32[1,2048]{1,0:T(1,128)S(1)} collective-permute-done((f32[1,2048]{1,0:T(1,128)S(1)}, f32[1,2048]{1,0:T(1,128)S(1)}, u32[]{:S(2)}, u32[]{:S(2)}) %collective-permute-start.25) | collective-permute-done | bytes 8224 | tf_op jit(solution)/shard_map/ppermute | solution.py:311
  104.0 0.1 slice_add_fusion
  104.1 1.3 %collective-permute-start.28 = (f32[1,2048]{1,0:T(1,128)S(1)}, f32[1,2048]{1,0:T(1,128)S(1)}, u32[]{:S(2)}, u32[]{:S(2)}) collective-permute-start(f32[1,2048]{1,0:T(1,128)S(1)} %add.67), channel_id=1, source_target_pairs={{0,16},{4,12},{8,24},{12,4},{16,0},{20,28},{24,8},{28,20},{1,17},{... | collective-permute-start | bytes 24584 | tf_op jit(solution)/shard_map/ppermute | solution.py:311
  105.5 0.1 collective-permute-start.19
  105.6 2.2 %collective-permute-done.28 = f32[1,2048]{1,0:T(1,128)S(1)} collective-permute-done((f32[1,2048]{1,0:T(1,128)S(1)}, f32[1,2048]{1,0:T(1,128)S(1)}, u32[]{:S(2)}, u32[]{:S(2)}) %collective-permute-start.28) | collective-permute-done | bytes 8224 | tf_op jit(solution)/shard_map/ppermute | solution.py:311
  107.9 0.9 multiply_add_fusion
  108.8 1.2 %collective-permute-start.27 = (bf16[64,2048]{1,0:T(8,128)(2,1)S(1)}, bf16[64,2048]{1,0:T(8,128)(2,1)S(1)}, u32[]{:S(2)}, u32[]{:S(2)}) collective-permute-start(bf16[64,2048]{1,0:T(8,128)(2,1)S(1)} %slice.84), channel_id=1, source_target_pairs={{0,16},{4,12},{8,24},{12,4},{16,0},{20,28},{24,8},{28,20},{1,17},{... | collective-permute-start | bytes 786440 | tf_op jit(solution)/shard_map/ppermute | solution.py:311
  110.1 7.9 %collective-permute-done.19.other = bf16[64,2048]{1,0:T(8,128)(2,1)S(1)} collective-permute-done((bf16[64,2048]{1,0:T(8,128)(2,1)S(1)}, bf16[64,2048]{1,0:T(8,128)(2,1)S(1)}, u32[]{:S(2)}, u32[]{:S(2)}) %collective-permute-start.19) | collective-permute-done | bytes 262176 | tf_op jit(solution)/shard_map/ppermute | solution.py:306
  117.9 1.1 shard_map.124
  119.0 0.9 slice_add_fusion.3
  (69 shorter events, 0.6 us)
Async XLA Ops:
  0.6 19.5 %copy-start.1 = (bf16[64,2048]{1,0:T(8,128)(2,1)S(1)}, bf16[64,2048]{1,0:T(8,128)(2,1)}, u32[]{:S(2)}) copy-start(bf16[64,2048]{1,0:T(8,128)(2,1)} %upstream.1) | copy-start | bytes 786436
  0.6 37.5 %copy-start.16 = (s32[16,4]{0,1:T(4,128)S(1)}, s32[16,4]{0,1:T(4,128)}, u32[]{:S(2)}) copy-start(s32[16,4]{0,1:T(4,128)} %param.13) | copy-start | bytes 772
  0.7 37.6 %copy-start.17 = (f32[128]{0:T(128)S(1)}, f32[128]{0:T(128)}, u32[]{:S(2)}) copy-start(f32[128]{0:T(128)} %param.15) | copy-start | bytes 1540
  0.7 39.3 %copy-start.3 = (f32[2048]{0:T(1024)S(1)}, f32[2048]{0:T(1024)}, u32[]{:S(2)}) copy-start(f32[2048]{0:T(1024)} %param.17) | copy-start | bytes 24580
  0.7 39.3 %copy-start.4 = (f32[2048]{0:T(1024)S(1)}, f32[2048]{0:T(1024)}, u32[]{:S(2)}) copy-start(f32[2048]{0:T(1024)} %param.10) | copy-start | bytes 24580
  0.7 39.3 %copy-start.5 = (s32[64]{0:T(128)S(1)}, s32[64]{0:T(128)}, u32[]{:S(2)}) copy-start(s32[64]{0:T(128)} %param.14) | copy-start | bytes 772
  1.9 10.2 %collective-permute-start.3 = (bf16[128,2048]{1,0:T(8,128)(2,1)S(1)}, bf16[128,2048]{1,0:T(8,128)(2,1)S(1)}, u32[]{:S(2)}, u32[]{:S(2)}) collective-permute-start(bf16[128,2048]{1,0:T(8,128)(2,1)S(1)} %pad_maximum_fusion.1), channel_id=1, source_target_pairs={{0,8},{4,20},{8,0},{12,28},{16,24},{20,4},{24,16},{28,12},{1,9},{5... | collective-permute-start | bytes 1572872 | tf_op jit(solution)/shard_map/ppermute | solution.py:311
  4.9 14.6 %collective-permute-start.1 = (bf16[64,2048]{1,0:T(8,128)(2,1)}, bf16[64,2048]{1,0:T(8,128)(2,1)S(1)}, u32[]{:S(2)}, u32[]{:S(2)}) collective-permute-start(bf16[64,2048]{1,0:T(8,128)(2,1)} %x_ref.1), channel_id=1, source_target_pairs={{0,2},{1,3},{2,0},{3,1},{4,6},{5,7},{6,4},{7,5},{8,10},{9,11},{10,... | collective-permute-start | bytes 786440 | tf_op jit(solution)/shard_map/ppermute | solution.py:306
  7.5 12.2 %collective-permute-start = (bf16[64,2048]{1,0:T(8,128)(2,1)}, bf16[64,2048]{1,0:T(8,128)(2,1)S(1)}, u32[]{:S(2)}, u32[]{:S(2)}) collective-permute-start(bf16[64,2048]{1,0:T(8,128)(2,1)} %x_ref.1), channel_id=1, source_target_pairs={{0,1},{1,0},{2,3},{3,2},{4,5},{5,4},{6,7},{7,6},{8,9},{9,8},{10,11... | collective-permute-start | bytes 786440 | tf_op jit(solution)/shard_map/ppermute | solution.py:306
  13.1 26.8 %copy-start.6 = (bf16[256,2048]{1,0:T(8,128)(2,1)}, bf16[256,2048]{1,0:T(8,128)(2,1)S(1)}, u32[]{:S(2)}) copy-start(bf16[256,2048]{1,0:T(8,128)(2,1)S(1)} %pad_maximum_fusion.refs_9_.refs_7_.refs_11_) | copy-start | bytes 3145732
  19.5 20.4 %copy-start.12 = (bf16[64,2048]{1,0:T(8,128)(2,1)}, bf16[64,2048]{1,0:T(8,128)(2,1)S(1)}, u32[]{:S(2)}) copy-start(bf16[64,2048]{1,0:T(8,128)(2,1)S(1)} %collective-permute-done.1.refs_4_) | copy-start | bytes 786436
  19.7 18.5 %copy-start.13 = (bf16[64,2048]{1,0:T(8,128)(2,1)}, bf16[64,2048]{1,0:T(8,128)(2,1)S(1)}, u32[]{:S(2)}) copy-start(bf16[64,2048]{1,0:T(8,128)(2,1)S(1)} %collective-permute-done.refs_3_) | copy-start | bytes 786436
  19.7 16.0 %collective-permute-start.4 = (bf16[256,2048]{1,0:T(8,128)(2,1)S(1)}, bf16[256,2048]{1,0:T(8,128)(2,1)S(1)}, u32[]{:S(2)}, u32[]{:S(2)}) collective-permute-start(bf16[256,2048]{1,0:T(8,128)(2,1)S(1)} %pad_maximum_fusion.refs_9_.refs_7_.refs_11_), channel_id=1, source_target_pairs={{0,16},{4,12},{8,24},{12,4},{16,0},{20,28},{24,8},{28,20},{1,17},{... | collective-permute-start | bytes 3145736 | tf_op jit(solution)/shard_map/ppermute | solution.py:311
  20.1 15.4 %collective-permute-start.5 = (bf16[64,2048]{1,0:T(8,128)(2,1)S(1)}, bf16[64,2048]{1,0:T(8,128)(2,1)S(1)}, u32[]{:S(2)}, u32[]{:S(2)}) collective-permute-start(bf16[64,2048]{1,0:T(8,128)(2,1)S(1)} %copy-done.1), channel_id=1, source_target_pairs={{0,2},{1,3},{2,0},{3,1},{4,6},{5,7},{6,4},{7,5},{8,10},{9,11},{10,... | collective-permute-start | bytes 786440 | tf_op jit(solution)/shard_map/ppermute | solution.py:306
  21.5 14.1 %collective-permute-start.2 = (bf16[64,2048]{1,0:T(8,128)(2,1)S(1)}, bf16[64,2048]{1,0:T(8,128)(2,1)S(1)}, u32[]{:S(2)}, u32[]{:S(2)}) collective-permute-start(bf16[64,2048]{1,0:T(8,128)(2,1)S(1)} %collective-permute-done.1.refs_4_), channel_id=1, source_target_pairs={{0,1},{1,0},{2,3},{3,2},{4,5},{5,4},{6,7},{7,6},{8,9},{9,8},{10,11... | collective-permute-start | bytes 786440 | tf_op jit(solution)/shard_map/ppermute | solution.py:306
  35.6 14.9 %copy-start.8 = (bf16[64,2048]{1,0:T(8,128)(2,1)}, bf16[64,2048]{1,0:T(8,128)(2,1)S(1)}, u32[]{:S(2)}) copy-start(bf16[64,2048]{1,0:T(8,128)(2,1)S(1)} %collective-permute-done.5.refs_4_) | copy-start | bytes 786436
  35.6 2.6 %copy-start.15 = (bf16[64,2048]{1,0:T(8,128)(2,1)}, bf16[64,2048]{1,0:T(8,128)(2,1)S(1)}, u32[]{:S(2)}) copy-start(bf16[64,2048]{1,0:T(8,128)(2,1)S(1)} %collective-permute-done.2.refs_5_) | copy-start | bytes 786436
  35.6 2.8 %collective-permute-start.6 = (bf16[256,2048]{1,0:T(8,128)(2,1)S(1)}, bf16[256,2048]{1,0:T(8,128)(2,1)}, u32[]{:S(2)}, u32[]{:S(2)}) collective-permute-start(bf16[256,2048]{1,0:T(8,128)(2,1)S(1)} %pad_maximum_fusion.refs_9_.refs_7_.refs_11_), channel_id=1, source_target_pairs={{0,4},{4,0},{8,12},{12,8},{16,20},{20,16},{24,28},{28,24},{1,5},{5... | collective-permute-start | bytes 3145736 | tf_op jit(solution)/shard_map/ppermute | solution.py:306
  35.7 4.3 %copy-start.7 = (bf16[256,2048]{1,0:T(8,128)(2,1)}, bf16[256,2048]{1,0:T(8,128)(2,1)S(1)}, u32[]{:S(2)}) copy-start(bf16[256,2048]{1,0:T(8,128)(2,1)S(1)} %collective-permute-done.4.refs_10_.refs_8_.refs_12_) | copy-start | bytes 3145732
  35.7 4.3 %collective-permute-start.7 = (bf16[256,2048]{1,0:T(8,128)(2,1)S(1)}, bf16[256,2048]{1,0:T(8,128)(2,1)}, u32[]{:S(2)}, u32[]{:S(2)}) collective-permute-start(bf16[256,2048]{1,0:T(8,128)(2,1)S(1)} %collective-permute-done.4.refs_10_.refs_8_.refs_12_), channel_id=1, source_target_pairs={{0,4},{4,0},{8,12},{12,8},{16,20},{20,16},{24,28},{28,24},{1,5},{5... | collective-permute-start | bytes 3145736 | tf_op jit(solution)/shard_map/ppermute | solution.py:306
  36.2 14.3 %collective-permute-start.10 = (bf16[64,2048]{1,0:T(8,128)(2,1)S(1)}, bf16[64,2048]{1,0:T(8,128)(2,1)S(1)}, u32[]{:S(2)}, u32[]{:S(2)}) collective-permute-start(bf16[64,2048]{1,0:T(8,128)(2,1)S(1)} %copy-done.1), channel_id=1, source_target_pairs={{0,1},{1,0},{2,3},{3,2},{4,5},{5,4},{6,7},{7,6},{8,9},{9,8},{10,11... | collective-permute-start | bytes 786440 | tf_op jit(solution)/shard_map/ppermute | solution.py:306
  36.4 14.1 %collective-permute-start.11 = (bf16[64,2048]{1,0:T(8,128)(2,1)S(1)}, bf16[64,2048]{1,0:T(8,128)(2,1)S(1)}, u32[]{:S(2)}, u32[]{:S(2)}) collective-permute-start(bf16[64,2048]{1,0:T(8,128)(2,1)S(1)} %collective-permute-done.5.refs_4_), channel_id=1, source_target_pairs={{0,1},{1,0},{2,3},{3,2},{4,5},{5,4},{6,7},{7,6},{8,9},{9,8},{10,11... | collective-permute-start | bytes 786440 | tf_op jit(solution)/shard_map/ppermute | solution.py:306
  50.4 0.7 copy-start.9
  50.5 0.8 copy-start.10
  55.4 18.0 %collective-permute-start.20 = (bf16[256,2048]{1,0:T(8,128)(2,1)S(1)}, bf16[256,2048]{1,0:T(8,128)(2,1)}, u32[]{:S(2)}, u32[]{:S(2)}) collective-permute-start(bf16[256,2048]{1,0:T(8,128)(2,1)S(1)} %get-tuple-element.73), channel_id=1, source_target_pairs={{0,4},{4,0},{8,12},{12,8},{16,20},{20,16},{24,28},{28,24},{1,5},{5... | collective-permute-start | bytes 3145736 | tf_op jit(solution)/shard_map/ppermute | solution.py:306
  55.6 9.2 %collective-permute-start.8 = (bf16[64,2048]{1,0:T(8,128)(2,1)}, bf16[64,2048]{1,0:T(8,128)(2,1)}, u32[]{:S(2)}, u32[]{:S(2)}) collective-permute-start(bf16[64,2048]{1,0:T(8,128)(2,1)} %get-tuple-element.50), channel_id=1, source_target_pairs={{0,1},{1,0},{2,3},{3,2},{4,5},{5,4},{6,7},{7,6},{8,9},{9,8},{10,11... | collective-permute-start | bytes 786440 | tf_op jit(solution)/shard_map/ppermute | solution.py:306
  55.9 12.0 %copy-start.14 = (bf16[64,2048]{1,0:T(8,128)(2,1)S(1)}, bf16[64,2048]{1,0:T(8,128)(2,1)}, u32[]{:S(2)}) copy-start(bf16[64,2048]{1,0:T(8,128)(2,1)} %get-tuple-element.49) | copy-start | bytes 786436
  55.9 8.7 %collective-permute-start.12 = (f32[1,320]{1,0:T(1,128)S(1)}, f32[1,320]{1,0:T(1,128)S(1)}, u32[]{:S(2)}, u32[]{:S(2)}) collective-permute-start(f32[1,320]{1,0:T(1,128)S(1)} %get-tuple-element.55), channel_id=1, source_target_pairs={{0,1},{1,0},{2,3},{3,2},{4,5},{5,4},{6,7},{7,6},{8,9},{9,8},{10,11... | collective-permute-start | bytes 3848 | tf_op jit(solution)/shard_map/ppermute | solution.py:306
  64.9 4.6 %collective-permute-start.13 = (f32[1,384]{1,0:T(1,128)S(1)}, f32[1,384]{1,0:T(1,128)S(1)}, u32[]{:S(2)}, u32[]{:S(2)}) collective-permute-start(f32[1,384]{1,0:T(1,128)S(1)} %pad_maximum_fusion.3), channel_id=1, source_target_pairs={{0,2},{1,3},{2,0},{3,1},{4,6},{5,7},{6,4},{7,5},{8,10},{9,11},{10,... | collective-permute-start | bytes 4616 | tf_op jit(solution)/shard_map/ppermute | solution.py:306
  66.2 20.7 %collective-permute-start.9 = (bf16[64,2048]{1,0:T(8,128)(2,1)}, bf16[64,2048]{1,0:T(8,128)(2,1)S(1)}, u32[]{:S(2)}, u32[]{:S(2)}) collective-permute-start(bf16[64,2048]{1,0:T(8,128)(2,1)} %get-tuple-element.51), channel_id=1, source_target_pairs={{0,1},{1,0},{2,3},{3,2},{4,5},{5,4},{6,7},{7,6},{8,9},{9,8},{10,11... | collective-permute-start | bytes 786440 | tf_op jit(solution)/shard_map/ppermute | solution.py:306
  69.6 9.1 %collective-permute-start.15 = (f32[1,512]{1,0:T(1,128)S(1)}, f32[1,512]{1,0:T(1,128)S(1)}, u32[]{:S(2)}, u32[]{:S(2)}) collective-permute-start(f32[1,512]{1,0:T(1,128)S(1)} %pad_maximum_fusion.2.refs_2_), channel_id=1, source_target_pairs={{0,4},{4,8},{8,12},{12,16},{16,20},{20,24},{24,28},{1,5},{5,9},{9,... | collective-permute-start | bytes 6152 | tf_op jit(solution)/shard_map/ppermute | solution.py:471
  70.9 7.8 %collective-permute-start.16 = (f32[1,512]{1,0:T(1,128)S(1)}, f32[1,512]{1,0:T(1,128)S(1)}, u32[]{:S(2)}, u32[]{:S(2)}) collective-permute-start(f32[1,512]{1,0:T(1,128)S(1)} %pad_maximum_fusion.2.refs_2_), channel_id=1, source_target_pairs={{4,0},{8,4},{12,8},{16,12},{20,16},{24,20},{28,24},{5,1},{9,5},{13... | collective-permute-start | bytes 6152 | tf_op jit(solution)/shard_map/ppermute | solution.py:472
  72.2 15.3 %collective-permute-start.14 = (bf16[64,2048]{1,0:T(8,128)(2,1)S(1)}, bf16[64,2048]{1,0:T(8,128)(2,1)S(1)}, u32[]{:S(2)}, u32[]{:S(2)}) collective-permute-start(bf16[64,2048]{1,0:T(8,128)(2,1)S(1)} %fusion), channel_id=1, source_target_pairs={{0,2},{1,3},{2,0},{3,1},{4,6},{5,7},{6,4},{7,5},{8,10},{9,11},{10,... | collective-permute-start | bytes 786440 | tf_op jit(solution)/shard_map/ppermute | solution.py:306
  75.1 13.3 %collective-permute-start.21 = (bf16[128,2048]{1,0:T(8,128)(2,1)S(1)}, bf16[128,2048]{1,0:T(8,128)(2,1)S(1)}, u32[]{:S(2)}, u32[]{:S(2)}) collective-permute-start(bf16[128,2048]{1,0:T(8,128)(2,1)S(1)} %slice.83), channel_id=1, source_target_pairs={{0,8},{4,20},{8,0},{12,28},{16,24},{20,4},{24,16},{28,12},{1,9},{5... | collective-permute-start | bytes 1572872 | tf_op jit(solution)/shard_map/ppermute | solution.py:311
  78.7 8.8 %copy-start = (bf16[64,2048]{1,0:T(8,128)(2,1)S(1)}, bf16[64,2048]{1,0:T(8,128)(2,1)}, u32[]{:S(2)}) copy-start(bf16[64,2048]{1,0:T(8,128)(2,1)} %x_ref.1) | copy-start | bytes 786436
  78.7 8.8 %copy-start.11 = (bf16[64,2048]{1,0:T(8,128)(2,1)S(1)}, bf16[64,2048]{1,0:T(8,128)(2,1)}, u32[]{:S(2)}) copy-start(bf16[64,2048]{1,0:T(8,128)(2,1)} %get-tuple-element.47) | copy-start | bytes 786436
  88.4 2.8 %collective-permute-start.22 = (bf16[256,2048]{1,0:T(8,128)(2,1)S(1)}, bf16[256,2048]{1,0:T(8,128)(2,1)S(1)}, u32[]{:S(2)}, u32[]{:S(2)}) collective-permute-start(bf16[256,2048]{1,0:T(8,128)(2,1)S(1)} %get-tuple-element.74), channel_id=1, source_target_pairs={{0,4},{4,0},{8,12},{12,8},{16,20},{20,16},{24,28},{28,24},{1,5},{5... | collective-permute-start | bytes 3145736 | tf_op jit(solution)/shard_map/ppermute | solution.py:306
  88.6 2.6 %collective-permute-start.23 = (f32[1,2048]{1,0:T(1,128)S(1)}, f32[1,2048]{1,0:T(1,128)S(1)}, u32[]{:S(2)}, u32[]{:S(2)}) collective-permute-start(f32[1,2048]{1,0:T(1,128)S(1)} %get-tuple-element.75), channel_id=1, source_target_pairs={{0,4},{4,0},{8,12},{12,8},{16,20},{20,16},{24,28},{28,24},{1,5},{5... | collective-permute-start | bytes 24584 | tf_op jit(solution)/shard_map/ppermute | solution.py:306
  91.6 12.3 %collective-permute-start.24 = (bf16[128,2048]{1,0:T(8,128)(2,1)S(1)}, bf16[128,2048]{1,0:T(8,128)(2,1)S(1)}, u32[]{:S(2)}, u32[]{:S(2)}) collective-permute-start(bf16[128,2048]{1,0:T(8,128)(2,1)S(1)} %slice.82), channel_id=1, source_target_pairs={{0,8},{4,20},{8,0},{12,28},{16,24},{20,4},{24,16},{28,12},{1,9},{5... | collective-permute-start | bytes 1572872 | tf_op jit(solution)/shard_map/ppermute | solution.py:311
  93.9 10.1 %collective-permute-start.25 = (f32[1,2048]{1,0:T(1,128)S(1)}, f32[1,2048]{1,0:T(1,128)S(1)}, u32[]{:S(2)}, u32[]{:S(2)}) collective-permute-start(f32[1,2048]{1,0:T(1,128)S(1)} %add.65), channel_id=1, source_target_pairs={{0,8},{4,20},{8,0},{12,28},{16,24},{20,4},{24,16},{28,12},{1,9},{5... | collective-permute-start | bytes 24584 | tf_op jit(solution)/shard_map/ppermute | solution.py:311
  94.0 11.5 %collective-permute-start.17 = (bf16[64,2048]{1,0:T(8,128)(2,1)S(1)}, bf16[64,2048]{1,0:T(8,128)(2,1)S(1)}, u32[]{:S(2)}, u32[]{:S(2)}) collective-permute-start(bf16[64,2048]{1,0:T(8,128)(2,1)S(1)} %get-tuple-element.68), channel_id=1, source_target_pairs={{0,1},{1,0},{2,3},{3,2},{4,5},{5,4},{6,7},{7,6},{8,9},{9,8},{10,11... | collective-permute-start | bytes 786440 | tf_op jit(solution)/shard_map/ppermute | solution.py:306
  95.0 15.0 %collective-permute-start.18 = (bf16[64,2048]{1,0:T(8,128)(2,1)S(1)}, bf16[64,2048]{1,0:T(8,128)(2,1)S(1)}, u32[]{:S(2)}, u32[]{:S(2)}) collective-permute-start(bf16[64,2048]{1,0:T(8,128)(2,1)S(1)} %get-tuple-element.69), channel_id=1, source_target_pairs={{0,1},{1,0},{2,3},{3,2},{4,5},{5,4},{6,7},{7,6},{8,9},{9,8},{10,11... | collective-permute-start | bytes 786440 | tf_op jit(solution)/shard_map/ppermute | solution.py:306
  96.0 11.8 %collective-permute-start.26 = (bf16[64,2048]{1,0:T(8,128)(2,1)S(1)}, bf16[64,2048]{1,0:T(8,128)(2,1)S(1)}, u32[]{:S(2)}, u32[]{:S(2)}) collective-permute-start(bf16[64,2048]{1,0:T(8,128)(2,1)S(1)} %slice.72), channel_id=1, source_target_pairs={{0,16},{4,12},{8,24},{12,4},{16,0},{20,28},{24,8},{28,20},{1,17},{... | collective-permute-start | bytes 786440 | tf_op jit(solution)/shard_map/ppermute | solution.py:311
  104.1 3.7 %collective-permute-start.28 = (f32[1,2048]{1,0:T(1,128)S(1)}, f32[1,2048]{1,0:T(1,128)S(1)}, u32[]{:S(2)}, u32[]{:S(2)}) collective-permute-start(f32[1,2048]{1,0:T(1,128)S(1)} %add.67), channel_id=1, source_target_pairs={{0,16},{4,12},{8,24},{12,4},{16,0},{20,28},{24,8},{28,20},{1,17},{... | collective-permute-start | bytes 24584 | tf_op jit(solution)/shard_map/ppermute | solution.py:311
  105.5 12.5 %copy-start.2 = (bf16[64,2048]{1,0:T(8,128)(2,1)S(1)}, bf16[64,2048]{1,0:T(8,128)(2,1)}, u32[]{:S(2)}) copy-start(bf16[64,2048]{1,0:T(8,128)(2,1)} %upstream.1) | copy-start | bytes 786436
  105.5 12.4 %collective-permute-start.19 = (bf16[64,2048]{1,0:T(8,128)(2,1)S(1)}, bf16[64,2048]{1,0:T(8,128)(2,1)S(1)}, u32[]{:S(2)}, u32[]{:S(2)}) collective-permute-start(bf16[64,2048]{1,0:T(8,128)(2,1)S(1)} %fusion.1), channel_id=1, source_target_pairs={{0,2},{1,3},{2,0},{3,1},{4,6},{5,7},{6,4},{7,5},{8,10},{9,11},{10,... | collective-permute-start | bytes 786440 | tf_op jit(solution)/shard_map/ppermute | solution.py:306
  108.8 10.2 %collective-permute-start.27 = (bf16[64,2048]{1,0:T(8,128)(2,1)S(1)}, bf16[64,2048]{1,0:T(8,128)(2,1)S(1)}, u32[]{:S(2)}, u32[]{:S(2)}) collective-permute-start(bf16[64,2048]{1,0:T(8,128)(2,1)S(1)} %slice.84), channel_id=1, source_target_pairs={{0,16},{4,12},{8,24},{12,4},{16,0},{20,28},{24,8},{28,20},{1,17},{... | collective-permute-start | bytes 786440 | tf_op jit(solution)/shard_map/ppermute | solution.py:311

commit v3 on v2

--- a/solution.py
+++ b/solution.py
@@ -65,7 +65,7 @@
     return copy.wait
 
 
-def loop(nj, unroll=4):
+def loop(nj, unroll=8):
     return pl.loop(0, nj, unroll=math.gcd(nj, unroll))
 
 
@@ -116,12 +116,14 @@
         a = (v * half).astype(BF16)
         act[j] = a
         dact[j] = half + 0.5 * v * (1.0 - t * t) * (GELU_A * (1.0 + 3.0 * GELU_B * v2))
+        pltpu.make_async_copy(act.at[j], act_out.at[j], sems.at[nf + 3]).start()
+        pltpu.make_async_copy(dact.at[j], dact_out.at[j], sems.at[nf + 4]).start()
         terms = dot(a, wout[:, column(j)], NT)
         for k, w in enumerate(which):
             acc[w] += terms[:, block(k)]
 
-    act_wait = load(act, act_out, sems.at[nf + 3])
-    dact_wait = load(dact, dact_out, sems.at[nf + 4])
+    act_wait = pltpu.make_async_copy(act, act_out, sems.at[nf + 3]).wait
+    dact_wait = pltpu.make_async_copy(dact, dact_out, sems.at[nf + 4]).wait
     spread(acc, [branch.at[d] for d in range(nf)], rows)
     waits = [load(branch.at[d], branch_out[d], sems.at[d]) for d in range(nf)]
     total = jnp.zeros((8, nf * rows), F32)
@@ -135,7 +137,7 @@
         wait()
 
 
-def store_grads(idx, place, orders, scale, left, right, keep, send):
+def store_grads(idx, place, orders, scale, pairs, keep, send):
     nj, kb = idx.shape
     count = 2 << len(orders[0])
     depth = kb * BLK // count
@@ -147,26 +149,29 @@
         pos = 0
         for bit in order:
             pos = 2 * pos + jnp.where((m & bit) != 0, 1, 0)
-        return pos * depth
+        return pos * len(pairs) * depth
 
     def slots(own):
         return [
-            pl.multiple_of(jnp.where(own == 0, slot(2 * q, orders[0]), slot(2 * q, orders[1])), depth)
+            jnp.where(own == 0, slot(2 * q, orders[0]), slot(2 * q, orders[1]))
             for q in range(count // 2)
         ]
 
     keep_at, send_at = slots(core), slots(1 - core)
 
-    @loop(nj)
+    @loop(nj, 4)
     def _(j):
-        for k in range(kb):
-            g = (dot(left[idx[j, k]], right[j], TN) * scale).astype(BF16)
-            for half in range(per // 2):
-                q = k * (per // 2) + half
-                even = g[2 * half * depth : (2 * half + 1) * depth]
-                odd = g[(2 * half + 1) * depth : (2 * half + 2) * depth]
-                keep[pl.ds(keep_at[q], depth), column(j)] = jnp.where(core == 0, even, odd)
-                send[pl.ds(send_at[q], depth), column(j)] = jnp.where(core == 0, odd, even)
+        for which, (left, right) in enumerate(pairs):
+            for k in range(kb):
+                g = (dot(left[idx[j, k]], right[j], TN) * scale).astype(BF16)
+                for half in range(per // 2):
+                    q = k * (per // 2) + half
+                    even = g[2 * half * depth : (2 * half + 1) * depth]
+                    odd = g[(2 * half + 1) * depth : (2 * half + 2) * depth]
+                    kept = pl.multiple_of(keep_at[q] + which * depth, depth)
+                    sent = pl.multiple_of(send_at[q] + which * depth, depth)
+                    keep[pl.ds(kept, depth), column(j)] = jnp.where(core == 0, even, odd)
+                    send[pl.ds(sent, depth), column(j)] = jnp.where(core == 0, odd, even)
 
 
 def upper_kernel(masks, nf, *refs):
@@ -174,11 +179,10 @@
     ups, refs = refs[2 : 2 + nf], refs[2 + nf:]
     readout, refs = refs[0], refs[1:]
     parts, refs = refs[: len(masks)], refs[len(masks):]
-    upper_out, turn, pattern, ubuf, up, wout, upper, flat, sems = refs
+    upper_out, turn, ubuf, up, wout, upper, sems = refs
     nj, kb = idx.shape
     fb = up.shape[0]
     rows = ubuf.shape[1]
-    depth = pattern.shape[0]
     waits = [load(ups[d], ubuf.at[d], sems.at[d]) for d in range(nf)]
     wout_wait = load_weight(place, parts, masks, 1, wout, sems.at[nf])
     for d in range(nf):
@@ -191,50 +195,29 @@
     def _(j):
         which = [idx[j, k] for k in range(kb)]
         picked = jnp.concatenate([up[w] for w in which], axis=1)
-        upper[j] = dot(picked, wout[:, column(j)])
+        turned = jnp.concatenate([three_terms(readout[:, column(w)]) for w in which], axis=1)
+        rows_of = jnp.concatenate([picked, turned, jnp.zeros_like(turned)], axis=0)
+        both = dot(rows_of, wout[:, column(j)])
+        upper[j] = both[: nf * rows]
         pltpu.make_async_copy(upper.at[j], upper_out.at[j], sems.at[nf + 1]).start()
-        turned = jnp.concatenate([three_terms(readout[:, column(w)]) for w in which], axis=1)
-        turn[:, column(j)] = jnp.sum(dot(turned, wout[:, column(j)]), axis=0, keepdims=True)
-
-    first = place[0] * depth
-    for j in range(nj):
-        row = readout[:, column(idx[j, first // BLK])]
-        flat[...] = jnp.transpose(jnp.broadcast_to(row, (BLK, BLK)))
-        pattern[:, block(j)] = flat[pl.ds(pl.multiple_of(first % BLK, depth), depth), :]
+        turn[:, column(j)] = jnp.sum(both[nf * rows : nf * rows + 8], axis=0, keepdims=True)
+
     pltpu.make_async_copy(upper, upper_out, sems.at[nf + 1]).wait()
 
 
-def fixed_grads_kernel(orders, scale, nf, *refs):
-    idx, place = refs[:2]
-    ups, refs = refs[2 : 2 + nf], refs[2 + nf:]
-    act_in, keep, send, ubuf, up, act, sems = refs
+def grads_kernel(orders, scale, nf, *refs):
+    idx, place, here, left, right, teacher, turn, readout, upper_in, dact_in, normed_in, act_in = refs[:12]
+    ups, refs = refs[12 : 12 + nf], refs[12 + nf:]
+    own_coeff, pre_grad, keep, send, upper, dact, normed, act, cot, ubuf, sems = refs
+    nj, kb = idx.shape
     rows = ubuf.shape[1]
-    waits = [load(ups[d], ubuf.at[d], sems.at[d]) for d in range(nf)]
-    act_wait = load(act_in, act, sems.at[nf])
-    for d in range(nf):
-        waits[d]()
-        for b in range(up.shape[0]):
-            up[b, d * rows : (d + 1) * rows, :] = ubuf[d, :, block(b)]
-    act_wait()
-    store_grads(idx, place, orders, scale, up, act, keep, send)
-
-
-def backward_kernel(masks, orders, scale, nf, *refs):
-    idx, place, here, left, right, teacher, turn, upper_in, dact_in, normed_in, act_in = refs[:11]
-    parts, refs = refs[11 : 11 + len(masks)], refs[11 + len(masks):]
-    own_coeff, along, keep, send = refs[:4]
-    outs, refs = refs[4 : 4 + nf], refs[4 + nf:]
-    upper, dact, normed, act, pre_grad, win, acc, sems = refs
-    nj, kb = idx.shape
-    rows = outs[0].shape[0]
     tokens = nf * rows
     nseg = teacher.shape[0]
+    up_waits = [load(ups[d], ubuf.at[d], sems.at[4 + d]) for d in range(nf)]
     upper_wait = load(upper_in, upper, sems.at[0])
     dact_wait = load(dact_in, dact, sems.at[1])
-    win_wait = load_weight(place, parts, masks, 0, win, sems.at[2])
-    normed_wait = load(normed_in, normed, sems.at[3])
-    act_wait = load(act_in, act, sems.at[4])
-    acc[...] = jnp.zeros_like(acc)
+    normed_wait = load(normed_in, normed, sems.at[2])
+    act_wait = load(act_in, act, sems.at[3])
     seg = (lax.broadcasted_iota(jnp.int32, (nseg, tokens), 0) + 1).astype(F32)
     sums = jnp.zeros((nseg, 1), F32)
     counts = jnp.zeros((nseg, 1), F32)
@@ -246,27 +229,42 @@
     coeff = 2.0 * LOSS_WEIGHT * jnp.sum(
         jnp.where(here[:, tokens:] == seg, misfit, 0.0), axis=0, keepdims=True
     )
-    terms_of = three_terms(coeff * scale)
     across = jnp.transpose(jnp.broadcast_to(coeff, (BLK, tokens)))
     own_coeff[...] = across[:rows]
+    for d in range(nf):
+        up_waits[d]()
+        part = across[d * rows : (d + 1) * rows]
+        for b in range(cot.shape[0]):
+            c = ubuf[d, :, block(b)].astype(F32) + part * readout[:, block(b)]
+            cot[b, d * rows : (d + 1) * rows, :] = c.astype(BF16)
     upper_wait()
     dact_wait()
-    win_wait()
 
     @loop(nj)
     def _(j):
-        p = ((upper[j] + across * turn[:, column(j)]) * dact[j]).astype(BF16)
-        pre_grad[j] = p
-        terms = dot(p, win[:, column(j)], NT)
+        pre_grad[j] = ((upper[j] + across * turn[:, column(j)]) * dact[j]).astype(BF16)
+
+    normed_wait()
+    act_wait()
+    store_grads(idx, place, orders, scale, ((cot, act), (normed, pre_grad)), keep, send)
+
+
+def back_kernel(masks, nf, *refs):
+    idx, place, pre_grad = refs[:3]
+    parts, refs = refs[3 : 3 + len(masks)], refs[3 + len(masks):]
+    outs, (win, acc, sem) = refs[:nf], refs[nf:]
+    nj, kb = idx.shape
+    win_wait = load_weight(place, parts, masks, 0, win, sem)
+    acc[...] = jnp.zeros_like(acc)
+    win_wait()
+
+    @loop(nj)
+    def _(j):
+        terms = dot(pre_grad[j], win[:, column(j)], NT)
         for k in range(kb):
             acc[idx[j, k]] += terms[:, block(k)]
 
-    spread(acc, outs, rows)
-    normed_wait()
-    store_grads(idx, place, orders, scale, normed, pre_grad, keep, send)
-    act_wait()
-    for j in range(nj):
-        along[:, block(j)] = jnp.sum(dot(terms_of, act[j]), axis=0, keepdims=True)
+    spread(acc, outs, outs[0].shape[0])
 
 
 def finish_kernel(x_ref, gain, upstream, readout, own_coeff, own, other, out):
@@ -328,6 +326,23 @@
     return held + other, masks + [[(b ^ 1, a ^ 1) for a, b in ms] for ms in masks]
 
 
+class Halving:
+    def __init__(self, terms):
+        self.terms = terms
+
+    def total(self):
+        return functools.reduce(lambda a, b: a + b, [t.astype(F32) for t in self.terms])
+
+    def away(self):
+        half = self.terms[0].shape[0] // 2
+        sent = Halving([t[half:] for t in self.terms]).total().astype(BF16)
+        self.terms = [t[:half] for t in self.terms]
+        return sent
+
+    def add(self, term):
+        self.terms.append(term)
+
+
 def gather_feat(own, bits, far=None):
     held = {0: own}
     for bit in bits[::-1]:
@@ -342,22 +357,20 @@
 
 
 def scatter_near(parts):
-    held = {}
-    for d in range(len(parts) - 2, 0, -2):
-        held[d] = parts[d].astype(F32) + swap(parts[d + 1], "feat", 1).astype(F32)
-    return held
+    return {d: swap(parts[d + 1], "feat", 1) for d in range(len(parts) - 2, 0, -2)}
 
 
 def scatter_far(parts, held, bits, tie):
     firsts = [held[d] for d in sorted(held)]
-    held = dict(held)
-    held[0] = parts[0].astype(F32) + swap(after(parts[1], *firsts), "feat", 1).astype(F32)
+    held = {d: parts[d].astype(F32) + got.astype(F32) for d, got in held.items()}
+    beside = swap(after(parts[1], *firsts), "feat", 1)
+    held[0] = parts[0].astype(F32) + beside.astype(F32)
     for bit in bits[1:]:
         stay = [d for d in held if not d & bit]
         for d in sorted(stay, reverse=True):
             got = swap(after(held[d | bit].astype(BF16), tie), "feat", bit)
             if d == 0 and bit == bits[-1]:
-                return held[0], got
+                return held[0], got, beside
             held[d] = held[d] + got.astype(F32)
         held = {d: held[d] for d in stay}
 
@@ -397,7 +410,6 @@
     weight = pltpu.VMEM((kb * BLK, hidden), BF16)
     summed = pltpu.VMEM((fb, tokens, BLK), F32)
     piece = sds((rows, width), BF16)
-    half_grad = sds((kb * BLK // 2, hidden), BF16)
 
     outs = call(
         functools.partial(forward_kernel, masks, nf),
@@ -428,12 +440,11 @@
     normed, act, dact, here = outs[:4]
     branch = outs[4:]
 
-    upper, turn, pattern = call(
+    upper, turn = call(
         functools.partial(upper_kernel, masks, nf),
         [
             (HBM, sds((nj, tokens, BLK), F32)),
             (VM, sds((1, hidden), F32)),
-            (VM, sds((depth, hidden), F32)),
         ],
         scalars + [(HBM, u) for u in ups] + [(VM, readout_row)] + parts,
         [
@@ -441,89 +452,68 @@
             by_feature,
             weight,
             by_hidden_wide,
-            pltpu.VMEM((BLK, BLK), F32),
             pltpu.SemaphoreType.DMA((nf + 2,)),
         ],
         flops,
     )
-    keep_out, send_out = call(
-        functools.partial(fixed_grads_kernel, orders, grad_scale, nf),
-        [(VM, half_grad), (VM, half_grad)],
-        scalars + [(HBM, u) for u in ups] + [(HBM, act)],
-        [
-            pltpu.VMEM((nf, rows, width), BF16),
-            by_feature,
-            by_hidden,
-            pltpu.SemaphoreType.DMA((nf + 1,)),
-        ],
-        flops,
-    )
-    branch_near = scatter_near(branch)
-    firsts = [branch_near[d] for d in sorted(branch_near)]
     for step, bit in enumerate(feat_bits):
-        ties = ups[1:] if step == 0 else [keep_out, turn] + firsts
-        there = swap(after(here, *ties), "feat", bit)
+        there = swap(after(here, *ups[1:]) if step == 0 else here, "feat", bit)
+        if step == 0:
+            branch_near = scatter_near([after(b, there) for b in branch])
+        if bit == feat_bits[-1]:
+            there = after(there, turn)
         turned = jnp.flip(there[:, :tokens].reshape(nf // (2 * bit), 2, bit * rows), axis=1)
         here = jnp.concatenate(
             [here[:, :tokens] + turned.reshape(1, tokens), here[:, tokens:], there[:, tokens:]],
             axis=1,
         )
-    left = lax.ppermute(here, "tok", [(i, i + 1) for i in range(nt - 1)])
-    right = lax.ppermute(here, "tok", [(i + 1, i) for i in range(nt - 1)])
-
-    own, got = scatter_far(branch, branch_near, feat_bits, here)
-    branch_sum = own + got.astype(F32)
-    layer_out = (inputs.astype(F32) + branch_sum).astype(BF16)
-    total_out = keep_out.astype(F32) + swap(send_out, "tok", 1).astype(F32)
-    even, odd = bits[0], bits[-1]
-    half = total_out.shape[0] // 2
-    total_out = total_out[:half] + swap_tok(total_out[half:].astype(BF16), even, odd).astype(F32)
-
-    outs = call(
-        functools.partial(backward_kernel, masks, orders, grad_scale, nf),
+    left = swap(here, "tok", 1)
+    odd = range(1, nt - 1, 2)
+    right = lax.ppermute(here, "tok", [(i, i + 1) for i in odd] + [(i + 1, i) for i in odd])
+
+    branch_near = {d: after(got, turn) for d, got in branch_near.items()}
+    half_grads = sds((kb * BLK, hidden), BF16)
+    own_coeff, pre_grad, keep, send = call(
+        functools.partial(grads_kernel, orders, grad_scale, nf),
         [
             (VM, sds((rows, BLK), F32)),
-            (VM, sds((1, hidden), F32)),
-            (VM, half_grad),
-            (VM, half_grad),
-        ]
-        + [(VM, piece)] * nf,
+            (VM, sds((nj, tokens, BLK), BF16)),
+            (VM, half_grads),
+            (VM, half_grads),
+        ],
         scalars
         + [(VM, here), (VM, left), (VM, right), (VM, teacher_scores.reshape(-1, 1)), (VM, turn)]
-        + [(HBM, upper), (HBM, dact), (HBM, normed), (HBM, act)]
-        + parts,
+        + [(VM, readout_row)]
+        + [(HBM, a) for a in (upper, dact, normed, act)]
+        + [(HBM, u) for u in ups],
         [
             by_hidden_wide,
             by_hidden_wide,
             by_feature,
             by_hidden,
-            by_hidden,
-            weight,
-            summed,
-            pltpu.SemaphoreType.DMA((5,)),
+            by_feature,
+            pltpu.VMEM((nf, rows, width), BF16),
+            pltpu.SemaphoreType.DMA((nf + 4,)),
         ],
         2 * flops,
     )
-    own_coeff, along, keep_in, send_in = outs[:4]
-    back = outs[4:]
-    back_near = scatter_near(back)
-    own, got = scatter_far(back, back_near, feat_bits, layer_out)
-
-    send_in = after(send_in, layer_out, total_out)
-    total = keep_in.astype(F32) + swap(send_in, "tok", 1).astype(F32)
-    along = along + swap(along, "tok", 1)
-    rest = list(zip(bits, bits[::-1]))
-    for step, (even, odd) in enumerate(rest):
-        half = total.shape[0] // 2
-        away = after(total[half:].astype(BF16), along, total_out)
-        along = along + swap_tok(after(along, total), even, odd)
-        if step + 1 < len(rest):
-            cut = total_out.shape[0] // 2
-            got_out = swap_tok(after(total_out[cut:], total).astype(BF16), *rest[step + 1])
-            total_out = total_out[:cut] + got_out.astype(F32)
-        total = total[:half] + swap_tok(away, even, odd).astype(F32)
-    grad_in = total
-    grad_out = total_out + pattern * along
+    back = call(
+        functools.partial(back_kernel, masks, nf),
+        [(VM, piece)] * nf,
+        scalars + [(VM, pre_grad)] + parts,
+        [weight, summed, pltpu.SemaphoreType.DMA],
+        flops,
+    )
+    branch_own, branch_got, beside = scatter_far(branch, branch_near, feat_bits, here)
+    branch_got = after(branch_got, own_coeff)
+    layer_out = (inputs.astype(F32) + (branch_own + branch_got.astype(F32))).astype(BF16)
+    send = after(send, branch_got, beside)
+    own, got, _ = scatter_far(back, scatter_near(back), feat_bits, branch_got)
+    sums = Halving([keep, after(swap(send, "tok", 1), back[1])])
+    for pair in zip(bits, bits[::-1]):
+        sums.add(swap_tok(sums.away(), *pair))
+    grads = sums.total()
+    grad_out, grad_in = grads[:depth], grads[depth:]
     (input_grad,) = call(
         finish_kernel,
         [(VM, piece)],

time: 120 us -> 109 us (0.908)
  starting transfers between devices: 35.6 us -> 29.8 us
  other arithmetic: 8.36 us -> 4.37 us
  Pallas kernels: 29.3 us -> 26.5 us
  waiting for transfers between devices: 44.2 us -> 46 us
    ppermute x19 -> x18, waiting for transfers between devices: 32.3 us -> 41.8 us  [swap(): return lax.ppermute(value, axis, [(i, i ^ mask) for i in range(n)])]
    ppermute x8 -> x4, waiting for transfers between devices: 11.9 us -> 4.14 us  [swap_tok(): lax.ppermute(value, 'tok', [(i, i ^ (odd if i & 1 else even)) for i in ra...]
    ppermute x8 -> x4, starting transfers between devices: 13.2 us -> 7.24 us  [swap_tok(): lax.ppermute(value, 'tok', [(i, i ^ (odd if i & 1 else even)) for i in ra...]
    add x10 -> x2, other arithmetic: 4.01 us -> 0.37 us  [the longest x1 0.32 us: total(): a + b]
    pallas_call x5, Pallas kernels: 29.3 us -> 26.5 us  [call(): pl.pallas_call(body, out_shape=[pltpu.HBM(o.shape, o.dtype) if m is HBM e...]
    ppermute x19 -> x18, starting transfers between devices: 19.7 us -> 21.9 us  [swap(): return lax.ppermute(value, axis, [(i, i ^ mask) for i in range(n)])]
    ppermute x2 -> x1, starting transfers between devices: 2.57 us -> 0.65 us  [on_device(): lax.ppermute(here, 'tok', [(i, i + 1) for i in odd] + [(i + 1, i) for i i...]
  transfers between devices with their start and end apart: 29 -> 23, of which waited for: 13 -> 14; matrix products, arithmetic and copies ran while one was open for 5% -> 2% of each run, Pallas kernels for 21% -> 24%
where the time goes in v3:
time: 109 us
  waiting for transfers between devices  46 us (42%)
  starting transfers between devices  29.8 us (27%)
  Pallas kernels  26.5 us (24%)
  other arithmetic  4.37 us (4%)
  local copies, waits for them, and re-layouts  1.77 us (2%)
    ppermute x18, waiting for transfers between devices, swap(): return lax.ppermute(value, axis, [(i, i ^ mask) for i in range(n)])  41.8 us
    pallas_call x5, Pallas kernels, call(): pl.pallas_call(body, out_shape=[pltpu.HBM(o.shape, o.dtype) if m is HBM e...  26.5 us
    ppermute x18, starting transfers between devices, swap(): return lax.ppermute(value, axis, [(i, i ^ mask) for i in range(n)])  21.9 us
    ppermute x4, starting transfers between devices, swap_tok(): lax.ppermute(value, 'tok', [(i, i ^ (odd if i & 1 else even)) for i in ra...  7.24 us
    ppermute x4, waiting for transfers between devices, swap_tok(): lax.ppermute(value, 'tok', [(i, i ^ (odd if i & 1 else even)) for i in ra...  4.14 us
    concatenate x2, other arithmetic, gather_tok(): whole = jnp.concatenate(held, axis=0)  2.23 us
  transfers between devices with their start and end apart: 23, of which 14 were waited for; matrix products, arithmetic and copies ran while one was open for 2% of the time, Pallas kernels for 24%

profile of v3, /device:TPU:0, one launch (start us, length us, event | category | flops | bytes accessed | tf_op | source)
XLA Modules:
  0.0 109.2 jit_solution(9524951474908358991)
XLA Ops:
  0.6 0.0 copy-start.1
  0.7 1.1 %pad_maximum_fusion.1 = bf16[128,2048]{1,0:T(8,128)(2,1)S(1)} fusion(bf16[64,2048]{1,0:T(8,128)(2,1)} %param.12, bf16[64,2048]{1,0:T(8,128)(2,1)} %param.11), kind=kLoop, calls=%fused_computation.4 | loop fusion | flops 1048576 | bytes 1048576 | tf_op jit(solution)/shard_map/concatenate | solution.py:319
  1.8 3.0 %collective-permute-start.3 = (bf16[128,2048]{1,0:T(8,128)(2,1)S(1)}, bf16[128,2048]{1,0:T(8,128)(2,1)S(1)}, u32[]{:S(2)}, u32[]{:S(2)}) collective-permute-start(bf16[128,2048]{1,0:T(8,128)(2,1)S(1)} %pad_maximum_fusion.1), channel_id=1, source_target_pairs={{0,8},{4,20},{8,0},{12,28},{16,24},{20,4},{24,16},{28,12},{1,9},{5... | collective-permute-start | bytes 1572872 | tf_op jit(solution)/shard_map/ppermute | solution.py:309
  4.8 2.6 %collective-permute-start.1 = (bf16[64,2048]{1,0:T(8,128)(2,1)}, bf16[64,2048]{1,0:T(8,128)(2,1)S(1)}, u32[]{:S(2)}, u32[]{:S(2)}) collective-permute-start(bf16[64,2048]{1,0:T(8,128)(2,1)} %x_ref.1), channel_id=1, source_target_pairs={{0,2},{1,3},{2,0},{3,1},{4,6},{5,7},{6,4},{7,5},{8,10},{9,11},{10,... | collective-permute-start | bytes 786440 | tf_op jit(solution)/shard_map/ppermute | solution.py:304
  7.4 1.6 %collective-permute-start = (bf16[64,2048]{1,0:T(8,128)(2,1)}, bf16[64,2048]{1,0:T(8,128)(2,1)S(1)}, u32[]{:S(2)}, u32[]{:S(2)}) collective-permute-start(bf16[64,2048]{1,0:T(8,128)(2,1)} %x_ref.1), channel_id=1, source_target_pairs={{0,1},{1,0},{2,3},{3,2},{4,5},{5,4},{6,7},{7,6},{8,9},{9,8},{10,11... | collective-permute-start | bytes 786440 | tf_op jit(solution)/shard_map/ppermute | solution.py:304
  9.0 3.0 %collective-permute-done.3 = bf16[128,2048]{1,0:T(8,128)(2,1)S(1)} collective-permute-done((bf16[128,2048]{1,0:T(8,128)(2,1)S(1)}, bf16[128,2048]{1,0:T(8,128)(2,1)S(1)}, u32[]{:S(2)}, u32[]{:S(2)}) %collective-permute-start.3) | collective-permute-done | bytes 524320 | tf_op jit(solution)/shard_map/ppermute | solution.py:309
  12.0 1.1 %pad_maximum_fusion.refs_9_.refs_7_.refs_3_ = bf16[256,2048]{1,0:T(8,128)(2,1)S(1)} fusion(bf16[128,2048]{1,0:T(8,128)(2,1)S(1)} %collective-permute-done.3, bf16[64,2048]{1,0:T(8,128)(2,1)} %param.12, bf16[64,2048]{1,0:T(8,128)(2,1)} %param.11), kind=kLoop, calls=%fused_computation.1 | loop fusion | flops 3145728 | bytes 2097152 | tf_op jit(solution)/shard_map/concatenate | solution.py:319
  13.1 6.3 %collective-permute-done.1.refs_4_ = bf16[64,2048]{1,0:T(8,128)(2,1)S(1)} collective-permute-done((bf16[64,2048]{1,0:T(8,128)(2,1)}, bf16[64,2048]{1,0:T(8,128)(2,1)S(1)}, u32[]{:S(2)}, u32[]{:S(2)}) %collective-permute-start.1) | collective-permute-done | bytes 262176 | tf_op jit(solution)/shard_map/ppermute | solution.py:304
  19.4 0.2 collective-permute-done.refs_3_
  19.6 0.5 collective-permute-start.4
  20.1 1.5 %collective-permute-start.2 = (bf16[64,2048]{1,0:T(8,128)(2,1)S(1)}, bf16[64,2048]{1,0:T(8,128)(2,1)S(1)}, u32[]{:S(2)}, u32[]{:S(2)}) collective-permute-start(bf16[64,2048]{1,0:T(8,128)(2,1)S(1)} %collective-permute-done.1.refs_4_), channel_id=1, source_target_pairs={{0,1},{1,0},{2,3},{3,2},{4,5},{5,4},{6,7},{7,6},{8,9},{9,8},{10,11... | collective-permute-start | bytes 786440 | tf_op jit(solution)/shard_map/ppermute | solution.py:304
  21.6 2.4 %collective-permute-start.5 = (bf16[64,2048]{1,0:T(8,128)(2,1)S(1)}, bf16[64,2048]{1,0:T(8,128)(2,1)}, u32[]{:S(2)}, u32[]{:S(2)}) collective-permute-start(bf16[64,2048]{1,0:T(8,128)(2,1)S(1)} %copy-done.1), channel_id=1, source_target_pairs={{0,2},{1,3},{2,0},{3,1},{4,6},{5,7},{6,4},{7,5},{8,10},{9,11},{10,... | collective-permute-start | bytes 786440 | tf_op jit(solution)/shard_map/ppermute | solution.py:304
  24.0 10.2 %collective-permute-done.2.refs_5_ = bf16[64,2048]{1,0:T(8,128)(2,1)S(1)} collective-permute-done((bf16[64,2048]{1,0:T(8,128)(2,1)S(1)}, bf16[64,2048]{1,0:T(8,128)(2,1)S(1)}, u32[]{:S(2)}, u32[]{:S(2)}) %collective-permute-start.2) | collective-permute-done | bytes 262176 | tf_op jit(solution)/shard_map/ppermute | solution.py:304
  34.2 2.5 %collective-permute-done.5.refs_4_.refs_14_ = bf16[64,2048]{1,0:T(8,128)(2,1)} collective-permute-done((bf16[64,2048]{1,0:T(8,128)(2,1)S(1)}, bf16[64,2048]{1,0:T(8,128)(2,1)}, u32[]{:S(2)}, u32[]{:S(2)}) %collective-permute-start.5) | collective-permute-done | bytes 262176 | tf_op jit(solution)/shard_map/ppermute | solution.py:304
  36.7 0.0 collective-permute-start.6
  36.7 0.0 collective-permute-done.4.refs_10_.refs_8_.refs_4_
  36.7 0.5 collective-permute-start.7
  37.2 0.1 collective-permute-start.8
  37.4 1.9 %collective-permute-start.9 = (bf16[64,2048]{1,0:T(8,128)(2,1)}, bf16[64,2048]{1,0:T(8,128)(2,1)}, u32[]{:S(2)}, u32[]{:S(2)}) collective-permute-start(bf16[64,2048]{1,0:T(8,128)(2,1)} %collective-permute-done.5.refs_4_.refs_14_), channel_id=1, source_target_pairs={{0,1},{1,0},{2,3},{3,2},{4,5},{5,4},{6,7},{7,6},{8,9},{9,8},{10,11... | collective-permute-start | bytes 786440 | tf_op jit(solution)/shard_map/ppermute | solution.py:304
  39.2 0.1 copy.13.refs_0_
  39.3 0.8 collective-permute-done.6.refs_11_.refs_9_.refs_5_
  40.1 0.9 collective-permute-done.7.refs_12_.refs_10_.refs_6_
  41.0 0.2 copy-done.8
  41.2 9.4 %shard_map.120 = (bf16[16,256,128]{2,1,0:T(8,128)(2,1)}, bf16[16,256,128]{2,1,0:T(8,128)(2,1)}, f32[16,256,128]{2,1,0:T(8,128)}, f32[1,320]{1,0:T(1,128)S(1)}, b...) custom-call(s32[16,4]{1,0:T(8,128)S(1)} %copy.13.refs_0_, ...), custom_call_target="tpu_custom_call" | custom-call | flops 1073741824 | bytes 5244160 | tf_op jit(solution)/shard_map/pallas_call | solution.py:287
  50.6 0.6 collective-permute-done.9.refs_5_.refs_15_
  51.2 0.3 collective-permute-start.10
  51.5 3.3 %collective-permute-done.10 = f32[1,320]{1,0:T(1,128)S(1)} collective-permute-done((f32[1,320]{1,0:T(1,128)S(1)}, f32[1,320]{1,0:T(1,128)S(1)}, u32[]{:S(2)}, u32[]{:S(2)}) %collective-permute-start.10) | collective-permute-done | bytes 1312 | tf_op jit(solution)/shard_map/ppermute | solution.py:304
  54.8 0.1 reshape.39
  54.9 0.1 reshape.40
  55.0 0.3 collective-permute-start.11
  55.3 0.1 pad_maximum_fusion.3
  55.4 2.7 %collective-permute-start.13 = (f32[1,384]{1,0:T(1,128)S(1)}, f32[1,384]{1,0:T(1,128)S(1)}, u32[]{:S(2)}, u32[]{:S(2)}) collective-permute-start(f32[1,384]{1,0:T(1,128)S(1)} %pad_maximum_fusion.3), channel_id=1, source_target_pairs={{0,2},{1,3},{2,0},{3,1},{4,6},{5,7},{6,4},{7,5},{8,10},{9,11},{10,... | collective-permute-start | bytes 4616 | tf_op jit(solution)/shard_map/ppermute | solution.py:304
  58.1 4.8 %shard_map.121 = (f32[16,256,128]{2,1,0:T(8,128)}, f32[1,2048]{1,0:T(1,128)S(1)}) custom-call(s32[16,4]{1,0:T(8,128)S(1)} %copy.13.refs_0_, s32[1]{0:T(128)} %bitcast.refs_1_, bf16[64,2048]{1,0:T(8,128)(2,1)} %upstream.1, bf16[64,2048]{1,0:T(8,128)(2,1)} %collective-permute-done.8.refs_3_.refs_13_, bf16[64,2048]{1,0:T(8,128)(2,1)} %collective-permute-done.5.refs_4_.refs_14_, ...), custom_call_target="tpu_custom_call" | custom-call | flops 536870912 | bytes 2105344 | tf_op jit(solution)/shard_map/pallas_call | solution.py:287
  62.9 0.1 pad_maximum_fusion.2.refs_2_
  63.0 0.1 add_convert_fusion.4
  63.1 0.3 collective-permute-start.14
  63.4 1.7 %collective-permute-start.12 = (bf16[64,2048]{1,0:T(8,128)(2,1)S(1)}, bf16[64,2048]{1,0:T(8,128)(2,1)S(1)}, u32[]{:S(2)}, u32[]{:S(2)}) collective-permute-start(bf16[64,2048]{1,0:T(8,128)(2,1)S(1)} %copy-done.16), channel_id=1, source_target_pairs={{0,1},{1,0},{2,3},{3,2},{4,5},{5,4},{6,7},{7,6},{8,9},{9,8},{10,11... | collective-permute-start | bytes 786440 | tf_op jit(solution)/shard_map/ppermute | solution.py:304
  65.2 0.6 collective-permute-start.16
  65.8 1.9 %collective-permute-start.15 = (f32[1,512]{1,0:T(1,128)S(1)}, f32[1,512]{1,0:T(1,128)S(1)}, u32[]{:S(2)}, u32[]{:S(2)}) collective-permute-start(f32[1,512]{1,0:T(1,128)S(1)} %pad_maximum_fusion.2.refs_2_), channel_id=1, source_target_pairs={{0,4},{4,0},{8,12},{12,8},{16,20},{20,16},{24,28},{28,24},{1,5},{5... | collective-permute-start | bytes 6152 | tf_op jit(solution)/shard_map/ppermute | solution.py:304
  67.7 0.1 copy.16.refs_5_
  67.9 0.7 collective-permute-done.15.refs_3_
  68.6 7.1 %shard_map.122 = (f32[64,128]{1,0:T(8,128)S(1)}, bf16[16,256,128]{2,1,0:T(8,128)(2,1)S(1)}, bf16[512,2048]{1,0:T(8,128)(2,1)S(1)}, bf16[512,2048]{1,0:T(8,128)(2,1)S(1)}) custom-call(s32[16,4]{1,0:T(8,128)S(1)} %copy.13.refs_0_, s32[1]{0:T(128)} %bitcast.refs_1_, f32[1,512]{1,0:T(1,128)S(1)} %pad_maximum_fusion.2.refs_2_, ...), custom_call_target="tpu_custom_call" | custom-call | flops 1073741824 | bytes 5275648 | tf_op jit(solution)/shard_map/pallas_call | solution.py:287
  75.7 0.7 collective-permute-start.20
  76.4 4.2 %shard_map.123 = (bf16[64,2048]{1,0:T(8,128)(2,1)S(1)}, bf16[64,2048]{1,0:T(8,128)(2,1)S(1)}, bf16[64,2048]{1,0:T(8,128)(2,1)S(1)}, bf16[64,2048]{1,0:T(8,128)(2,1)S(1)}) custom-call(s32[16,4]{1,0:T(8,128)S(1)} %copy.13.refs_0_, s32[1]{0:T(128)} %bitcast.refs_1_, bf16[16,256,128]{2,1,0:T(8,128)(2,1)S(1)} %get-tuple-element.63.refs_2_, ...), custom_call_target="tpu_custom_call" | custom-call | flops 536870912 | bytes 1048576 | tf_op jit(solution)/shard_map/pallas_call | solution.py:287
  80.6 0.4 add_convert_fusion
  81.0 0.0 copy-start
  81.0 0.0 copy-start.9
  81.0 1.5 %collective-permute-start.21 = (bf16[256,2048]{1,0:T(8,128)(2,1)S(1)}, bf16[256,2048]{1,0:T(8,128)(2,1)S(1)}, u32[]{:S(2)}, u32[]{:S(2)}) collective-permute-start(bf16[256,2048]{1,0:T(8,128)(2,1)S(1)} %add_convert_fusion), channel_id=1, source_target_pairs={{0,8},{4,20},{8,0},{12,28},{16,24},{20,4},{24,16},{28,12},{1,9},{5... | collective-permute-start | bytes 3145736 | tf_op jit(solution)/shard_map/ppermute | solution.py:309
  82.5 0.3 collective-permute-start.17
  82.8 8.8 %collective-permute-done.17 = bf16[64,2048]{1,0:T(8,128)(2,1)S(1)} collective-permute-done((bf16[64,2048]{1,0:T(8,128)(2,1)S(1)}, bf16[64,2048]{1,0:T(8,128)(2,1)S(1)}, u32[]{:S(2)}, u32[]{:S(2)}) %collective-permute-start.17) | collective-permute-done | bytes 262176 | tf_op jit(solution)/shard_map/ppermute | solution.py:304
  91.7 0.3 collective-permute-start.18
  92.0 0.1 add_convert_fusion.2
  92.1 0.0 copy-start.2
  92.1 2.7 %collective-permute-start.19 = (bf16[64,2048]{1,0:T(8,128)(2,1)S(1)}, bf16[64,2048]{1,0:T(8,128)(2,1)S(1)}, u32[]{:S(2)}, u32[]{:S(2)}) collective-permute-start(bf16[64,2048]{1,0:T(8,128)(2,1)S(1)} %add_convert_fusion.2), channel_id=1, source_target_pairs={{0,2},{1,3},{2,0},{3,1},{4,6},{5,7},{6,4},{7,5},{8,10},{9,11},{10,... | collective-permute-start | bytes 786440 | tf_op jit(solution)/shard_map/ppermute | solution.py:304
  94.7 1.1 %collective-permute-done.21 = bf16[256,2048]{1,0:T(8,128)(2,1)S(1)} collective-permute-done((bf16[256,2048]{1,0:T(8,128)(2,1)S(1)}, bf16[256,2048]{1,0:T(8,128)(2,1)S(1)}, u32[]{:S(2)}, u32[]{:S(2)}) %collective-permute-start.21) | collective-permute-done | bytes 1048608 | tf_op jit(solution)/shard_map/ppermute | solution.py:309
  95.9 0.2 add_convert_fusion.1
  96.1 2.3 %collective-permute-start.22 = (bf16[128,2048]{1,0:T(8,128)(2,1)S(1)}, bf16[128,2048]{1,0:T(8,128)(2,1)S(1)}, u32[]{:S(2)}, u32[]{:S(2)}) collective-permute-start(bf16[128,2048]{1,0:T(8,128)(2,1)S(1)} %add_convert_fusion.1), channel_id=1, source_target_pairs={{0,16},{4,12},{8,24},{12,4},{16,0},{20,28},{24,8},{28,20},{1,17},{... | collective-permute-start | bytes 1572872 | tf_op jit(solution)/shard_map/ppermute | solution.py:309
  98.4 0.8 add_convert_fusion.3
  99.2 6.0 %collective-permute-done.18 = bf16[64,2048]{1,0:T(8,128)(2,1)S(1)} collective-permute-done((bf16[64,2048]{1,0:T(8,128)(2,1)S(1)}, bf16[64,2048]{1,0:T(8,128)(2,1)S(1)}, u32[]{:S(2)}, u32[]{:S(2)}) %collective-permute-start.18) | collective-permute-done | bytes 262176 | tf_op jit(solution)/shard_map/ppermute | solution.py:304
  105.2 0.1 convert_add_fusion.1.own
  105.3 1.5 %collective-permute-done.19.other = bf16[64,2048]{1,0:T(8,128)(2,1)S(1)} collective-permute-done((bf16[64,2048]{1,0:T(8,128)(2,1)S(1)}, bf16[64,2048]{1,0:T(8,128)(2,1)S(1)}, u32[]{:S(2)}, u32[]{:S(2)}) %collective-permute-start.19) | collective-permute-done | bytes 262176 | tf_op jit(solution)/shard_map/ppermute | solution.py:304
  106.8 1.1 shard_map.124
  107.9 0.3 convert_add_fusion
  108.2 1.1 fusion
  (46 shorter events, 0.2 us)
Async XLA Ops:
  0.6 20.9 %copy-start.1 = (bf16[64,2048]{1,0:T(8,128)(2,1)S(1)}, bf16[64,2048]{1,0:T(8,128)(2,1)}, u32[]{:S(2)}) copy-start(bf16[64,2048]{1,0:T(8,128)(2,1)} %upstream.1) | copy-start | bytes 786436
  0.6 38.6 %copy-start.14 = (s32[16,4]{0,1:T(4,128)S(1)}, s32[16,4]{0,1:T(4,128)}, u32[]{:S(2)}) copy-start(s32[16,4]{0,1:T(4,128)} %param.13) | copy-start | bytes 772
  0.7 40.5 %copy-start.3 = (f32[2048]{0:T(1024)S(1)}, f32[2048]{0:T(1024)}, u32[]{:S(2)}) copy-start(f32[2048]{0:T(1024)} %param.17) | copy-start | bytes 24580
  0.7 40.5 %copy-start.5 = (s32[64]{0:T(128)S(1)}, s32[64]{0:T(128)}, u32[]{:S(2)}) copy-start(s32[64]{0:T(128)} %param.14) | copy-start | bytes 772
  0.7 40.5 %copy-start.4 = (f32[2048]{0:T(1024)S(1)}, f32[2048]{0:T(1024)}, u32[]{:S(2)}) copy-start(f32[2048]{0:T(1024)} %param.10) | copy-start | bytes 24580
  1.8 10.2 %collective-permute-start.3 = (bf16[128,2048]{1,0:T(8,128)(2,1)S(1)}, bf16[128,2048]{1,0:T(8,128)(2,1)S(1)}, u32[]{:S(2)}, u32[]{:S(2)}) collective-permute-start(bf16[128,2048]{1,0:T(8,128)(2,1)S(1)} %pad_maximum_fusion.1), channel_id=1, source_target_pairs={{0,8},{4,20},{8,0},{12,28},{16,24},{20,4},{24,16},{28,12},{1,9},{5... | collective-permute-start | bytes 1572872 | tf_op jit(solution)/shard_map/ppermute | solution.py:309
  4.8 14.6 %collective-permute-start.1 = (bf16[64,2048]{1,0:T(8,128)(2,1)}, bf16[64,2048]{1,0:T(8,128)(2,1)S(1)}, u32[]{:S(2)}, u32[]{:S(2)}) collective-permute-start(bf16[64,2048]{1,0:T(8,128)(2,1)} %x_ref.1), channel_id=1, source_target_pairs={{0,2},{1,3},{2,0},{3,1},{4,6},{5,7},{6,4},{7,5},{8,10},{9,11},{10,... | collective-permute-start | bytes 786440 | tf_op jit(solution)/shard_map/ppermute | solution.py:304
  7.4 12.2 %collective-permute-start = (bf16[64,2048]{1,0:T(8,128)(2,1)}, bf16[64,2048]{1,0:T(8,128)(2,1)S(1)}, u32[]{:S(2)}, u32[]{:S(2)}) collective-permute-start(bf16[64,2048]{1,0:T(8,128)(2,1)} %x_ref.1), channel_id=1, source_target_pairs={{0,1},{1,0},{2,3},{3,2},{4,5},{5,4},{6,7},{7,6},{8,9},{9,8},{10,11... | collective-permute-start | bytes 786440 | tf_op jit(solution)/shard_map/ppermute | solution.py:304
  13.1 27.9 %copy-start.6 = (bf16[256,2048]{1,0:T(8,128)(2,1)}, bf16[256,2048]{1,0:T(8,128)(2,1)S(1)}, u32[]{:S(2)}) copy-start(bf16[256,2048]{1,0:T(8,128)(2,1)S(1)} %pad_maximum_fusion.refs_9_.refs_7_.refs_3_) | copy-start | bytes 3145732
  19.4 17.9 %copy-start.10 = (bf16[64,2048]{1,0:T(8,128)(2,1)}, bf16[64,2048]{1,0:T(8,128)(2,1)S(1)}, u32[]{:S(2)}) copy-start(bf16[64,2048]{1,0:T(8,128)(2,1)S(1)} %collective-permute-done.1.refs_4_) | copy-start | bytes 786436
  19.6 19.6 %copy-start.11 = (bf16[64,2048]{1,0:T(8,128)(2,1)}, bf16[64,2048]{1,0:T(8,128)(2,1)S(1)}, u32[]{:S(2)}) copy-start(bf16[64,2048]{1,0:T(8,128)(2,1)S(1)} %collective-permute-done.refs_3_) | copy-start | bytes 786436
  19.6 17.1 %collective-permute-start.4 = (bf16[256,2048]{1,0:T(8,128)(2,1)S(1)}, bf16[256,2048]{1,0:T(8,128)(2,1)S(1)}, u32[]{:S(2)}, u32[]{:S(2)}) collective-permute-start(bf16[256,2048]{1,0:T(8,128)(2,1)S(1)} %pad_maximum_fusion.refs_9_.refs_7_.refs_3_), channel_id=1, source_target_pairs={{0,16},{4,12},{8,24},{12,4},{16,0},{20,28},{24,8},{28,20},{1,17},{... | collective-permute-start | bytes 3145736 | tf_op jit(solution)/shard_map/ppermute | solution.py:309
  20.1 14.1 %collective-permute-start.2 = (bf16[64,2048]{1,0:T(8,128)(2,1)S(1)}, bf16[64,2048]{1,0:T(8,128)(2,1)S(1)}, u32[]{:S(2)}, u32[]{:S(2)}) collective-permute-start(bf16[64,2048]{1,0:T(8,128)(2,1)S(1)} %collective-permute-done.1.refs_4_), channel_id=1, source_target_pairs={{0,1},{1,0},{2,3},{3,2},{4,5},{5,4},{6,7},{7,6},{8,9},{9,8},{10,11... | collective-permute-start | bytes 786440 | tf_op jit(solution)/shard_map/ppermute | solution.py:304
  21.6 15.1 %collective-permute-start.5 = (bf16[64,2048]{1,0:T(8,128)(2,1)S(1)}, bf16[64,2048]{1,0:T(8,128)(2,1)}, u32[]{:S(2)}, u32[]{:S(2)}) collective-permute-start(bf16[64,2048]{1,0:T(8,128)(2,1)S(1)} %copy-done.1), channel_id=1, source_target_pairs={{0,2},{1,3},{2,0},{3,1},{4,6},{5,7},{6,4},{7,5},{8,10},{9,11},{10,... | collective-permute-start | bytes 786440 | tf_op jit(solution)/shard_map/ppermute | solution.py:304
  34.2 5.1 %copy-start.13 = (bf16[64,2048]{1,0:T(8,128)(2,1)}, bf16[64,2048]{1,0:T(8,128)(2,1)S(1)}, u32[]{:S(2)}) copy-start(bf16[64,2048]{1,0:T(8,128)(2,1)S(1)} %collective-permute-done.2.refs_5_) | copy-start | bytes 786436
  36.7 3.4 %collective-permute-start.6 = (bf16[256,2048]{1,0:T(8,128)(2,1)S(1)}, bf16[256,2048]{1,0:T(8,128)(2,1)S(1)}, u32[]{:S(2)}, u32[]{:S(2)}) collective-permute-start(bf16[256,2048]{1,0:T(8,128)(2,1)S(1)} %pad_maximum_fusion.refs_9_.refs_7_.refs_3_), channel_id=1, source_target_pairs={{0,4},{4,0},{8,12},{12,8},{16,20},{20,16},{24,28},{28,24},{1,5},{5... | collective-permute-start | bytes 3145736 | tf_op jit(solution)/shard_map/ppermute | solution.py:304
  36.7 4.3 %copy-start.7 = (bf16[256,2048]{1,0:T(8,128)(2,1)}, bf16[256,2048]{1,0:T(8,128)(2,1)S(1)}, u32[]{:S(2)}) copy-start(bf16[256,2048]{1,0:T(8,128)(2,1)S(1)} %collective-permute-done.4.refs_10_.refs_8_.refs_4_) | copy-start | bytes 3145732
  36.7 4.3 %collective-permute-start.7 = (bf16[256,2048]{1,0:T(8,128)(2,1)S(1)}, bf16[256,2048]{1,0:T(8,128)(2,1)}, u32[]{:S(2)}, u32[]{:S(2)}) collective-permute-start(bf16[256,2048]{1,0:T(8,128)(2,1)S(1)} %collective-permute-done.4.refs_10_.refs_8_.refs_4_), channel_id=1, source_target_pairs={{0,4},{4,0},{8,12},{12,8},{16,20},{20,16},{24,28},{28,24},{1,5},{5... | collective-permute-start | bytes 3145736 | tf_op jit(solution)/shard_map/ppermute | solution.py:304
  37.2 13.4 %collective-permute-start.8 = (bf16[64,2048]{1,0:T(8,128)(2,1)S(1)}, bf16[64,2048]{1,0:T(8,128)(2,1)}, u32[]{:S(2)}, u32[]{:S(2)}) collective-permute-start(bf16[64,2048]{1,0:T(8,128)(2,1)S(1)} %copy-done.1), channel_id=1, source_target_pairs={{0,1},{1,0},{2,3},{3,2},{4,5},{5,4},{6,7},{7,6},{8,9},{9,8},{10,11... | collective-permute-start | bytes 786440 | tf_op jit(solution)/shard_map/ppermute | solution.py:304
  37.4 13.9 %collective-permute-start.9 = (bf16[64,2048]{1,0:T(8,128)(2,1)}, bf16[64,2048]{1,0:T(8,128)(2,1)}, u32[]{:S(2)}, u32[]{:S(2)}) collective-permute-start(bf16[64,2048]{1,0:T(8,128)(2,1)} %collective-permute-done.5.refs_4_.refs_14_), channel_id=1, source_target_pairs={{0,1},{1,0},{2,3},{3,2},{4,5},{5,4},{6,7},{7,6},{8,9},{9,8},{10,11... | collective-permute-start | bytes 786440 | tf_op jit(solution)/shard_map/ppermute | solution.py:304
  40.1 1.1 copy-start.8
  51.2 3.6 %collective-permute-start.10 = (f32[1,320]{1,0:T(1,128)S(1)}, f32[1,320]{1,0:T(1,128)S(1)}, u32[]{:S(2)}, u32[]{:S(2)}) collective-permute-start(f32[1,320]{1,0:T(1,128)S(1)} %get-tuple-element.49), channel_id=1, source_target_pairs={{0,1},{1,0},{2,3},{3,2},{4,5},{5,4},{6,7},{7,6},{8,9},{9,8},{10,11... | collective-permute-start | bytes 3848 | tf_op jit(solution)/shard_map/ppermute | solution.py:304
  55.0 8.0 %collective-permute-start.11 = (bf16[64,2048]{1,0:T(8,128)(2,1)}, bf16[64,2048]{1,0:T(8,128)(2,1)S(1)}, u32[]{:S(2)}, u32[]{:S(2)}) collective-permute-start(bf16[64,2048]{1,0:T(8,128)(2,1)} %get-tuple-element.50), channel_id=1, source_target_pairs={{0,1},{1,0},{2,3},{3,2},{4,5},{5,4},{6,7},{7,6},{8,9},{9,8},{10,11... | collective-permute-start | bytes 786440 | tf_op jit(solution)/shard_map/ppermute | solution.py:304
  55.4 7.6 %copy-start.12 = (bf16[64,2048]{1,0:T(8,128)(2,1)S(1)}, bf16[64,2048]{1,0:T(8,128)(2,1)}, u32[]{:S(2)}) copy-start(bf16[64,2048]{1,0:T(8,128)(2,1)} %get-tuple-element.54) | copy-start | bytes 786436
  55.4 8.1 %copy-start.16 = (bf16[64,2048]{1,0:T(8,128)(2,1)S(1)}, bf16[64,2048]{1,0:T(8,128)(2,1)}, u32[]{:S(2)}) copy-start(bf16[64,2048]{1,0:T(8,128)(2,1)} %get-tuple-element.53) | copy-start | bytes 786436
  55.4 12.4 %copy-start.15 = (f32[128]{0:T(128)S(1)}, f32[128]{0:T(128)}, u32[]{:S(2)}) copy-start(f32[128]{0:T(128)} %param.15) | copy-start | bytes 1540
  55.4 7.5 %collective-permute-start.13 = (f32[1,384]{1,0:T(1,128)S(1)}, f32[1,384]{1,0:T(1,128)S(1)}, u32[]{:S(2)}, u32[]{:S(2)}) collective-permute-start(f32[1,384]{1,0:T(1,128)S(1)} %pad_maximum_fusion.3), channel_id=1, source_target_pairs={{0,2},{1,3},{2,0},{3,1},{4,6},{5,7},{6,4},{7,5},{8,10},{9,11},{10,... | collective-permute-start | bytes 4616 | tf_op jit(solution)/shard_map/ppermute | solution.py:304
  63.1 12.6 %collective-permute-start.14 = (bf16[64,2048]{1,0:T(8,128)(2,1)S(1)}, bf16[64,2048]{1,0:T(8,128)(2,1)S(1)}, u32[]{:S(2)}, u32[]{:S(2)}) collective-permute-start(bf16[64,2048]{1,0:T(8,128)(2,1)S(1)} %add_convert_fusion.4), channel_id=1, source_target_pairs={{0,2},{1,3},{2,0},{3,1},{4,6},{5,7},{6,4},{7,5},{8,10},{9,11},{10,... | collective-permute-start | bytes 786440 | tf_op jit(solution)/shard_map/ppermute | solution.py:304
  63.4 12.2 %collective-permute-start.12 = (bf16[64,2048]{1,0:T(8,128)(2,1)S(1)}, bf16[64,2048]{1,0:T(8,128)(2,1)S(1)}, u32[]{:S(2)}, u32[]{:S(2)}) collective-permute-start(bf16[64,2048]{1,0:T(8,128)(2,1)S(1)} %copy-done.16), channel_id=1, source_target_pairs={{0,1},{1,0},{2,3},{3,2},{4,5},{5,4},{6,7},{7,6},{8,9},{9,8},{10,11... | collective-permute-start | bytes 786440 | tf_op jit(solution)/shard_map/ppermute | solution.py:304
  65.2 2.7 %collective-permute-start.16 = (f32[1,512]{1,0:T(1,128)S(1)}, f32[1,512]{1,0:T(1,128)S(1)}, u32[]{:S(2)}, u32[]{:S(2)}) collective-permute-start(f32[1,512]{1,0:T(1,128)S(1)} %pad_maximum_fusion.2.refs_2_), channel_id=1, source_target_pairs={{4,8},{12,16},{20,24},{8,4},{16,12},{24,20},{5,9},{13,17},{21,25},... | collective-permute-start | bytes 6152 | tf_op jit(solution)/shard_map/ppermute | solution.py:472
  65.8 2.7 %collective-permute-start.15 = (f32[1,512]{1,0:T(1,128)S(1)}, f32[1,512]{1,0:T(1,128)S(1)}, u32[]{:S(2)}, u32[]{:S(2)}) collective-permute-start(f32[1,512]{1,0:T(1,128)S(1)} %pad_maximum_fusion.2.refs_2_), channel_id=1, source_target_pairs={{0,4},{4,0},{8,12},{12,8},{16,20},{20,16},{24,28},{28,24},{1,5},{5... | collective-permute-start | bytes 6152 | tf_op jit(solution)/shard_map/ppermute | solution.py:304
  75.7 4.9 %collective-permute-start.20 = (bf16[512,2048]{1,0:T(8,128)(2,1)S(1)}, bf16[512,2048]{1,0:T(8,128)(2,1)S(1)}, u32[]{:S(2)}, u32[]{:S(2)}) collective-permute-start(bf16[512,2048]{1,0:T(8,128)(2,1)S(1)} %get-tuple-element.72), channel_id=1, source_target_pairs={{0,4},{4,0},{8,12},{12,8},{16,20},{20,16},{24,28},{28,24},{1,5},{5... | collective-permute-start | bytes 6291464 | tf_op jit(solution)/shard_map/ppermute | solution.py:304
  81.0 17.4 %copy-start = (bf16[64,2048]{1,0:T(8,128)(2,1)S(1)}, bf16[64,2048]{1,0:T(8,128)(2,1)}, u32[]{:S(2)}) copy-start(bf16[64,2048]{1,0:T(8,128)(2,1)} %x_ref.1) | copy-start | bytes 786436
  81.0 17.4 %copy-start.9 = (bf16[64,2048]{1,0:T(8,128)(2,1)S(1)}, bf16[64,2048]{1,0:T(8,128)(2,1)}, u32[]{:S(2)}) copy-start(bf16[64,2048]{1,0:T(8,128)(2,1)} %get-tuple-element.43) | copy-start | bytes 786436
  81.0 14.9 %collective-permute-start.21 = (bf16[256,2048]{1,0:T(8,128)(2,1)S(1)}, bf16[256,2048]{1,0:T(8,128)(2,1)S(1)}, u32[]{:S(2)}, u32[]{:S(2)}) collective-permute-start(bf16[256,2048]{1,0:T(8,128)(2,1)S(1)} %add_convert_fusion), channel_id=1, source_target_pairs={{0,8},{4,20},{8,0},{12,28},{16,24},{20,4},{24,16},{28,12},{1,9},{5... | collective-permute-start | bytes 3145736 | tf_op jit(solution)/shard_map/ppermute | solution.py:309
  82.5 9.2 %collective-permute-start.17 = (bf16[64,2048]{1,0:T(8,128)(2,1)S(1)}, bf16[64,2048]{1,0:T(8,128)(2,1)S(1)}, u32[]{:S(2)}, u32[]{:S(2)}) collective-permute-start(bf16[64,2048]{1,0:T(8,128)(2,1)S(1)} %get-tuple-element.66), channel_id=1, source_target_pairs={{0,1},{1,0},{2,3},{3,2},{4,5},{5,4},{6,7},{7,6},{8,9},{9,8},{10,11... | collective-permute-start | bytes 786440 | tf_op jit(solution)/shard_map/ppermute | solution.py:304
  91.7 13.6 %collective-permute-start.18 = (bf16[64,2048]{1,0:T(8,128)(2,1)S(1)}, bf16[64,2048]{1,0:T(8,128)(2,1)S(1)}, u32[]{:S(2)}, u32[]{:S(2)}) collective-permute-start(bf16[64,2048]{1,0:T(8,128)(2,1)S(1)} %get-tuple-element.67), channel_id=1, source_target_pairs={{0,1},{1,0},{2,3},{3,2},{4,5},{5,4},{6,7},{7,6},{8,9},{9,8},{10,11... | collective-permute-start | bytes 786440 | tf_op jit(solution)/shard_map/ppermute | solution.py:304
  92.1 14.7 %copy-start.2 = (bf16[64,2048]{1,0:T(8,128)(2,1)S(1)}, bf16[64,2048]{1,0:T(8,128)(2,1)}, u32[]{:S(2)}) copy-start(bf16[64,2048]{1,0:T(8,128)(2,1)} %upstream.1) | copy-start | bytes 786436
  92.1 14.7 %collective-permute-start.19 = (bf16[64,2048]{1,0:T(8,128)(2,1)S(1)}, bf16[64,2048]{1,0:T(8,128)(2,1)S(1)}, u32[]{:S(2)}, u32[]{:S(2)}) collective-permute-start(bf16[64,2048]{1,0:T(8,128)(2,1)S(1)} %add_convert_fusion.2), channel_id=1, source_target_pairs={{0,2},{1,3},{2,0},{3,1},{4,6},{5,7},{6,4},{7,5},{8,10},{9,11},{10,... | collective-permute-start | bytes 786440 | tf_op jit(solution)/shard_map/ppermute | solution.py:304
  96.1 11.7 %collective-permute-start.22 = (bf16[128,2048]{1,0:T(8,128)(2,1)S(1)}, bf16[128,2048]{1,0:T(8,128)(2,1)S(1)}, u32[]{:S(2)}, u32[]{:S(2)}) collective-permute-start(bf16[128,2048]{1,0:T(8,128)(2,1)S(1)} %add_convert_fusion.1), channel_id=1, source_target_pairs={{0,16},{4,12},{8,24},{12,4},{16,0},{20,28},{24,8},{28,20},{1,17},{... | collective-permute-start | bytes 1572872 | tf_op jit(solution)/shard_map/ppermute | solution.py:309

commit v4 on v3

--- a/solution.py
+++ b/solution.py
@@ -115,7 +115,8 @@
         half = 0.5 * (1.0 + t)
         a = (v * half).astype(BF16)
         act[j] = a
-        dact[j] = half + 0.5 * v * (1.0 - t * t) * (GELU_A * (1.0 + 3.0 * GELU_B * v2))
+        slope = half + 0.5 * v * (1.0 - t * t) * (GELU_A * (1.0 + 3.0 * GELU_B * v2))
+        dact[j] = slope.astype(BF16)
         pltpu.make_async_copy(act.at[j], act_out.at[j], sems.at[nf + 3]).start()
         pltpu.make_async_copy(dact.at[j], dact_out.at[j], sems.at[nf + 4]).start()
         terms = dot(a, wout[:, column(j)], NT)
@@ -198,7 +199,7 @@
         turned = jnp.concatenate([three_terms(readout[:, column(w)]) for w in which], axis=1)
         rows_of = jnp.concatenate([picked, turned, jnp.zeros_like(turned)], axis=0)
         both = dot(rows_of, wout[:, column(j)])
-        upper[j] = both[: nf * rows]
+        upper[j] = both[: nf * rows].astype(BF16)
         pltpu.make_async_copy(upper.at[j], upper_out.at[j], sems.at[nf + 1]).start()
         turn[:, column(j)] = jnp.sum(both[nf * rows : nf * rows + 8], axis=0, keepdims=True)
 
@@ -242,7 +243,8 @@
 
     @loop(nj)
     def _(j):
-        pre_grad[j] = ((upper[j] + across * turn[:, column(j)]) * dact[j]).astype(BF16)
+        whole = upper[j].astype(F32) + across * turn[:, column(j)]
+        pre_grad[j] = (whole * dact[j].astype(F32)).astype(BF16)
 
     normed_wait()
     act_wait()
@@ -322,7 +324,7 @@
         flat = [m for ms in masks for m in ms]
         held = [whole, swap_tok(whole, even, odd)]
         masks = [flat, [(a ^ even, b ^ odd) for a, b in flat]]
-    other = [swap(after(h, *ties[1]), "tok", 1) for h in held]
+    other = [swap(after(h, *tie), "tok", 1) for h, tie in zip(held, ties[1:])]
     return held + other, masks + [[(b ^ 1, a ^ 1) for a, b in ms] for ms in masks]
 
 
@@ -400,13 +402,12 @@
     upstream_far = swap(after(upstream, near, far), "feat", feat_bits[-1])
     ups = gather_feat(upstream, feat_bits, upstream_far)
     parts, masks = gather_tok(
-        w_in, w_out, bits, ((near, far), xs[2:] + [upstream_far])
+        w_in, w_out, bits, ((near, far), [upstream_far], xs[2:])
     )
     parts = [(HBM, p) for p in parts]
 
     by_feature = pltpu.VMEM((fb, tokens, BLK), BF16)
     by_hidden = pltpu.VMEM((nj, tokens, BLK), BF16)
-    by_hidden_wide = pltpu.VMEM((nj, tokens, BLK), F32)
     weight = pltpu.VMEM((kb * BLK, hidden), BF16)
     summed = pltpu.VMEM((fb, tokens, BLK), F32)
     piece = sds((rows, width), BF16)
@@ -416,7 +417,7 @@
         [
             (HBM, sds((fb, tokens, BLK), BF16)),
             (HBM, sds((nj, tokens, BLK), BF16)),
-            (HBM, sds((nj, tokens, BLK), F32)),
+            (HBM, sds((nj, tokens, BLK), BF16)),
             (VM, sds((1, tokens + rows), F32)),
         ]
         + [(HBM, piece)] * nf,
@@ -428,7 +429,7 @@
             pltpu.VMEM((nf, rows, width), BF16),
             by_feature,
             by_hidden,
-            by_hidden_wide,
+            by_hidden,
             weight,
             weight,
             summed,
@@ -443,7 +444,7 @@
     upper, turn = call(
         functools.partial(upper_kernel, masks, nf),
         [
-            (HBM, sds((nj, tokens, BLK), F32)),
+            (HBM, sds((nj, tokens, BLK), BF16)),
             (VM, sds((1, hidden), F32)),
         ],
         scalars + [(HBM, u) for u in ups] + [(VM, readout_row)] + parts,
@@ -451,7 +452,7 @@
             pltpu.VMEM((nf, rows, width), BF16),
             by_feature,
             weight,
-            by_hidden_wide,
+            by_hidden,
             pltpu.SemaphoreType.DMA((nf + 2,)),
         ],
         flops,
@@ -487,8 +488,8 @@
         + [(HBM, a) for a in (upper, dact, normed, act)]
         + [(HBM, u) for u in ups],
         [
-            by_hidden_wide,
-            by_hidden_wide,
+            by_hidden,
+            by_hidden,
             by_feature,
             by_hidden,
             by_feature,
@@ -514,6 +515,7 @@
         sums.add(swap_tok(sums.away(), *pair))
     grads = sums.total()
     grad_out, grad_in = grads[:depth], grads[depth:]
+    got = after(got, grad_out, grad_in)
     (input_grad,) = call(
         finish_kernel,
         [(VM, piece)],

time: 109 us -> 107 us (0.982)
  waiting for transfers between devices: 46 us -> 44 us
    ppermute x18, waiting for transfers between devices: 41.8 us -> 38 us  [swap(): return lax.ppermute(value, axis, [(i, i ^ mask) for i in range(n)])]
    ppermute x4, waiting for transfers between devices: 4.14 us -> 6.01 us  [swap_tok(): lax.ppermute(value, 'tok', [(i, i ^ (odd if i & 1 else even)) for i in ra...]
  transfers between devices with their start and end apart: 23 -> 23, of which waited for: 14 -> 13; matrix products, arithmetic and copies ran while one was open for 2% -> 4% of each run, Pallas kernels for 24% -> 23%
where the time goes in v4:
time: 107 us
  waiting for transfers between devices  44 us (41%)
  starting transfers between devices  30 us (28%)
  Pallas kernels  25.9 us (24%)
  other arithmetic  4.36 us (4%)
  local copies, waits for them, and re-layouts  1.56 us (1%)
    ppermute x18, waiting for transfers between devices, swap(): return lax.ppermute(value, axis, [(i, i ^ mask) for i in range(n)])  38 us
    pallas_call x5, Pallas kernels, call(): pl.pallas_call(body, out_shape=[pltpu.HBM(o.shape, o.dtype) if m is HBM e...  25.9 us
    ppermute x18, starting transfers between devices, swap(): return lax.ppermute(value, axis, [(i, i ^ mask) for i in range(n)])  22.9 us
    ppermute x4, starting transfers between devices, swap_tok(): lax.ppermute(value, 'tok', [(i, i ^ (odd if i & 1 else even)) for i in ra...  6.43 us
    ppermute x4, waiting for transfers between devices, swap_tok(): lax.ppermute(value, 'tok', [(i, i ^ (odd if i & 1 else even)) for i in ra...  6.01 us
    concatenate x2, other arithmetic, gather_tok(): whole = jnp.concatenate(held, axis=0)  2.23 us
  transfers between devices with their start and end apart: 23, of which 13 were waited for; matrix products, arithmetic and copies ran while one was open for 4% of the time, Pallas kernels for 23%

profile of v4, /device:TPU:0, one launch (start us, length us, event | category | flops | bytes accessed | tf_op | source)
XLA Modules:
  0.0 106.7 jit_solution(10042540576664113312)
XLA Ops:
  0.6 0.0 copy-start.1
  0.7 1.1 %pad_maximum_fusion.1 = bf16[128,2048]{1,0:T(8,128)(2,1)S(1)} fusion(bf16[64,2048]{1,0:T(8,128)(2,1)} %param.12, bf16[64,2048]{1,0:T(8,128)(2,1)} %param.11), kind=kLoop, calls=%fused_computation.4 | loop fusion | flops 1048576 | bytes 1048576 | tf_op jit(solution)/shard_map/concatenate | solution.py:321
  1.8 3.0 %collective-permute-start.3 = (bf16[128,2048]{1,0:T(8,128)(2,1)S(1)}, bf16[128,2048]{1,0:T(8,128)(2,1)S(1)}, u32[]{:S(2)}, u32[]{:S(2)}) collective-permute-start(bf16[128,2048]{1,0:T(8,128)(2,1)S(1)} %pad_maximum_fusion.1), channel_id=1, source_target_pairs={{0,8},{4,20},{8,0},{12,28},{16,24},{20,4},{24,16},{28,12},{1,9},{5... | collective-permute-start | bytes 1572872 | tf_op jit(solution)/shard_map/ppermute | solution.py:311
  4.8 2.6 %collective-permute-start.1 = (bf16[64,2048]{1,0:T(8,128)(2,1)}, bf16[64,2048]{1,0:T(8,128)(2,1)S(1)}, u32[]{:S(2)}, u32[]{:S(2)}) collective-permute-start(bf16[64,2048]{1,0:T(8,128)(2,1)} %x_ref.1), channel_id=1, source_target_pairs={{0,2},{1,3},{2,0},{3,1},{4,6},{5,7},{6,4},{7,5},{8,10},{9,11},{10,... | collective-permute-start | bytes 786440 | tf_op jit(solution)/shard_map/ppermute | solution.py:306
  7.4 1.6 %collective-permute-start = (bf16[64,2048]{1,0:T(8,128)(2,1)}, bf16[64,2048]{1,0:T(8,128)(2,1)S(1)}, u32[]{:S(2)}, u32[]{:S(2)}) collective-permute-start(bf16[64,2048]{1,0:T(8,128)(2,1)} %x_ref.1), channel_id=1, source_target_pairs={{0,1},{1,0},{2,3},{3,2},{4,5},{5,4},{6,7},{7,6},{8,9},{9,8},{10,11... | collective-permute-start | bytes 786440 | tf_op jit(solution)/shard_map/ppermute | solution.py:306
  9.0 3.0 %collective-permute-done.3 = bf16[128,2048]{1,0:T(8,128)(2,1)S(1)} collective-permute-done((bf16[128,2048]{1,0:T(8,128)(2,1)S(1)}, bf16[128,2048]{1,0:T(8,128)(2,1)S(1)}, u32[]{:S(2)}, u32[]{:S(2)}) %collective-permute-start.3) | collective-permute-done | bytes 524320 | tf_op jit(solution)/shard_map/ppermute | solution.py:311
  12.0 1.1 %pad_maximum_fusion.refs_9_.refs_7_.refs_3_ = bf16[256,2048]{1,0:T(8,128)(2,1)S(1)} fusion(bf16[128,2048]{1,0:T(8,128)(2,1)S(1)} %collective-permute-done.3, bf16[64,2048]{1,0:T(8,128)(2,1)} %param.12, bf16[64,2048]{1,0:T(8,128)(2,1)} %param.11), kind=kLoop, calls=%fused_computation.1 | loop fusion | flops 3145728 | bytes 2097152 | tf_op jit(solution)/shard_map/concatenate | solution.py:321
  13.1 6.3 %collective-permute-done.1.refs_4_ = bf16[64,2048]{1,0:T(8,128)(2,1)S(1)} collective-permute-done((bf16[64,2048]{1,0:T(8,128)(2,1)}, bf16[64,2048]{1,0:T(8,128)(2,1)S(1)}, u32[]{:S(2)}, u32[]{:S(2)}) %collective-permute-start.1) | collective-permute-done | bytes 262176 | tf_op jit(solution)/shard_map/ppermute | solution.py:306
  19.4 0.2 collective-permute-done.refs_3_
  19.6 0.5 collective-permute-start.4
  20.1 1.4 %collective-permute-start.5 = (bf16[64,2048]{1,0:T(8,128)(2,1)S(1)}, bf16[64,2048]{1,0:T(8,128)(2,1)}, u32[]{:S(2)}, u32[]{:S(2)}) collective-permute-start(bf16[64,2048]{1,0:T(8,128)(2,1)S(1)} %copy-done.1), channel_id=1, source_target_pairs={{0,2},{1,3},{2,0},{3,1},{4,6},{5,7},{6,4},{7,5},{8,10},{9,11},{10,... | collective-permute-start | bytes 786440 | tf_op jit(solution)/shard_map/ppermute | solution.py:306
  21.5 2.5 %collective-permute-start.2 = (bf16[64,2048]{1,0:T(8,128)(2,1)S(1)}, bf16[64,2048]{1,0:T(8,128)(2,1)S(1)}, u32[]{:S(2)}, u32[]{:S(2)}) collective-permute-start(bf16[64,2048]{1,0:T(8,128)(2,1)S(1)} %collective-permute-done.1.refs_4_), channel_id=1, source_target_pairs={{0,1},{1,0},{2,3},{3,2},{4,5},{5,4},{6,7},{7,6},{8,9},{9,8},{10,11... | collective-permute-start | bytes 786440 | tf_op jit(solution)/shard_map/ppermute | solution.py:306
  24.0 11.6 %collective-permute-done.5.refs_4_.refs_14_ = bf16[64,2048]{1,0:T(8,128)(2,1)} collective-permute-done((bf16[64,2048]{1,0:T(8,128)(2,1)S(1)}, bf16[64,2048]{1,0:T(8,128)(2,1)}, u32[]{:S(2)}, u32[]{:S(2)}) %collective-permute-start.5) | collective-permute-done | bytes 262176 | tf_op jit(solution)/shard_map/ppermute | solution.py:306
  35.6 0.0 collective-permute-start.6
  35.6 0.0 collective-permute-done.2.refs_5_
  35.6 0.0 collective-permute-done.4.refs_10_.refs_8_.refs_4_
  35.6 0.6 collective-permute-start.7
  36.2 2.0 %collective-permute-start.9 = (bf16[64,2048]{1,0:T(8,128)(2,1)}, bf16[64,2048]{1,0:T(8,128)(2,1)}, u32[]{:S(2)}, u32[]{:S(2)}) collective-permute-start(bf16[64,2048]{1,0:T(8,128)(2,1)} %collective-permute-done.5.refs_4_.refs_14_), channel_id=1, source_target_pairs={{0,1},{1,0},{2,3},{3,2},{4,5},{5,4},{6,7},{7,6},{8,9},{9,8},{10,11... | collective-permute-start | bytes 786440 | tf_op jit(solution)/shard_map/ppermute | solution.py:306
  38.2 0.1 copy.13.refs_0_
  38.3 0.5 collective-permute-done.6.refs_11_.refs_9_.refs_5_
  38.8 1.1 %collective-permute-done.7.refs_12_.refs_10_.refs_6_ = bf16[256,2048]{1,0:T(8,128)(2,1)} collective-permute-done((bf16[256,2048]{1,0:T(8,128)(2,1)S(1)}, bf16[256,2048]{1,0:T(8,128)(2,1)}, u32[]{:S(2)}, u32[]{:S(2)}) %collective-permute-start.7) | collective-permute-done | bytes 1048608 | tf_op jit(solution)/shard_map/ppermute | solution.py:306
  39.9 9.4 %shard_map.120 = (bf16[16,256,128]{2,1,0:T(8,128)(2,1)}, bf16[16,256,128]{2,1,0:T(8,128)(2,1)}, bf16[16,256,128]{2,1,0:T(8,128)(2,1)}, f32[1,320]{1,0:T(1,128)S(...) custom-call(s32[16,4]{1,0:T(8,128)S(1)} %copy.13.refs_0_, ...), custom_call_target="tpu_custom_call" | custom-call | flops 1073741824 | bytes 4195584 | tf_op jit(solution)/shard_map/pallas_call | solution.py:289
  49.4 0.0 collective-permute-done.8.refs_3_.refs_13_
  49.4 0.8 collective-permute-done.9.refs_5_.refs_15_
  50.2 0.3 collective-permute-start.10
  50.5 3.3 %collective-permute-done.10 = f32[1,320]{1,0:T(1,128)S(1)} collective-permute-done((f32[1,320]{1,0:T(1,128)S(1)}, f32[1,320]{1,0:T(1,128)S(1)}, u32[]{:S(2)}, u32[]{:S(2)}) %collective-permute-start.10) | collective-permute-done | bytes 1312 | tf_op jit(solution)/shard_map/ppermute | solution.py:306
  53.8 0.1 reshape.39
  53.9 0.1 reshape.40
  54.0 0.3 collective-permute-start.11
  54.3 0.1 pad_maximum_fusion.3
  54.4 2.6 %collective-permute-start.13 = (f32[1,384]{1,0:T(1,128)S(1)}, f32[1,384]{1,0:T(1,128)S(1)}, u32[]{:S(2)}, u32[]{:S(2)}) collective-permute-start(f32[1,384]{1,0:T(1,128)S(1)} %pad_maximum_fusion.3), channel_id=1, source_target_pairs={{0,2},{1,3},{2,0},{3,1},{4,6},{5,7},{6,4},{7,5},{8,10},{9,11},{10,... | collective-permute-start | bytes 4616 | tf_op jit(solution)/shard_map/ppermute | solution.py:306
  57.0 4.7 %shard_map.121 = (bf16[16,256,128]{2,1,0:T(8,128)(2,1)}, f32[1,2048]{1,0:T(1,128)S(1)}) custom-call(s32[16,4]{1,0:T(8,128)S(1)} %copy.13.refs_0_, s32[1]{0:T(128)} %bitcast.refs_1_, bf16[64,2048]{1,0:T(8,128)(2,1)} %upstream.1, bf16[64,2048]{1,0:T(8,128)(2,1)} %collective-permute-done.8.refs_3_.refs_13_, ...), custom_call_target="tpu_custom_call" | custom-call | flops 536870912 | bytes 1056768 | tf_op jit(solution)/shard_map/pallas_call | solution.py:289
  61.8 0.1 pad_maximum_fusion.2.refs_2_
  61.9 0.0 collective-permute-done.11
  61.9 0.1 add_convert_fusion.4
  62.0 0.4 collective-permute-start.14
  62.4 1.7 %collective-permute-start.12 = (bf16[64,2048]{1,0:T(8,128)(2,1)S(1)}, bf16[64,2048]{1,0:T(8,128)(2,1)S(1)}, u32[]{:S(2)}, u32[]{:S(2)}) collective-permute-start(bf16[64,2048]{1,0:T(8,128)(2,1)S(1)} %copy-done.16), channel_id=1, source_target_pairs={{0,1},{1,0},{2,3},{3,2},{4,5},{5,4},{6,7},{7,6},{8,9},{9,8},{10,11... | collective-permute-start | bytes 786440 | tf_op jit(solution)/shard_map/ppermute | solution.py:306
  64.1 0.6 collective-permute-start.16
  64.8 2.5 %collective-permute-start.15 = (f32[1,512]{1,0:T(1,128)S(1)}, f32[1,512]{1,0:T(1,128)S(1)}, u32[]{:S(2)}, u32[]{:S(2)}) collective-permute-start(f32[1,512]{1,0:T(1,128)S(1)} %pad_maximum_fusion.2.refs_2_), channel_id=1, source_target_pairs={{0,4},{4,0},{8,12},{12,8},{16,20},{20,16},{24,28},{28,24},{1,5},{5... | collective-permute-start | bytes 6152 | tf_op jit(solution)/shard_map/ppermute | solution.py:306
  67.3 0.1 copy.16.refs_5_
  67.4 0.7 collective-permute-done.15.refs_3_
  68.1 6.5 %shard_map.122 = (f32[64,128]{1,0:T(8,128)S(1)}, bf16[16,256,128]{2,1,0:T(8,128)(2,1)S(1)}, bf16[512,2048]{1,0:T(8,128)(2,1)S(1)}, bf16[512,2048]{1,0:T(8,128)(2,1)S(1)}) custom-call(s32[16,4]{1,0:T(8,128)S(1)} %copy.13.refs_0_, s32[1]{0:T(128)} %bitcast.refs_1_, f32[1,512]{1,0:T(1,128)S(1)} %pad_maximum_fusion.2.refs_2_, ...), custom_call_target="tpu_custom_call" | custom-call | flops 1073741824 | bytes 5275648 | tf_op jit(solution)/shard_map/pallas_call | solution.py:289
  74.6 0.7 collective-permute-start.20
  75.3 4.2 %shard_map.123 = (bf16[64,2048]{1,0:T(8,128)(2,1)S(1)}, bf16[64,2048]{1,0:T(8,128)(2,1)S(1)}, bf16[64,2048]{1,0:T(8,128)(2,1)S(1)}, bf16[64,2048]{1,0:T(8,128)(2,1)S(1)}) custom-call(s32[16,4]{1,0:T(8,128)S(1)} %copy.13.refs_0_, s32[1]{0:T(128)} %bitcast.refs_1_, bf16[16,256,128]{2,1,0:T(8,128)(2,1)S(1)} %get-tuple-element.64.refs_2_, ...), custom_call_target="tpu_custom_call" | custom-call | flops 536870912 | bytes 1048576 | tf_op jit(solution)/shard_map/pallas_call | solution.py:289
  79.5 0.4 add_convert_fusion
  79.9 0.0 copy-start
  79.9 0.0 copy-start.9
  79.9 1.4 %collective-permute-start.21 = (bf16[256,2048]{1,0:T(8,128)(2,1)S(1)}, bf16[256,2048]{1,0:T(8,128)(2,1)S(1)}, u32[]{:S(2)}, u32[]{:S(2)}) collective-permute-start(bf16[256,2048]{1,0:T(8,128)(2,1)S(1)} %add_convert_fusion), channel_id=1, source_target_pairs={{0,8},{4,20},{8,0},{12,28},{16,24},{20,4},{24,16},{28,12},{1,9},{5... | collective-permute-start | bytes 3145736 | tf_op jit(solution)/shard_map/ppermute | solution.py:311
  81.3 0.6 collective-permute-start.17
  82.0 8.0 %collective-permute-done.17 = bf16[64,2048]{1,0:T(8,128)(2,1)S(1)} collective-permute-done((bf16[64,2048]{1,0:T(8,128)(2,1)S(1)}, bf16[64,2048]{1,0:T(8,128)(2,1)S(1)}, u32[]{:S(2)}, u32[]{:S(2)}) %collective-permute-start.17) | collective-permute-done | bytes 262176 | tf_op jit(solution)/shard_map/ppermute | solution.py:306
  89.9 0.4 collective-permute-start.18
  90.3 0.1 add_convert_fusion.2
  90.4 2.7 %collective-permute-start.19 = (bf16[64,2048]{1,0:T(8,128)(2,1)S(1)}, bf16[64,2048]{1,0:T(8,128)(2,1)S(1)}, u32[]{:S(2)}, u32[]{:S(2)}) collective-permute-start(bf16[64,2048]{1,0:T(8,128)(2,1)S(1)} %add_convert_fusion.2), channel_id=1, source_target_pairs={{0,2},{1,3},{2,0},{3,1},{4,6},{5,7},{6,4},{7,5},{8,10},{9,11},{10,... | collective-permute-start | bytes 786440 | tf_op jit(solution)/shard_map/ppermute | solution.py:306
  93.0 1.7 %collective-permute-done.21 = bf16[256,2048]{1,0:T(8,128)(2,1)S(1)} collective-permute-done((bf16[256,2048]{1,0:T(8,128)(2,1)S(1)}, bf16[256,2048]{1,0:T(8,128)(2,1)S(1)}, u32[]{:S(2)}, u32[]{:S(2)}) %collective-permute-start.21) | collective-permute-done | bytes 1048608 | tf_op jit(solution)/shard_map/ppermute | solution.py:311
  94.8 0.2 add_convert_fusion.1
  95.0 1.6 %collective-permute-start.22 = (bf16[128,2048]{1,0:T(8,128)(2,1)S(1)}, bf16[128,2048]{1,0:T(8,128)(2,1)S(1)}, u32[]{:S(2)}, u32[]{:S(2)}) collective-permute-start(bf16[128,2048]{1,0:T(8,128)(2,1)S(1)} %add_convert_fusion.1), channel_id=1, source_target_pairs={{0,16},{4,12},{8,24},{12,4},{16,0},{20,28},{24,8},{28,20},{1,17},{... | collective-permute-start | bytes 1572872 | tf_op jit(solution)/shard_map/ppermute | solution.py:311
  96.6 0.8 add_convert_fusion.3
  97.4 5.5 %collective-permute-done.18 = bf16[64,2048]{1,0:T(8,128)(2,1)S(1)} collective-permute-done((bf16[64,2048]{1,0:T(8,128)(2,1)S(1)}, bf16[64,2048]{1,0:T(8,128)(2,1)S(1)}, u32[]{:S(2)}, u32[]{:S(2)}) %collective-permute-start.18) | collective-permute-done | bytes 262176 | tf_op jit(solution)/shard_map/ppermute | solution.py:306
  102.9 0.1 convert_add_fusion.1.own
  103.0 0.0 copy-start.2
  103.0 1.3 %collective-permute-done.22 = bf16[128,2048]{1,0:T(8,128)(2,1)S(1)} collective-permute-done((bf16[128,2048]{1,0:T(8,128)(2,1)S(1)}, bf16[128,2048]{1,0:T(8,128)(2,1)S(1)}, u32[]{:S(2)}, u32[]{:S(2)}) %collective-permute-start.22) | collective-permute-done | bytes 524320 | tf_op jit(solution)/shard_map/ppermute | solution.py:311
  104.3 0.3 convert_add_fusion
  104.6 1.0 fusion
  105.6 1.1 %shard_map.124 = bf16[64,2048]{1,0:T(8,128)(2,1)} custom-call(bf16[64,2048]{1,0:T(8,128)(2,1)S(1)} %copy-done, f32[1,2048]{1,0:T(1,128)S(1)} %bitcast.12, bf16[64,2048]{1,0:T(8,128)(2,1)S(1)} %copy-done.2, f32[1,2048]{1,0:T(1,128)S(1)} %bitcast.10, f32[64,128]{1,0:T(8,128)S(1)} %get-tuple-element.62.own_coeff, f32[64,2048]{1,0:T(8,128)S(1)} %convert_add_fusion.1.own, ...), custom_call_target="tpu_custom_call" | custom-call | flops 131072 | bytes 262144 | tf_op jit(solution)/shard_map/pallas_call | solution.py:289
  (46 shorter events, 0.2 us)
Async XLA Ops:
  0.6 19.4 %copy-start.1 = (bf16[64,2048]{1,0:T(8,128)(2,1)S(1)}, bf16[64,2048]{1,0:T(8,128)(2,1)}, u32[]{:S(2)}) copy-start(bf16[64,2048]{1,0:T(8,128)(2,1)} %upstream.1) | copy-start | bytes 786436
  0.6 37.6 %copy-start.14 = (s32[16,4]{0,1:T(4,128)S(1)}, s32[16,4]{0,1:T(4,128)}, u32[]{:S(2)}) copy-start(s32[16,4]{0,1:T(4,128)} %param.13) | copy-start | bytes 772
  0.7 39.3 %copy-start.3 = (f32[2048]{0:T(1024)S(1)}, f32[2048]{0:T(1024)}, u32[]{:S(2)}) copy-start(f32[2048]{0:T(1024)} %param.17) | copy-start | bytes 24580
  0.7 39.3 %copy-start.5 = (s32[64]{0:T(128)S(1)}, s32[64]{0:T(128)}, u32[]{:S(2)}) copy-start(s32[64]{0:T(128)} %param.14) | copy-start | bytes 772
  0.7 39.3 %copy-start.4 = (f32[2048]{0:T(1024)S(1)}, f32[2048]{0:T(1024)}, u32[]{:S(2)}) copy-start(f32[2048]{0:T(1024)} %param.10) | copy-start | bytes 24580
  1.8 10.2 %collective-permute-start.3 = (bf16[128,2048]{1,0:T(8,128)(2,1)S(1)}, bf16[128,2048]{1,0:T(8,128)(2,1)S(1)}, u32[]{:S(2)}, u32[]{:S(2)}) collective-permute-start(bf16[128,2048]{1,0:T(8,128)(2,1)S(1)} %pad_maximum_fusion.1), channel_id=1, source_target_pairs={{0,8},{4,20},{8,0},{12,28},{16,24},{20,4},{24,16},{28,12},{1,9},{5... | collective-permute-start | bytes 1572872 | tf_op jit(solution)/shard_map/ppermute | solution.py:311
  4.8 14.6 %collective-permute-start.1 = (bf16[64,2048]{1,0:T(8,128)(2,1)}, bf16[64,2048]{1,0:T(8,128)(2,1)S(1)}, u32[]{:S(2)}, u32[]{:S(2)}) collective-permute-start(bf16[64,2048]{1,0:T(8,128)(2,1)} %x_ref.1), channel_id=1, source_target_pairs={{0,2},{1,3},{2,0},{3,1},{4,6},{5,7},{6,4},{7,5},{8,10},{9,11},{10,... | collective-permute-start | bytes 786440 | tf_op jit(solution)/shard_map/ppermute | solution.py:306
  7.4 12.2 %collective-permute-start = (bf16[64,2048]{1,0:T(8,128)(2,1)}, bf16[64,2048]{1,0:T(8,128)(2,1)S(1)}, u32[]{:S(2)}, u32[]{:S(2)}) collective-permute-start(bf16[64,2048]{1,0:T(8,128)(2,1)} %x_ref.1), channel_id=1, source_target_pairs={{0,1},{1,0},{2,3},{3,2},{4,5},{5,4},{6,7},{7,6},{8,9},{9,8},{10,11... | collective-permute-start | bytes 786440 | tf_op jit(solution)/shard_map/ppermute | solution.py:306
  13.1 26.8 %copy-start.6 = (bf16[256,2048]{1,0:T(8,128)(2,1)}, bf16[256,2048]{1,0:T(8,128)(2,1)S(1)}, u32[]{:S(2)}) copy-start(bf16[256,2048]{1,0:T(8,128)(2,1)S(1)} %pad_maximum_fusion.refs_9_.refs_7_.refs_3_) | copy-start | bytes 3145732
  19.4 16.8 %copy-start.10 = (bf16[64,2048]{1,0:T(8,128)(2,1)}, bf16[64,2048]{1,0:T(8,128)(2,1)S(1)}, u32[]{:S(2)}) copy-start(bf16[64,2048]{1,0:T(8,128)(2,1)S(1)} %collective-permute-done.1.refs_4_) | copy-start | bytes 786436
  19.6 18.6 %copy-start.11 = (bf16[64,2048]{1,0:T(8,128)(2,1)}, bf16[64,2048]{1,0:T(8,128)(2,1)S(1)}, u32[]{:S(2)}) copy-start(bf16[64,2048]{1,0:T(8,128)(2,1)S(1)} %collective-permute-done.refs_3_) | copy-start | bytes 786436
  19.6 16.0 %collective-permute-start.4 = (bf16[256,2048]{1,0:T(8,128)(2,1)S(1)}, bf16[256,2048]{1,0:T(8,128)(2,1)S(1)}, u32[]{:S(2)}, u32[]{:S(2)}) collective-permute-start(bf16[256,2048]{1,0:T(8,128)(2,1)S(1)} %pad_maximum_fusion.refs_9_.refs_7_.refs_3_), channel_id=1, source_target_pairs={{0,16},{4,12},{8,24},{12,4},{16,0},{20,28},{24,8},{28,20},{1,17},{... | collective-permute-start | bytes 3145736 | tf_op jit(solution)/shard_map/ppermute | solution.py:311
  20.1 15.5 %collective-permute-start.5 = (bf16[64,2048]{1,0:T(8,128)(2,1)S(1)}, bf16[64,2048]{1,0:T(8,128)(2,1)}, u32[]{:S(2)}, u32[]{:S(2)}) collective-permute-start(bf16[64,2048]{1,0:T(8,128)(2,1)S(1)} %copy-done.1), channel_id=1, source_target_pairs={{0,2},{1,3},{2,0},{3,1},{4,6},{5,7},{6,4},{7,5},{8,10},{9,11},{10,... | collective-permute-start | bytes 786440 | tf_op jit(solution)/shard_map/ppermute | solution.py:306
  21.5 14.2 %collective-permute-start.2 = (bf16[64,2048]{1,0:T(8,128)(2,1)S(1)}, bf16[64,2048]{1,0:T(8,128)(2,1)S(1)}, u32[]{:S(2)}, u32[]{:S(2)}) collective-permute-start(bf16[64,2048]{1,0:T(8,128)(2,1)S(1)} %collective-permute-done.1.refs_4_), channel_id=1, source_target_pairs={{0,1},{1,0},{2,3},{3,2},{4,5},{5,4},{6,7},{7,6},{8,9},{9,8},{10,11... | collective-permute-start | bytes 786440 | tf_op jit(solution)/shard_map/ppermute | solution.py:306
  35.6 3.2 %collective-permute-start.6 = (bf16[256,2048]{1,0:T(8,128)(2,1)S(1)}, bf16[256,2048]{1,0:T(8,128)(2,1)S(1)}, u32[]{:S(2)}, u32[]{:S(2)}) collective-permute-start(bf16[256,2048]{1,0:T(8,128)(2,1)S(1)} %pad_maximum_fusion.refs_9_.refs_7_.refs_3_), channel_id=1, source_target_pairs={{0,4},{4,0},{8,12},{12,8},{16,20},{20,16},{24,28},{28,24},{1,5},{5... | collective-permute-start | bytes 3145736 | tf_op jit(solution)/shard_map/ppermute | solution.py:306
  35.6 2.6 %copy-start.13 = (bf16[64,2048]{1,0:T(8,128)(2,1)}, bf16[64,2048]{1,0:T(8,128)(2,1)S(1)}, u32[]{:S(2)}) copy-start(bf16[64,2048]{1,0:T(8,128)(2,1)S(1)} %collective-permute-done.2.refs_5_) | copy-start | bytes 786436
  35.6 4.3 %copy-start.7 = (bf16[256,2048]{1,0:T(8,128)(2,1)}, bf16[256,2048]{1,0:T(8,128)(2,1)S(1)}, u32[]{:S(2)}) copy-start(bf16[256,2048]{1,0:T(8,128)(2,1)S(1)} %collective-permute-done.4.refs_10_.refs_8_.refs_4_) | copy-start | bytes 3145732
  35.6 4.3 %collective-permute-start.7 = (bf16[256,2048]{1,0:T(8,128)(2,1)S(1)}, bf16[256,2048]{1,0:T(8,128)(2,1)}, u32[]{:S(2)}, u32[]{:S(2)}) collective-permute-start(bf16[256,2048]{1,0:T(8,128)(2,1)S(1)} %collective-permute-done.4.refs_10_.refs_8_.refs_4_), channel_id=1, source_target_pairs={{0,4},{4,0},{8,12},{12,8},{16,20},{20,16},{24,28},{28,24},{1,5},{5... | collective-permute-start | bytes 3145736 | tf_op jit(solution)/shard_map/ppermute | solution.py:306
  36.2 13.2 %collective-permute-start.8 = (bf16[64,2048]{1,0:T(8,128)(2,1)S(1)}, bf16[64,2048]{1,0:T(8,128)(2,1)}, u32[]{:S(2)}, u32[]{:S(2)}) collective-permute-start(bf16[64,2048]{1,0:T(8,128)(2,1)S(1)} %copy-done.1), channel_id=1, source_target_pairs={{0,1},{1,0},{2,3},{3,2},{4,5},{5,4},{6,7},{7,6},{8,9},{9,8},{10,11... | collective-permute-start | bytes 786440 | tf_op jit(solution)/shard_map/ppermute | solution.py:306
  36.2 14.0 %collective-permute-start.9 = (bf16[64,2048]{1,0:T(8,128)(2,1)}, bf16[64,2048]{1,0:T(8,128)(2,1)}, u32[]{:S(2)}, u32[]{:S(2)}) collective-permute-start(bf16[64,2048]{1,0:T(8,128)(2,1)} %collective-permute-done.5.refs_4_.refs_14_), channel_id=1, source_target_pairs={{0,1},{1,0},{2,3},{3,2},{4,5},{5,4},{6,7},{7,6},{8,9},{9,8},{10,11... | collective-permute-start | bytes 786440 | tf_op jit(solution)/shard_map/ppermute | solution.py:306
  38.8 1.1 %copy-start.8 = (bf16[256,2048]{1,0:T(8,128)(2,1)}, bf16[256,2048]{1,0:T(8,128)(2,1)S(1)}, u32[]{:S(2)}) copy-start(bf16[256,2048]{1,0:T(8,128)(2,1)S(1)} %collective-permute-done.6.refs_11_.refs_9_.refs_5_) | copy-start | bytes 3145732
  50.2 3.6 %collective-permute-start.10 = (f32[1,320]{1,0:T(1,128)S(1)}, f32[1,320]{1,0:T(1,128)S(1)}, u32[]{:S(2)}, u32[]{:S(2)}) collective-permute-start(f32[1,320]{1,0:T(1,128)S(1)} %get-tuple-element.50), channel_id=1, source_target_pairs={{0,1},{1,0},{2,3},{3,2},{4,5},{5,4},{6,7},{7,6},{8,9},{9,8},{10,11... | collective-permute-start | bytes 3848 | tf_op jit(solution)/shard_map/ppermute | solution.py:306
  54.0 7.9 %collective-permute-start.11 = (bf16[64,2048]{1,0:T(8,128)(2,1)}, bf16[64,2048]{1,0:T(8,128)(2,1)S(1)}, u32[]{:S(2)}, u32[]{:S(2)}) collective-permute-start(bf16[64,2048]{1,0:T(8,128)(2,1)} %get-tuple-element.51), channel_id=1, source_target_pairs={{0,1},{1,0},{2,3},{3,2},{4,5},{5,4},{6,7},{7,6},{8,9},{9,8},{10,11... | collective-permute-start | bytes 786440 | tf_op jit(solution)/shard_map/ppermute | solution.py:306
  54.4 7.5 %copy-start.12 = (bf16[64,2048]{1,0:T(8,128)(2,1)S(1)}, bf16[64,2048]{1,0:T(8,128)(2,1)}, u32[]{:S(2)}) copy-start(bf16[64,2048]{1,0:T(8,128)(2,1)} %get-tuple-element.55) | copy-start | bytes 786436
  54.4 8.0 %copy-start.16 = (bf16[64,2048]{1,0:T(8,128)(2,1)S(1)}, bf16[64,2048]{1,0:T(8,128)(2,1)}, u32[]{:S(2)}) copy-start(bf16[64,2048]{1,0:T(8,128)(2,1)} %get-tuple-element.54) | copy-start | bytes 786436
  54.4 12.9 %copy-start.15 = (f32[128]{0:T(128)S(1)}, f32[128]{0:T(128)}, u32[]{:S(2)}) copy-start(f32[128]{0:T(128)} %param.15) | copy-start | bytes 1540
  54.4 7.3 %collective-permute-start.13 = (f32[1,384]{1,0:T(1,128)S(1)}, f32[1,384]{1,0:T(1,128)S(1)}, u32[]{:S(2)}, u32[]{:S(2)}) collective-permute-start(f32[1,384]{1,0:T(1,128)S(1)} %pad_maximum_fusion.3), channel_id=1, source_target_pairs={{0,2},{1,3},{2,0},{3,1},{4,6},{5,7},{6,4},{7,5},{8,10},{9,11},{10,... | collective-permute-start | bytes 4616 | tf_op jit(solution)/shard_map/ppermute | solution.py:306
  62.0 12.6 %collective-permute-start.14 = (bf16[64,2048]{1,0:T(8,128)(2,1)S(1)}, bf16[64,2048]{1,0:T(8,128)(2,1)S(1)}, u32[]{:S(2)}, u32[]{:S(2)}) collective-permute-start(bf16[64,2048]{1,0:T(8,128)(2,1)S(1)} %add_convert_fusion.4), channel_id=1, source_target_pairs={{0,2},{1,3},{2,0},{3,1},{4,6},{5,7},{6,4},{7,5},{8,10},{9,11},{10,... | collective-permute-start | bytes 786440 | tf_op jit(solution)/shard_map/ppermute | solution.py:306
  62.4 12.2 %collective-permute-start.12 = (bf16[64,2048]{1,0:T(8,128)(2,1)S(1)}, bf16[64,2048]{1,0:T(8,128)(2,1)S(1)}, u32[]{:S(2)}, u32[]{:S(2)}) collective-permute-start(bf16[64,2048]{1,0:T(8,128)(2,1)S(1)} %copy-done.16), channel_id=1, source_target_pairs={{0,1},{1,0},{2,3},{3,2},{4,5},{5,4},{6,7},{7,6},{8,9},{9,8},{10,11... | collective-permute-start | bytes 786440 | tf_op jit(solution)/shard_map/ppermute | solution.py:306
  64.1 3.3 %collective-permute-start.16 = (f32[1,512]{1,0:T(1,128)S(1)}, f32[1,512]{1,0:T(1,128)S(1)}, u32[]{:S(2)}, u32[]{:S(2)}) collective-permute-start(f32[1,512]{1,0:T(1,128)S(1)} %pad_maximum_fusion.2.refs_2_), channel_id=1, source_target_pairs={{4,8},{12,16},{20,24},{8,4},{16,12},{24,20},{5,9},{13,17},{21,25},... | collective-permute-start | bytes 6152 | tf_op jit(solution)/shard_map/ppermute | solution.py:473
  64.8 3.3 %collective-permute-start.15 = (f32[1,512]{1,0:T(1,128)S(1)}, f32[1,512]{1,0:T(1,128)S(1)}, u32[]{:S(2)}, u32[]{:S(2)}) collective-permute-start(f32[1,512]{1,0:T(1,128)S(1)} %pad_maximum_fusion.2.refs_2_), channel_id=1, source_target_pairs={{0,4},{4,0},{8,12},{12,8},{16,20},{20,16},{24,28},{28,24},{1,5},{5... | collective-permute-start | bytes 6152 | tf_op jit(solution)/shard_map/ppermute | solution.py:306
  74.6 4.9 %collective-permute-start.20 = (bf16[512,2048]{1,0:T(8,128)(2,1)S(1)}, bf16[512,2048]{1,0:T(8,128)(2,1)S(1)}, u32[]{:S(2)}, u32[]{:S(2)}) collective-permute-start(bf16[512,2048]{1,0:T(8,128)(2,1)S(1)} %get-tuple-element.73), channel_id=1, source_target_pairs={{0,4},{4,0},{8,12},{12,8},{16,20},{20,16},{24,28},{28,24},{1,5},{5... | collective-permute-start | bytes 6291464 | tf_op jit(solution)/shard_map/ppermute | solution.py:306
  79.9 16.7 %copy-start = (bf16[64,2048]{1,0:T(8,128)(2,1)S(1)}, bf16[64,2048]{1,0:T(8,128)(2,1)}, u32[]{:S(2)}) copy-start(bf16[64,2048]{1,0:T(8,128)(2,1)} %x_ref.1) | copy-start | bytes 786436
  79.9 16.7 %copy-start.9 = (bf16[64,2048]{1,0:T(8,128)(2,1)S(1)}, bf16[64,2048]{1,0:T(8,128)(2,1)}, u32[]{:S(2)}) copy-start(bf16[64,2048]{1,0:T(8,128)(2,1)} %get-tuple-element.44) | copy-start | bytes 786436
  79.9 14.9 %collective-permute-start.21 = (bf16[256,2048]{1,0:T(8,128)(2,1)S(1)}, bf16[256,2048]{1,0:T(8,128)(2,1)S(1)}, u32[]{:S(2)}, u32[]{:S(2)}) collective-permute-start(bf16[256,2048]{1,0:T(8,128)(2,1)S(1)} %add_convert_fusion), channel_id=1, source_target_pairs={{0,8},{4,20},{8,0},{12,28},{16,24},{20,4},{24,16},{28,12},{1,9},{5... | collective-permute-start | bytes 3145736 | tf_op jit(solution)/shard_map/ppermute | solution.py:311
  81.3 8.6 %collective-permute-start.17 = (bf16[64,2048]{1,0:T(8,128)(2,1)S(1)}, bf16[64,2048]{1,0:T(8,128)(2,1)S(1)}, u32[]{:S(2)}, u32[]{:S(2)}) collective-permute-start(bf16[64,2048]{1,0:T(8,128)(2,1)S(1)} %get-tuple-element.67), channel_id=1, source_target_pairs={{0,1},{1,0},{2,3},{3,2},{4,5},{5,4},{6,7},{7,6},{8,9},{9,8},{10,11... | collective-permute-start | bytes 786440 | tf_op jit(solution)/shard_map/ppermute | solution.py:306
  89.9 13.0 %collective-permute-start.18 = (bf16[64,2048]{1,0:T(8,128)(2,1)S(1)}, bf16[64,2048]{1,0:T(8,128)(2,1)S(1)}, u32[]{:S(2)}, u32[]{:S(2)}) collective-permute-start(bf16[64,2048]{1,0:T(8,128)(2,1)S(1)} %get-tuple-element.68), channel_id=1, source_target_pairs={{0,1},{1,0},{2,3},{3,2},{4,5},{5,4},{6,7},{7,6},{8,9},{9,8},{10,11... | collective-permute-start | bytes 786440 | tf_op jit(solution)/shard_map/ppermute | solution.py:306
  90.4 15.3 %collective-permute-start.19 = (bf16[64,2048]{1,0:T(8,128)(2,1)S(1)}, bf16[64,2048]{1,0:T(8,128)(2,1)S(1)}, u32[]{:S(2)}, u32[]{:S(2)}) collective-permute-start(bf16[64,2048]{1,0:T(8,128)(2,1)S(1)} %add_convert_fusion.2), channel_id=1, source_target_pairs={{0,2},{1,3},{2,0},{3,1},{4,6},{5,7},{6,4},{7,5},{8,10},{9,11},{10,... | collective-permute-start | bytes 786440 | tf_op jit(solution)/shard_map/ppermute | solution.py:306
  95.0 9.2 %collective-permute-start.22 = (bf16[128,2048]{1,0:T(8,128)(2,1)S(1)}, bf16[128,2048]{1,0:T(8,128)(2,1)S(1)}, u32[]{:S(2)}, u32[]{:S(2)}) collective-permute-start(bf16[128,2048]{1,0:T(8,128)(2,1)S(1)} %add_convert_fusion.1), channel_id=1, source_target_pairs={{0,16},{4,12},{8,24},{12,4},{16,0},{20,28},{24,8},{28,20},{1,17},{... | collective-permute-start | bytes 1572872 | tf_op jit(solution)/shard_map/ppermute | solution.py:311
  103.0 2.6 %copy-start.2 = (bf16[64,2048]{1,0:T(8,128)(2,1)S(1)}, bf16[64,2048]{1,0:T(8,128)(2,1)}, u32[]{:S(2)}) copy-start(bf16[64,2048]{1,0:T(8,128)(2,1)} %upstream.1) | copy-start | bytes 786436

commit v5 on v4

--- a/solution.py
+++ b/solution.py
@@ -301,6 +301,21 @@
     )(*[pltpu.with_memory_space_constraint(a, pltpu.HBM) if m is HBM else a for m, a in args])
 
 
+def stack_kernel(*refs):
+    at = 0
+    for p in refs[:-1]:
+        refs[-1][at : at + p.shape[0]] = p[...]
+        at += p.shape[0]
+
+
+def stack(parts):
+    rows = sum(p.shape[0] for p in parts)
+    whole = jax.ShapeDtypeStruct((rows,) + parts[0].shape[1:], parts[0].dtype)
+    return call(
+        stack_kernel, [(VM, whole)], [(VM, p) for p in parts], [], 0
+    )[0]
+
+
 def swap(value, axis, mask):
     n = lax.axis_size(axis)
     return lax.ppermute(value, axis, [(i, i ^ mask) for i in range(n)])
@@ -318,9 +333,14 @@
 def gather_tok(w_in, w_out, bits, ties):
     held, masks = [w_in, w_out], [[(0, 0)]]
     for step, (even, odd) in enumerate(zip(bits, bits[::-1])):
-        whole = jnp.concatenate(held, axis=0)
+        if step == 0 and len(bits) > 1:
+            own = stack(held)
+            held = [own] + [swap_tok(after(h, own), even, odd) for h in held]
+            masks = [[(0, 0), (even, odd)]]
+            continue
         if step == len(bits) - 1:
-            whole = after(whole, *ties[0])
+            held = [after(held[0], *ties[0])] + held[1:]
+        whole = stack(held)
         flat = [m for ms in masks for m in ms]
         held = [whole, swap_tok(whole, even, odd)]
         masks = [flat, [(a ^ even, b ^ odd) for a, b in flat]]

time: 107 us -> 105 us (0.981)
  waiting for transfers between devices: 44 us -> 38.2 us
  starting transfers between devices: 30 us -> 34.2 us
  other arithmetic: 4.36 us -> 2.13 us
  local copies, waits for them, and re-layouts: 1.56 us -> 3.46 us
    ppermute x4 -> x5, waiting for transfers between devices: 6.01 us -> 1.5 us  [swap_tok(): lax.ppermute(value, 'tok', [(i, i ^ (odd if i & 1 else even)) for i in ra...]
    ppermute x18, starting transfers between devices: 22.9 us -> 25.5 us  [swap(): return lax.ppermute(value, axis, [(i, i ^ mask) for i in range(n)])]
    concatenate x2 -> x0, other arithmetic: 2.23 us -> none  [gather_tok(): whole = jnp.concatenate(held, axis=0)]
    unnamed x35 -> x39, local copies, waits for them, and re-layouts: 0.16 us -> 2.06 us
    ppermute x4 -> x5, starting transfers between devices: 6.43 us -> 8.05 us  [swap_tok(): lax.ppermute(value, 'tok', [(i, i ^ (odd if i & 1 else even)) for i in ra...]
    ppermute x18, waiting for transfers between devices: 38 us -> 36.7 us  [swap(): return lax.ppermute(value, axis, [(i, i ^ mask) for i in range(n)])]
    pallas_call x5 -> x7, Pallas kernels: 25.9 us -> 26 us  [call(): pl.pallas_call(body, out_shape=[pltpu.HBM(o.shape, o.dtype) if m is HBM e...]
  transfers between devices with their start and end apart: 23 -> 24, of which waited for: 13 -> 13; matrix products, arithmetic and copies ran while one was open for 4% -> 3% of each run, Pallas kernels for 23% -> 24%
where the time goes in v5:
time: 105 us
  waiting for transfers between devices  38.2 us (36%)
  starting transfers between devices  34.2 us (33%)
  Pallas kernels  26 us (25%)
  local copies, waits for them, and re-layouts  3.46 us (3%)
  other arithmetic  2.13 us (2%)
    ppermute x18, waiting for transfers between devices, swap(): return lax.ppermute(value, axis, [(i, i ^ mask) for i in range(n)])  36.7 us
    pallas_call x7, Pallas kernels, call(): pl.pallas_call(body, out_shape=[pltpu.HBM(o.shape, o.dtype) if m is HBM e...  26 us
    ppermute x18, starting transfers between devices, swap(): return lax.ppermute(value, axis, [(i, i ^ mask) for i in range(n)])  25.5 us
    ppermute x5, starting transfers between devices, swap_tok(): lax.ppermute(value, 'tok', [(i, i ^ (odd if i & 1 else even)) for i in ra...  8.05 us
  transfers between devices with their start and end apart: 24, of which 13 were waited for; matrix products, arithmetic and copies ran while one was open for 3% of the time, Pallas kernels for 24%

profile of v5, /device:TPU:0, one launch (start us, length us, event | category | flops | bytes accessed | tf_op | source)
XLA Modules:
  0.0 104.9 jit_solution(14207922292525416537)
XLA Ops:
  0.6 0.0 copy-start.2
  0.6 4.1 %collective-permute-start.1 = (bf16[64,2048]{1,0:T(8,128)(2,1)}, bf16[64,2048]{1,0:T(8,128)(2,1)S(1)}, u32[]{:S(2)}, u32[]{:S(2)}) collective-permute-start(bf16[64,2048]{1,0:T(8,128)(2,1)} %x_ref.1), channel_id=1, source_target_pairs={{0,2},{1,3},{2,0},{3,1},{4,6},{5,7},{6,4},{7,5},{8,10},{9,11},{10,... | collective-permute-start | bytes 786440 | tf_op jit(solution)/shard_map/ppermute | solution.py:321
  4.7 1.6 %collective-permute-start = (bf16[64,2048]{1,0:T(8,128)(2,1)}, bf16[64,2048]{1,0:T(8,128)(2,1)S(1)}, u32[]{:S(2)}, u32[]{:S(2)}) collective-permute-start(bf16[64,2048]{1,0:T(8,128)(2,1)} %x_ref.1), channel_id=1, source_target_pairs={{0,1},{1,0},{2,3},{3,2},{4,5},{5,4},{6,7},{7,6},{8,9},{9,8},{10,11... | collective-permute-start | bytes 786440 | tf_op jit(solution)/shard_map/ppermute | solution.py:321
  6.3 0.9 copy-done.4
  7.3 0.9 copy-done.5
  8.3 1.6 %collective-permute-start.3 = (bf16[64,2048]{1,0:T(8,128)(2,1)S(1)}, bf16[64,2048]{1,0:T(8,128)(2,1)S(1)}, u32[]{:S(2)}, u32[]{:S(2)}) collective-permute-start(bf16[64,2048]{1,0:T(8,128)(2,1)S(1)} %copy-done.4), channel_id=1, source_target_pairs={{0,8},{4,20},{8,0},{12,28},{16,24},{20,4},{24,16},{28,12},{1,9},{5... | collective-permute-start | bytes 786440 | tf_op jit(solution)/shard_map/ppermute | solution.py:326
  9.8 0.5 collective-permute-start.4
  10.4 6.6 %collective-permute-done.1.refs_4_ = bf16[64,2048]{1,0:T(8,128)(2,1)S(1)} collective-permute-done((bf16[64,2048]{1,0:T(8,128)(2,1)}, bf16[64,2048]{1,0:T(8,128)(2,1)S(1)}, u32[]{:S(2)}, u32[]{:S(2)}) %collective-permute-start.1) | collective-permute-done | bytes 262176 | tf_op jit(solution)/shard_map/ppermute | solution.py:321
  17.0 0.2 collective-permute-done.refs_3_
  17.2 0.3 collective-permute-done.4.refs_2_
  17.5 0.1 shard_map.121.refs_9_.refs_7_.refs_3_
  17.6 1.6 %collective-permute-start.5 = (bf16[256,2048]{1,0:T(8,128)(2,1)S(1)}, bf16[256,2048]{1,0:T(8,128)(2,1)S(1)}, u32[]{:S(2)}, u32[]{:S(2)}) collective-permute-start(bf16[256,2048]{1,0:T(8,128)(2,1)S(1)} %shard_map.121.refs_9_.refs_7_.refs_3_), channel_id=1, source_target_pairs={{0,16},{4,12},{8,24},{12,4},{16,0},{20,28},{24,8},{28,20},{1,17},{... | collective-permute-start | bytes 3145736 | tf_op jit(solution)/shard_map/ppermute | solution.py:326
  19.2 1.0 collective-permute-start.6
  20.2 2.4 %collective-permute-start.2 = (bf16[64,2048]{1,0:T(8,128)(2,1)S(1)}, bf16[64,2048]{1,0:T(8,128)(2,1)S(1)}, u32[]{:S(2)}, u32[]{:S(2)}) collective-permute-start(bf16[64,2048]{1,0:T(8,128)(2,1)S(1)} %collective-permute-done.1.refs_4_), channel_id=1, source_target_pairs={{0,1},{1,0},{2,3},{3,2},{4,5},{5,4},{6,7},{7,6},{8,9},{9,8},{10,11... | collective-permute-start | bytes 786440 | tf_op jit(solution)/shard_map/ppermute | solution.py:321
  22.7 9.6 %collective-permute-done.6.refs_4_.refs_14_ = bf16[64,2048]{1,0:T(8,128)(2,1)} collective-permute-done((bf16[64,2048]{1,0:T(8,128)(2,1)S(1)}, bf16[64,2048]{1,0:T(8,128)(2,1)}, u32[]{:S(2)}, u32[]{:S(2)}) %collective-permute-start.6) | collective-permute-done | bytes 262176 | tf_op jit(solution)/shard_map/ppermute | solution.py:321
  32.3 0.0 collective-permute-start.7
  32.3 0.0 collective-permute-done.2.refs_5_
  32.3 0.2 collective-permute-done.5.refs_10_.refs_8_.refs_4_
  32.5 0.4 collective-permute-start.8
  32.9 0.7 collective-permute-start.9
  33.6 1.3 %collective-permute-start.10 = (bf16[64,2048]{1,0:T(8,128)(2,1)}, bf16[64,2048]{1,0:T(8,128)(2,1)}, u32[]{:S(2)}, u32[]{:S(2)}) collective-permute-start(bf16[64,2048]{1,0:T(8,128)(2,1)} %collective-permute-done.6.refs_4_.refs_14_), channel_id=1, source_target_pairs={{0,1},{1,0},{2,3},{3,2},{4,5},{5,4},{6,7},{7,6},{8,9},{9,8},{10,11... | collective-permute-start | bytes 786440 | tf_op jit(solution)/shard_map/ppermute | solution.py:321
  34.9 0.1 copy.13.refs_0_
  35.0 1.6 %collective-permute-done.8.refs_12_.refs_10_.refs_6_ = bf16[256,2048]{1,0:T(8,128)(2,1)} collective-permute-done((bf16[256,2048]{1,0:T(8,128)(2,1)S(1)}, bf16[256,2048]{1,0:T(8,128)(2,1)}, u32[]{:S(2)}, u32[]{:S(2)}) %collective-permute-start.8) | collective-permute-done | bytes 1048608 | tf_op jit(solution)/shard_map/ppermute | solution.py:321
  36.6 9.4 %shard_map.122 = (bf16[16,256,128]{2,1,0:T(8,128)(2,1)}, bf16[16,256,128]{2,1,0:T(8,128)(2,1)}, bf16[16,256,128]{2,1,0:T(8,128)(2,1)}, f32[1,320]{1,0:T(1,128)S(...) custom-call(s32[16,4]{1,0:T(8,128)S(1)} %copy.13.refs_0_, ...), custom_call_target="tpu_custom_call" | custom-call | flops 1073741824 | bytes 4195584 | tf_op jit(solution)/shard_map/pallas_call | solution.py:289
  46.1 0.9 collective-permute-done.10.refs_5_.refs_15_
  46.9 1.2 %collective-permute-start.11 = (f32[1,320]{1,0:T(1,128)S(1)}, f32[1,320]{1,0:T(1,128)S(1)}, u32[]{:S(2)}, u32[]{:S(2)}) collective-permute-start(f32[1,320]{1,0:T(1,128)S(1)} %get-tuple-element.54), channel_id=1, source_target_pairs={{0,1},{1,0},{2,3},{3,2},{4,5},{5,4},{6,7},{7,6},{8,9},{9,8},{10,11... | collective-permute-start | bytes 3848 | tf_op jit(solution)/shard_map/ppermute | solution.py:321
  48.1 2.4 %collective-permute-done.11 = f32[1,320]{1,0:T(1,128)S(1)} collective-permute-done((f32[1,320]{1,0:T(1,128)S(1)}, f32[1,320]{1,0:T(1,128)S(1)}, u32[]{:S(2)}, u32[]{:S(2)}) %collective-permute-start.11) | collective-permute-done | bytes 1312 | tf_op jit(solution)/shard_map/ppermute | solution.py:321
  50.5 0.1 reshape.39
  50.6 0.1 reshape.40
  50.7 1.2 %collective-permute-start.12 = (bf16[64,2048]{1,0:T(8,128)(2,1)}, bf16[64,2048]{1,0:T(8,128)(2,1)S(1)}, u32[]{:S(2)}, u32[]{:S(2)}) collective-permute-start(bf16[64,2048]{1,0:T(8,128)(2,1)} %get-tuple-element.55), channel_id=1, source_target_pairs={{0,1},{1,0},{2,3},{3,2},{4,5},{5,4},{6,7},{7,6},{8,9},{9,8},{10,11... | collective-permute-start | bytes 786440 | tf_op jit(solution)/shard_map/ppermute | solution.py:321
  51.9 0.1 pad_maximum_fusion.1
  52.0 2.7 %collective-permute-start.14 = (f32[1,384]{1,0:T(1,128)S(1)}, f32[1,384]{1,0:T(1,128)S(1)}, u32[]{:S(2)}, u32[]{:S(2)}) collective-permute-start(f32[1,384]{1,0:T(1,128)S(1)} %pad_maximum_fusion.1), channel_id=1, source_target_pairs={{0,2},{1,3},{2,0},{3,1},{4,6},{5,7},{6,4},{7,5},{8,10},{9,11},{10,... | collective-permute-start | bytes 4616 | tf_op jit(solution)/shard_map/ppermute | solution.py:321
  54.7 4.7 %shard_map.123 = (bf16[16,256,128]{2,1,0:T(8,128)(2,1)}, f32[1,2048]{1,0:T(1,128)S(1)}) custom-call(s32[16,4]{1,0:T(8,128)S(1)} %copy.13.refs_0_, s32[1]{0:T(128)} %bitcast.refs_1_, bf16[64,2048]{1,0:T(8,128)(2,1)} %upstream.1, bf16[64,2048]{1,0:T(8,128)(2,1)} %collective-permute-done.9.refs_3_.refs_13_, ...), custom_call_target="tpu_custom_call" | custom-call | flops 536870912 | bytes 1056768 | tf_op jit(solution)/shard_map/pallas_call | solution.py:289
  59.5 0.1 pad_maximum_fusion.refs_2_
  59.6 0.1 add_convert_fusion.4
  59.6 0.4 collective-permute-start.15
  60.1 1.6 %collective-permute-start.13 = (bf16[64,2048]{1,0:T(8,128)(2,1)S(1)}, bf16[64,2048]{1,0:T(8,128)(2,1)S(1)}, u32[]{:S(2)}, u32[]{:S(2)}) collective-permute-start(bf16[64,2048]{1,0:T(8,128)(2,1)S(1)} %copy-done.18), channel_id=1, source_target_pairs={{0,1},{1,0},{2,3},{3,2},{4,5},{5,4},{6,7},{7,6},{8,9},{9,8},{10,11... | collective-permute-start | bytes 786440 | tf_op jit(solution)/shard_map/ppermute | solution.py:321
  61.7 0.6 collective-permute-start.17
  62.3 2.7 %collective-permute-start.16 = (f32[1,512]{1,0:T(1,128)S(1)}, f32[1,512]{1,0:T(1,128)S(1)}, u32[]{:S(2)}, u32[]{:S(2)}) collective-permute-start(f32[1,512]{1,0:T(1,128)S(1)} %pad_maximum_fusion.refs_2_), channel_id=1, source_target_pairs={{0,4},{4,0},{8,12},{12,8},{16,20},{20,16},{24,28},{28,24},{1,5},{5... | collective-permute-start | bytes 6152 | tf_op jit(solution)/shard_map/ppermute | solution.py:321
  65.0 0.1 copy.16.refs_5_
  65.1 0.7 collective-permute-done.16.refs_3_
  65.8 6.5 %shard_map.124 = (f32[64,128]{1,0:T(8,128)S(1)}, bf16[16,256,128]{2,1,0:T(8,128)(2,1)S(1)}, bf16[512,2048]{1,0:T(8,128)(2,1)S(1)}, bf16[512,2048]{1,0:T(8,128)(2,1)S(1)}) custom-call(s32[16,4]{1,0:T(8,128)S(1)} %copy.13.refs_0_, s32[1]{0:T(128)} %bitcast.refs_1_, f32[1,512]{1,0:T(1,128)S(1)} %pad_maximum_fusion.refs_2_, ...), custom_call_target="tpu_custom_call" | custom-call | flops 1073741824 | bytes 5275648 | tf_op jit(solution)/shard_map/pallas_call | solution.py:289
  72.3 0.7 collective-permute-start.21
  73.1 4.2 %shard_map.125 = (bf16[64,2048]{1,0:T(8,128)(2,1)S(1)}, bf16[64,2048]{1,0:T(8,128)(2,1)S(1)}, bf16[64,2048]{1,0:T(8,128)(2,1)S(1)}, bf16[64,2048]{1,0:T(8,128)(2,1)S(1)}) custom-call(s32[16,4]{1,0:T(8,128)S(1)} %copy.13.refs_0_, s32[1]{0:T(128)} %bitcast.refs_1_, bf16[16,256,128]{2,1,0:T(8,128)(2,1)S(1)} %get-tuple-element.68.refs_2_, ...), custom_call_target="tpu_custom_call" | custom-call | flops 536870912 | bytes 1048576 | tf_op jit(solution)/shard_map/pallas_call | solution.py:289
  77.2 0.4 add_convert_fusion
  77.6 0.0 copy-start.1
  77.6 0.0 copy-start.11
  77.6 1.8 %collective-permute-start.22 = (bf16[256,2048]{1,0:T(8,128)(2,1)S(1)}, bf16[256,2048]{1,0:T(8,128)(2,1)S(1)}, u32[]{:S(2)}, u32[]{:S(2)}) collective-permute-start(bf16[256,2048]{1,0:T(8,128)(2,1)S(1)} %add_convert_fusion), channel_id=1, source_target_pairs={{0,8},{4,20},{8,0},{12,28},{16,24},{20,4},{24,16},{28,12},{1,9},{5... | collective-permute-start | bytes 3145736 | tf_op jit(solution)/shard_map/ppermute | solution.py:326
  79.4 0.4 collective-permute-start.18
  79.9 8.7 %collective-permute-done.18 = bf16[64,2048]{1,0:T(8,128)(2,1)S(1)} collective-permute-done((bf16[64,2048]{1,0:T(8,128)(2,1)S(1)}, bf16[64,2048]{1,0:T(8,128)(2,1)S(1)}, u32[]{:S(2)}, u32[]{:S(2)}) %collective-permute-start.18) | collective-permute-done | bytes 262176 | tf_op jit(solution)/shard_map/ppermute | solution.py:321
  88.6 0.4 collective-permute-start.19
  89.0 0.1 add_convert_fusion.2
  89.1 2.6 %collective-permute-start.20 = (bf16[64,2048]{1,0:T(8,128)(2,1)S(1)}, bf16[64,2048]{1,0:T(8,128)(2,1)S(1)}, u32[]{:S(2)}, u32[]{:S(2)}) collective-permute-start(bf16[64,2048]{1,0:T(8,128)(2,1)S(1)} %add_convert_fusion.2), channel_id=1, source_target_pairs={{0,2},{1,3},{2,0},{3,1},{4,6},{5,7},{6,4},{7,5},{8,10},{9,11},{10,... | collective-permute-start | bytes 786440 | tf_op jit(solution)/shard_map/ppermute | solution.py:321
  91.7 0.8 collective-permute-done.22
  92.5 0.2 add_convert_fusion.1
  92.8 2.6 %collective-permute-start.23 = (bf16[128,2048]{1,0:T(8,128)(2,1)S(1)}, bf16[128,2048]{1,0:T(8,128)(2,1)S(1)}, u32[]{:S(2)}, u32[]{:S(2)}) collective-permute-start(bf16[128,2048]{1,0:T(8,128)(2,1)S(1)} %add_convert_fusion.1), channel_id=1, source_target_pairs={{0,16},{4,12},{8,24},{12,4},{16,0},{20,28},{24,8},{28,20},{1,17},{... | collective-permute-start | bytes 1572872 | tf_op jit(solution)/shard_map/ppermute | solution.py:326
  95.3 0.8 add_convert_fusion.3
  96.2 6.0 %collective-permute-done.19 = bf16[64,2048]{1,0:T(8,128)(2,1)S(1)} collective-permute-done((bf16[64,2048]{1,0:T(8,128)(2,1)S(1)}, bf16[64,2048]{1,0:T(8,128)(2,1)S(1)}, u32[]{:S(2)}, u32[]{:S(2)}) %collective-permute-start.19) | collective-permute-done | bytes 262176 | tf_op jit(solution)/shard_map/ppermute | solution.py:321
  102.2 0.1 convert_add_fusion.1.own
  102.3 0.0 copy-start.3
  102.3 0.2 collective-permute-done.23
  102.5 0.3 convert_add_fusion
  102.8 1.0 fusion
  103.9 1.1 %shard_map.126 = bf16[64,2048]{1,0:T(8,128)(2,1)} custom-call(bf16[64,2048]{1,0:T(8,128)(2,1)S(1)} %copy-done.1, f32[1,2048]{1,0:T(1,128)S(1)} %bitcast.12, bf16[64,2048]{1,0:T(8,128)(2,1)S(1)} %copy-done.3, f32[1,2048]{1,0:T(1,128)S(1)} %bitcast.10, f32[64,128]{1,0:T(8,128)S(1)} %get-tuple-element.66.own_coeff, f32[64,2048]{1,0:T(8,128)S(1)} %convert_add_fusion.1.own, ...), custom_call_target="tpu_custom_call" | custom-call | flops 131072 | bytes 262144 | tf_op jit(solution)/shard_map/pallas_call | solution.py:289
  (52 shorter events, 0.2 us)
Async XLA Ops:
  0.6 18.6 %copy-start.2 = (bf16[64,2048]{1,0:T(8,128)(2,1)S(1)}, bf16[64,2048]{1,0:T(8,128)(2,1)}, u32[]{:S(2)}) copy-start(bf16[64,2048]{1,0:T(8,128)(2,1)} %upstream.1) | copy-start | bytes 786436
  0.6 16.3 %collective-permute-start.1 = (bf16[64,2048]{1,0:T(8,128)(2,1)}, bf16[64,2048]{1,0:T(8,128)(2,1)S(1)}, u32[]{:S(2)}, u32[]{:S(2)}) collective-permute-start(bf16[64,2048]{1,0:T(8,128)(2,1)} %x_ref.1), channel_id=1, source_target_pairs={{0,2},{1,3},{2,0},{3,1},{4,6},{5,7},{6,4},{7,5},{8,10},{9,11},{10,... | collective-permute-start | bytes 786440 | tf_op jit(solution)/shard_map/ppermute | solution.py:321
  4.7 12.4 %collective-permute-start = (bf16[64,2048]{1,0:T(8,128)(2,1)}, bf16[64,2048]{1,0:T(8,128)(2,1)S(1)}, u32[]{:S(2)}, u32[]{:S(2)}) collective-permute-start(bf16[64,2048]{1,0:T(8,128)(2,1)} %x_ref.1), channel_id=1, source_target_pairs={{0,1},{1,0},{2,3},{3,2},{4,5},{5,4},{6,7},{7,6},{8,9},{9,8},{10,11... | collective-permute-start | bytes 786440 | tf_op jit(solution)/shard_map/ppermute | solution.py:321
  6.3 0.9 copy-start.4
  7.3 0.9 copy-start.5
  8.2 26.7 %copy-start.16 = (s32[16,4]{0,1:T(4,128)S(1)}, s32[16,4]{0,1:T(4,128)}, u32[]{:S(2)}) copy-start(s32[16,4]{0,1:T(4,128)} %param.13) | copy-start | bytes 772
  8.2 28.4 %copy-start.6 = (f32[2048]{0:T(1024)S(1)}, f32[2048]{0:T(1024)}, u32[]{:S(2)}) copy-start(f32[2048]{0:T(1024)} %param.17) | copy-start | bytes 24580
  8.2 28.4 %copy-start.7 = (f32[2048]{0:T(1024)S(1)}, f32[2048]{0:T(1024)}, u32[]{:S(2)}) copy-start(f32[2048]{0:T(1024)} %param.10) | copy-start | bytes 24580
  8.2 28.4 %copy-start.8 = (s32[64]{0:T(128)S(1)}, s32[64]{0:T(128)}, u32[]{:S(2)}) copy-start(s32[64]{0:T(128)} %param.14) | copy-start | bytes 772
  8.3 8.9 %collective-permute-start.3 = (bf16[64,2048]{1,0:T(8,128)(2,1)S(1)}, bf16[64,2048]{1,0:T(8,128)(2,1)S(1)}, u32[]{:S(2)}, u32[]{:S(2)}) collective-permute-start(bf16[64,2048]{1,0:T(8,128)(2,1)S(1)} %copy-done.4), channel_id=1, source_target_pairs={{0,8},{4,20},{8,0},{12,28},{16,24},{20,4},{24,16},{28,12},{1,9},{5... | collective-permute-start | bytes 786440 | tf_op jit(solution)/shard_map/ppermute | solution.py:326
  9.8 7.7 %collective-permute-start.4 = (bf16[64,2048]{1,0:T(8,128)(2,1)S(1)}, bf16[64,2048]{1,0:T(8,128)(2,1)S(1)}, u32[]{:S(2)}, u32[]{:S(2)}) collective-permute-start(bf16[64,2048]{1,0:T(8,128)(2,1)S(1)} %copy-done.5), channel_id=1, source_target_pairs={{0,8},{4,20},{8,0},{12,28},{16,24},{20,4},{24,16},{28,12},{1,9},{5... | collective-permute-start | bytes 786440 | tf_op jit(solution)/shard_map/ppermute | solution.py:326
  17.0 16.6 %copy-start.12 = (bf16[64,2048]{1,0:T(8,128)(2,1)}, bf16[64,2048]{1,0:T(8,128)(2,1)S(1)}, u32[]{:S(2)}) copy-start(bf16[64,2048]{1,0:T(8,128)(2,1)S(1)} %collective-permute-done.1.refs_4_) | copy-start | bytes 786436
  17.2 17.7 %copy-start.13 = (bf16[64,2048]{1,0:T(8,128)(2,1)}, bf16[64,2048]{1,0:T(8,128)(2,1)S(1)}, u32[]{:S(2)}) copy-start(bf16[64,2048]{1,0:T(8,128)(2,1)S(1)} %collective-permute-done.refs_3_) | copy-start | bytes 786436
  17.6 19.0 %copy-start = (bf16[256,2048]{1,0:T(8,128)(2,1)}, bf16[256,2048]{1,0:T(8,128)(2,1)S(1)}, u32[]{:S(2)}) copy-start(bf16[256,2048]{1,0:T(8,128)(2,1)S(1)} %shard_map.121.refs_9_.refs_7_.refs_3_) | copy-start | bytes 3145732
  17.6 14.9 %collective-permute-start.5 = (bf16[256,2048]{1,0:T(8,128)(2,1)S(1)}, bf16[256,2048]{1,0:T(8,128)(2,1)S(1)}, u32[]{:S(2)}, u32[]{:S(2)}) collective-permute-start(bf16[256,2048]{1,0:T(8,128)(2,1)S(1)} %shard_map.121.refs_9_.refs_7_.refs_3_), channel_id=1, source_target_pairs={{0,16},{4,12},{8,24},{12,4},{16,0},{20,28},{24,8},{28,20},{1,17},{... | collective-permute-start | bytes 3145736 | tf_op jit(solution)/shard_map/ppermute | solution.py:326
  19.2 13.1 %collective-permute-start.6 = (bf16[64,2048]{1,0:T(8,128)(2,1)S(1)}, bf16[64,2048]{1,0:T(8,128)(2,1)}, u32[]{:S(2)}, u32[]{:S(2)}) collective-permute-start(bf16[64,2048]{1,0:T(8,128)(2,1)S(1)} %copy-done.2), channel_id=1, source_target_pairs={{0,2},{1,3},{2,0},{3,1},{4,6},{5,7},{6,4},{7,5},{8,10},{9,11},{10,... | collective-permute-start | bytes 786440 | tf_op jit(solution)/shard_map/ppermute | solution.py:321
  20.2 12.1 %collective-permute-start.2 = (bf16[64,2048]{1,0:T(8,128)(2,1)S(1)}, bf16[64,2048]{1,0:T(8,128)(2,1)S(1)}, u32[]{:S(2)}, u32[]{:S(2)}) collective-permute-start(bf16[64,2048]{1,0:T(8,128)(2,1)S(1)} %collective-permute-done.1.refs_4_), channel_id=1, source_target_pairs={{0,1},{1,0},{2,3},{3,2},{4,5},{5,4},{6,7},{7,6},{8,9},{9,8},{10,11... | collective-permute-start | bytes 786440 | tf_op jit(solution)/shard_map/ppermute | solution.py:321
  32.3 2.7 %collective-permute-start.7 = (bf16[256,2048]{1,0:T(8,128)(2,1)S(1)}, bf16[256,2048]{1,0:T(8,128)(2,1)S(1)}, u32[]{:S(2)}, u32[]{:S(2)}) collective-permute-start(bf16[256,2048]{1,0:T(8,128)(2,1)S(1)} %shard_map.121.refs_9_.refs_7_.refs_3_), channel_id=1, source_target_pairs={{0,4},{4,0},{8,12},{12,8},{16,20},{20,16},{24,28},{28,24},{1,5},{5... | collective-permute-start | bytes 3145736 | tf_op jit(solution)/shard_map/ppermute | solution.py:321
  32.3 2.6 %copy-start.15 = (bf16[64,2048]{1,0:T(8,128)(2,1)}, bf16[64,2048]{1,0:T(8,128)(2,1)S(1)}, u32[]{:S(2)}) copy-start(bf16[64,2048]{1,0:T(8,128)(2,1)S(1)} %collective-permute-done.2.refs_5_) | copy-start | bytes 786436
  32.5 4.1 %copy-start.9 = (bf16[256,2048]{1,0:T(8,128)(2,1)}, bf16[256,2048]{1,0:T(8,128)(2,1)S(1)}, u32[]{:S(2)}) copy-start(bf16[256,2048]{1,0:T(8,128)(2,1)S(1)} %collective-permute-done.5.refs_10_.refs_8_.refs_4_) | copy-start | bytes 3145732
  32.5 4.1 %collective-permute-start.8 = (bf16[256,2048]{1,0:T(8,128)(2,1)S(1)}, bf16[256,2048]{1,0:T(8,128)(2,1)}, u32[]{:S(2)}, u32[]{:S(2)}) collective-permute-start(bf16[256,2048]{1,0:T(8,128)(2,1)S(1)} %collective-permute-done.5.refs_10_.refs_8_.refs_4_), channel_id=1, source_target_pairs={{0,4},{4,0},{8,12},{12,8},{16,20},{20,16},{24,28},{28,24},{1,5},{5... | collective-permute-start | bytes 3145736 | tf_op jit(solution)/shard_map/ppermute | solution.py:321
  32.9 13.2 %collective-permute-start.9 = (bf16[64,2048]{1,0:T(8,128)(2,1)S(1)}, bf16[64,2048]{1,0:T(8,128)(2,1)}, u32[]{:S(2)}, u32[]{:S(2)}) collective-permute-start(bf16[64,2048]{1,0:T(8,128)(2,1)S(1)} %copy-done.2), channel_id=1, source_target_pairs={{0,1},{1,0},{2,3},{3,2},{4,5},{5,4},{6,7},{7,6},{8,9},{9,8},{10,11... | collective-permute-start | bytes 786440 | tf_op jit(solution)/shard_map/ppermute | solution.py:321
  33.6 13.3 %collective-permute-start.10 = (bf16[64,2048]{1,0:T(8,128)(2,1)}, bf16[64,2048]{1,0:T(8,128)(2,1)}, u32[]{:S(2)}, u32[]{:S(2)}) collective-permute-start(bf16[64,2048]{1,0:T(8,128)(2,1)} %collective-permute-done.6.refs_4_.refs_14_), channel_id=1, source_target_pairs={{0,1},{1,0},{2,3},{3,2},{4,5},{5,4},{6,7},{7,6},{8,9},{9,8},{10,11... | collective-permute-start | bytes 786440 | tf_op jit(solution)/shard_map/ppermute | solution.py:321
  35.0 1.6 %copy-start.10 = (bf16[256,2048]{1,0:T(8,128)(2,1)}, bf16[256,2048]{1,0:T(8,128)(2,1)S(1)}, u32[]{:S(2)}) copy-start(bf16[256,2048]{1,0:T(8,128)(2,1)S(1)} %collective-permute-done.7.refs_11_.refs_9_.refs_5_) | copy-start | bytes 3145732
  46.9 3.6 %collective-permute-start.11 = (f32[1,320]{1,0:T(1,128)S(1)}, f32[1,320]{1,0:T(1,128)S(1)}, u32[]{:S(2)}, u32[]{:S(2)}) collective-permute-start(f32[1,320]{1,0:T(1,128)S(1)} %get-tuple-element.54), channel_id=1, source_target_pairs={{0,1},{1,0},{2,3},{3,2},{4,5},{5,4},{6,7},{7,6},{8,9},{9,8},{10,11... | collective-permute-start | bytes 3848 | tf_op jit(solution)/shard_map/ppermute | solution.py:321
  50.7 8.8 %collective-permute-start.12 = (bf16[64,2048]{1,0:T(8,128)(2,1)}, bf16[64,2048]{1,0:T(8,128)(2,1)S(1)}, u32[]{:S(2)}, u32[]{:S(2)}) collective-permute-start(bf16[64,2048]{1,0:T(8,128)(2,1)} %get-tuple-element.55), channel_id=1, source_target_pairs={{0,1},{1,0},{2,3},{3,2},{4,5},{5,4},{6,7},{7,6},{8,9},{9,8},{10,11... | collective-permute-start | bytes 786440 | tf_op jit(solution)/shard_map/ppermute | solution.py:321
  52.0 7.6 %copy-start.14 = (bf16[64,2048]{1,0:T(8,128)(2,1)S(1)}, bf16[64,2048]{1,0:T(8,128)(2,1)}, u32[]{:S(2)}) copy-start(bf16[64,2048]{1,0:T(8,128)(2,1)} %get-tuple-element.59) | copy-start | bytes 786436
  52.0 8.1 %copy-start.18 = (bf16[64,2048]{1,0:T(8,128)(2,1)S(1)}, bf16[64,2048]{1,0:T(8,128)(2,1)}, u32[]{:S(2)}) copy-start(bf16[64,2048]{1,0:T(8,128)(2,1)} %get-tuple-element.58) | copy-start | bytes 786436
  52.0 13.0 %copy-start.17 = (f32[128]{0:T(128)S(1)}, f32[128]{0:T(128)}, u32[]{:S(2)}) copy-start(f32[128]{0:T(128)} %param.15) | copy-start | bytes 1540
  52.0 7.4 %collective-permute-start.14 = (f32[1,384]{1,0:T(1,128)S(1)}, f32[1,384]{1,0:T(1,128)S(1)}, u32[]{:S(2)}, u32[]{:S(2)}) collective-permute-start(f32[1,384]{1,0:T(1,128)S(1)} %pad_maximum_fusion.1), channel_id=1, source_target_pairs={{0,2},{1,3},{2,0},{3,1},{4,6},{5,7},{6,4},{7,5},{8,10},{9,11},{10,... | collective-permute-start | bytes 4616 | tf_op jit(solution)/shard_map/ppermute | solution.py:321
  59.6 12.7 %collective-permute-start.15 = (bf16[64,2048]{1,0:T(8,128)(2,1)S(1)}, bf16[64,2048]{1,0:T(8,128)(2,1)S(1)}, u32[]{:S(2)}, u32[]{:S(2)}) collective-permute-start(bf16[64,2048]{1,0:T(8,128)(2,1)S(1)} %add_convert_fusion.4), channel_id=1, source_target_pairs={{0,2},{1,3},{2,0},{3,1},{4,6},{5,7},{6,4},{7,5},{8,10},{9,11},{10,... | collective-permute-start | bytes 786440 | tf_op jit(solution)/shard_map/ppermute | solution.py:321
  60.1 12.2 %collective-permute-start.13 = (bf16[64,2048]{1,0:T(8,128)(2,1)S(1)}, bf16[64,2048]{1,0:T(8,128)(2,1)S(1)}, u32[]{:S(2)}, u32[]{:S(2)}) collective-permute-start(bf16[64,2048]{1,0:T(8,128)(2,1)S(1)} %copy-done.18), channel_id=1, source_target_pairs={{0,1},{1,0},{2,3},{3,2},{4,5},{5,4},{6,7},{7,6},{8,9},{9,8},{10,11... | collective-permute-start | bytes 786440 | tf_op jit(solution)/shard_map/ppermute | solution.py:321
  61.7 3.4 %collective-permute-start.17 = (f32[1,512]{1,0:T(1,128)S(1)}, f32[1,512]{1,0:T(1,128)S(1)}, u32[]{:S(2)}, u32[]{:S(2)}) collective-permute-start(f32[1,512]{1,0:T(1,128)S(1)} %pad_maximum_fusion.refs_2_), channel_id=1, source_target_pairs={{4,8},{12,16},{20,24},{8,4},{16,12},{24,20},{5,9},{13,17},{21,25},... | collective-permute-start | bytes 6152 | tf_op jit(solution)/shard_map/ppermute | solution.py:493
  62.3 3.5 %collective-permute-start.16 = (f32[1,512]{1,0:T(1,128)S(1)}, f32[1,512]{1,0:T(1,128)S(1)}, u32[]{:S(2)}, u32[]{:S(2)}) collective-permute-start(f32[1,512]{1,0:T(1,128)S(1)} %pad_maximum_fusion.refs_2_), channel_id=1, source_target_pairs={{0,4},{4,0},{8,12},{12,8},{16,20},{20,16},{24,28},{28,24},{1,5},{5... | collective-permute-start | bytes 6152 | tf_op jit(solution)/shard_map/ppermute | solution.py:321
  72.3 4.9 %collective-permute-start.21 = (bf16[512,2048]{1,0:T(8,128)(2,1)S(1)}, bf16[512,2048]{1,0:T(8,128)(2,1)S(1)}, u32[]{:S(2)}, u32[]{:S(2)}) collective-permute-start(bf16[512,2048]{1,0:T(8,128)(2,1)S(1)} %get-tuple-element.77), channel_id=1, source_target_pairs={{0,4},{4,0},{8,12},{12,8},{16,20},{20,16},{24,28},{28,24},{1,5},{5... | collective-permute-start | bytes 6291464 | tf_op jit(solution)/shard_map/ppermute | solution.py:321
  77.6 17.7 %copy-start.1 = (bf16[64,2048]{1,0:T(8,128)(2,1)S(1)}, bf16[64,2048]{1,0:T(8,128)(2,1)}, u32[]{:S(2)}) copy-start(bf16[64,2048]{1,0:T(8,128)(2,1)} %x_ref.1) | copy-start | bytes 786436
  77.6 17.7 %copy-start.11 = (bf16[64,2048]{1,0:T(8,128)(2,1)S(1)}, bf16[64,2048]{1,0:T(8,128)(2,1)}, u32[]{:S(2)}) copy-start(bf16[64,2048]{1,0:T(8,128)(2,1)} %get-tuple-element.48) | copy-start | bytes 786436
  77.6 14.9 %collective-permute-start.22 = (bf16[256,2048]{1,0:T(8,128)(2,1)S(1)}, bf16[256,2048]{1,0:T(8,128)(2,1)S(1)}, u32[]{:S(2)}, u32[]{:S(2)}) collective-permute-start(bf16[256,2048]{1,0:T(8,128)(2,1)S(1)} %add_convert_fusion), channel_id=1, source_target_pairs={{0,8},{4,20},{8,0},{12,28},{16,24},{20,4},{24,16},{28,12},{1,9},{5... | collective-permute-start | bytes 3145736 | tf_op jit(solution)/shard_map/ppermute | solution.py:326
  79.4 9.2 %collective-permute-start.18 = (bf16[64,2048]{1,0:T(8,128)(2,1)S(1)}, bf16[64,2048]{1,0:T(8,128)(2,1)S(1)}, u32[]{:S(2)}, u32[]{:S(2)}) collective-permute-start(bf16[64,2048]{1,0:T(8,128)(2,1)S(1)} %get-tuple-element.71), channel_id=1, source_target_pairs={{0,1},{1,0},{2,3},{3,2},{4,5},{5,4},{6,7},{7,6},{8,9},{9,8},{10,11... | collective-permute-start | bytes 786440 | tf_op jit(solution)/shard_map/ppermute | solution.py:321
  88.6 13.6 %collective-permute-start.19 = (bf16[64,2048]{1,0:T(8,128)(2,1)S(1)}, bf16[64,2048]{1,0:T(8,128)(2,1)S(1)}, u32[]{:S(2)}, u32[]{:S(2)}) collective-permute-start(bf16[64,2048]{1,0:T(8,128)(2,1)S(1)} %get-tuple-element.72), channel_id=1, source_target_pairs={{0,1},{1,0},{2,3},{3,2},{4,5},{5,4},{6,7},{7,6},{8,9},{9,8},{10,11... | collective-permute-start | bytes 786440 | tf_op jit(solution)/shard_map/ppermute | solution.py:321
  89.1 14.7 %collective-permute-start.20 = (bf16[64,2048]{1,0:T(8,128)(2,1)S(1)}, bf16[64,2048]{1,0:T(8,128)(2,1)S(1)}, u32[]{:S(2)}, u32[]{:S(2)}) collective-permute-start(bf16[64,2048]{1,0:T(8,128)(2,1)S(1)} %add_convert_fusion.2), channel_id=1, source_target_pairs={{0,2},{1,3},{2,0},{3,1},{4,6},{5,7},{6,4},{7,5},{8,10},{9,11},{10,... | collective-permute-start | bytes 786440 | tf_op jit(solution)/shard_map/ppermute | solution.py:321
  92.8 9.7 %collective-permute-start.23 = (bf16[128,2048]{1,0:T(8,128)(2,1)S(1)}, bf16[128,2048]{1,0:T(8,128)(2,1)S(1)}, u32[]{:S(2)}, u32[]{:S(2)}) collective-permute-start(bf16[128,2048]{1,0:T(8,128)(2,1)S(1)} %add_convert_fusion.1), channel_id=1, source_target_pairs={{0,16},{4,12},{8,24},{12,4},{16,0},{20,28},{24,8},{28,20},{1,17},{... | collective-permute-start | bytes 1572872 | tf_op jit(solution)/shard_map/ppermute | solution.py:326
  102.3 1.6 %copy-start.3 = (bf16[64,2048]{1,0:T(8,128)(2,1)S(1)}, bf16[64,2048]{1,0:T(8,128)(2,1)}, u32[]{:S(2)}) copy-start(bf16[64,2048]{1,0:T(8,128)(2,1)} %upstream.1) | copy-start | bytes 786436

commit v6 on v5

--- a/solution.py
+++ b/solution.py
@@ -206,10 +206,11 @@
     pltpu.make_async_copy(upper, upper_out, sems.at[nf + 1]).wait()
 
 
-def grads_kernel(orders, scale, nf, *refs):
+def grads_kernel(masks, orders, scale, nf, *refs):
     idx, place, here, left, right, teacher, turn, readout, upper_in, dact_in, normed_in, act_in = refs[:12]
     ups, refs = refs[12 : 12 + nf], refs[12 + nf:]
-    own_coeff, pre_grad, keep, send, upper, dact, normed, act, cot, ubuf, sems = refs
+    parts, refs = refs[: len(masks)], refs[len(masks):]
+    own_coeff, pre_grad, keep, send, win, upper, dact, normed, act, cot, ubuf, sems = refs
     nj, kb = idx.shape
     rows = ubuf.shape[1]
     tokens = nf * rows
@@ -219,6 +220,7 @@
     dact_wait = load(dact_in, dact, sems.at[1])
     normed_wait = load(normed_in, normed, sems.at[2])
     act_wait = load(act_in, act, sems.at[3])
+    win_wait = load_weight(place, parts, masks, 0, win, sems.at[4 + nf])
     seg = (lax.broadcasted_iota(jnp.int32, (nseg, tokens), 0) + 1).astype(F32)
     sums = jnp.zeros((nseg, 1), F32)
     counts = jnp.zeros((nseg, 1), F32)
@@ -249,16 +251,13 @@
     normed_wait()
     act_wait()
     store_grads(idx, place, orders, scale, ((cot, act), (normed, pre_grad)), keep, send)
-
-
-def back_kernel(masks, nf, *refs):
-    idx, place, pre_grad = refs[:3]
-    parts, refs = refs[3 : 3 + len(masks)], refs[3 + len(masks):]
-    outs, (win, acc, sem) = refs[:nf], refs[nf:]
+    win_wait()
+
+
+def back_kernel(nf, idx, pre_grad, win, *refs):
+    outs, acc = refs[:nf], refs[nf]
     nj, kb = idx.shape
-    win_wait = load_weight(place, parts, masks, 0, win, sem)
     acc[...] = jnp.zeros_like(acc)
-    win_wait()
 
     @loop(nj)
     def _(j):
@@ -494,19 +493,21 @@
 
     branch_near = {d: after(got, turn) for d, got in branch_near.items()}
     half_grads = sds((kb * BLK, hidden), BF16)
-    own_coeff, pre_grad, keep, send = call(
-        functools.partial(grads_kernel, orders, grad_scale, nf),
+    own_coeff, pre_grad, keep, send, win = call(
+        functools.partial(grads_kernel, masks, orders, grad_scale, nf),
         [
             (VM, sds((rows, BLK), F32)),
             (VM, sds((nj, tokens, BLK), BF16)),
             (VM, half_grads),
             (VM, half_grads),
+            (VM, sds((kb * BLK, hidden), BF16)),
         ],
         scalars
         + [(VM, here), (VM, left), (VM, right), (VM, teacher_scores.reshape(-1, 1)), (VM, turn)]
         + [(VM, readout_row)]
         + [(HBM, a) for a in (upper, dact, normed, act)]
-        + [(HBM, u) for u in ups],
+        + [(HBM, u) for u in ups]
+        + parts,
         [
             by_hidden,
             by_hidden,
@@ -514,15 +515,15 @@
             by_hidden,
             by_feature,
             pltpu.VMEM((nf, rows, width), BF16),
-            pltpu.SemaphoreType.DMA((nf + 4,)),
+            pltpu.SemaphoreType.DMA((nf + 5,)),
         ],
         2 * flops,
     )
     back = call(
-        functools.partial(back_kernel, masks, nf),
+        functools.partial(back_kernel, nf),
         [(VM, piece)] * nf,
-        scalars + [(VM, pre_grad)] + parts,
-        [weight, summed, pltpu.SemaphoreType.DMA],
+        [(SM, block_index), (VM, pre_grad), (VM, win)],
+        [summed],
         flops,
     )
     branch_own, branch_got, beside = scatter_far(branch, branch_near, feat_bits, here)

time: 105 us -> 105 us (level)
  Pallas kernels: 26 us -> 24.5 us
    pallas_call x7, Pallas kernels: 26 us -> 24.5 us  [call(): pl.pallas_call(body, out_shape=[pltpu.HBM(o.shape, o.dtype) if m is HBM e...]
  transfers between devices with their start and end apart: 24 -> 24, of which waited for: 13 -> 14; matrix products, arithmetic and copies ran while one was open for 3% -> 3% of each run, Pallas kernels for 24% -> 22%
where the time goes in v6:
time: 105 us
  waiting for transfers between devices  39 us (37%)
  starting transfers between devices  34.8 us (33%)
  Pallas kernels  24.5 us (23%)
  local copies, waits for them, and re-layouts  3.46 us (3%)
  other arithmetic  2.12 us (2%)
    ppermute x18, waiting for transfers between devices, swap(): return lax.ppermute(value, axis, [(i, i ^ mask) for i in range(n)])  37.2 us
    ppermute x18, starting transfers between devices, swap(): return lax.ppermute(value, axis, [(i, i ^ mask) for i in range(n)])  25.8 us
    pallas_call x7, Pallas kernels, call(): pl.pallas_call(body, out_shape=[pltpu.HBM(o.shape, o.dtype) if m is HBM e...  24.5 us
    ppermute x5, starting transfers between devices, swap_tok(): lax.ppermute(value, 'tok', [(i, i ^ (odd if i & 1 else even)) for i in ra...  8.42 us
  transfers between devices with their start and end apart: 24, of which 14 were waited for; matrix products, arithmetic and copies ran while one was open for 3% of the time, Pallas kernels for 22%

profile of v6, /device:TPU:0, one launch (start us, length us, event | category | flops | bytes accessed | tf_op | source)
XLA Modules:
  0.0 104.8 jit_solution(16574843586138147759)
XLA Ops:
  0.6 0.0 copy-start.2
  0.6 4.1 %collective-permute-start.1 = (bf16[64,2048]{1,0:T(8,128)(2,1)}, bf16[64,2048]{1,0:T(8,128)(2,1)S(1)}, u32[]{:S(2)}, u32[]{:S(2)}) collective-permute-start(bf16[64,2048]{1,0:T(8,128)(2,1)} %x_ref.1), channel_id=1, source_target_pairs={{0,2},{1,3},{2,0},{3,1},{4,6},{5,7},{6,4},{7,5},{8,10},{9,11},{10,... | collective-permute-start | bytes 786440 | tf_op jit(solution)/shard_map/ppermute | solution.py:320
  4.7 1.6 %collective-permute-start = (bf16[64,2048]{1,0:T(8,128)(2,1)}, bf16[64,2048]{1,0:T(8,128)(2,1)S(1)}, u32[]{:S(2)}, u32[]{:S(2)}) collective-permute-start(bf16[64,2048]{1,0:T(8,128)(2,1)} %x_ref.1), channel_id=1, source_target_pairs={{0,1},{1,0},{2,3},{3,2},{4,5},{5,4},{6,7},{7,6},{8,9},{9,8},{10,11... | collective-permute-start | bytes 786440 | tf_op jit(solution)/shard_map/ppermute | solution.py:320
  6.3 0.9 copy-done.4
  7.3 0.9 copy-done.5
  8.3 1.6 %collective-permute-start.3 = (bf16[64,2048]{1,0:T(8,128)(2,1)S(1)}, bf16[64,2048]{1,0:T(8,128)(2,1)S(1)}, u32[]{:S(2)}, u32[]{:S(2)}) collective-permute-start(bf16[64,2048]{1,0:T(8,128)(2,1)S(1)} %copy-done.4), channel_id=1, source_target_pairs={{0,8},{4,20},{8,0},{12,28},{16,24},{20,4},{24,16},{28,12},{1,9},{5... | collective-permute-start | bytes 786440 | tf_op jit(solution)/shard_map/ppermute | solution.py:325
  9.8 0.5 collective-permute-start.4
  10.4 6.6 %collective-permute-done.1.refs_4_ = bf16[64,2048]{1,0:T(8,128)(2,1)S(1)} collective-permute-done((bf16[64,2048]{1,0:T(8,128)(2,1)}, bf16[64,2048]{1,0:T(8,128)(2,1)S(1)}, u32[]{:S(2)}, u32[]{:S(2)}) %collective-permute-start.1) | collective-permute-done | bytes 262176 | tf_op jit(solution)/shard_map/ppermute | solution.py:320
  17.0 0.2 collective-permute-done.refs_3_
  17.2 0.3 collective-permute-done.4.refs_2_
  17.5 0.1 shard_map.121.refs_9_.refs_7_.refs_16_
  17.6 1.6 %collective-permute-start.5 = (bf16[256,2048]{1,0:T(8,128)(2,1)S(1)}, bf16[256,2048]{1,0:T(8,128)(2,1)S(1)}, u32[]{:S(2)}, u32[]{:S(2)}) collective-permute-start(bf16[256,2048]{1,0:T(8,128)(2,1)S(1)} %shard_map.121.refs_9_.refs_7_.refs_16_), channel_id=1, source_target_pairs={{0,16},{4,12},{8,24},{12,4},{16,0},{20,28},{24,8},{28,20},{1,17},{... | collective-permute-start | bytes 3145736 | tf_op jit(solution)/shard_map/ppermute | solution.py:325
  19.2 1.0 collective-permute-start.6
  20.2 2.4 %collective-permute-start.2 = (bf16[64,2048]{1,0:T(8,128)(2,1)S(1)}, bf16[64,2048]{1,0:T(8,128)(2,1)S(1)}, u32[]{:S(2)}, u32[]{:S(2)}) collective-permute-start(bf16[64,2048]{1,0:T(8,128)(2,1)S(1)} %collective-permute-done.1.refs_4_), channel_id=1, source_target_pairs={{0,1},{1,0},{2,3},{3,2},{4,5},{5,4},{6,7},{7,6},{8,9},{9,8},{10,11... | collective-permute-start | bytes 786440 | tf_op jit(solution)/shard_map/ppermute | solution.py:320
  22.7 9.6 %collective-permute-done.6.refs_4_.refs_14_ = bf16[64,2048]{1,0:T(8,128)(2,1)} collective-permute-done((bf16[64,2048]{1,0:T(8,128)(2,1)S(1)}, bf16[64,2048]{1,0:T(8,128)(2,1)}, u32[]{:S(2)}, u32[]{:S(2)}) %collective-permute-start.6) | collective-permute-done | bytes 262176 | tf_op jit(solution)/shard_map/ppermute | solution.py:320
  32.3 0.2 collective-permute-done.5.refs_10_.refs_8_.refs_17_
  32.5 0.4 collective-permute-start.8
  32.9 0.7 collective-permute-start.9
  33.6 1.3 %collective-permute-start.10 = (bf16[64,2048]{1,0:T(8,128)(2,1)}, bf16[64,2048]{1,0:T(8,128)(2,1)}, u32[]{:S(2)}, u32[]{:S(2)}) collective-permute-start(bf16[64,2048]{1,0:T(8,128)(2,1)} %collective-permute-done.6.refs_4_.refs_14_), channel_id=1, source_target_pairs={{0,1},{1,0},{2,3},{3,2},{4,5},{5,4},{6,7},{7,6},{8,9},{9,8},{10,11... | collective-permute-start | bytes 786440 | tf_op jit(solution)/shard_map/ppermute | solution.py:320
  34.9 0.1 copy.13.refs_0_.idx
  35.0 1.6 %collective-permute-done.8.refs_12_.refs_10_.refs_19_ = bf16[256,2048]{1,0:T(8,128)(2,1)} collective-permute-done((bf16[256,2048]{1,0:T(8,128)(2,1)S(1)}, bf16[256,2048]{1,0:T(8,128)(2,1)}, u32[]{:S(2)}, u32[]{:S(2)}) %collective-permute-start.8) | collective-permute-done | bytes 1048608 | tf_op jit(solution)/shard_map/ppermute | solution.py:320
  36.6 9.4 %shard_map.122 = (bf16[16,256,128]{2,1,0:T(8,128)(2,1)}, bf16[16,256,128]{2,1,0:T(8,128)(2,1)}, bf16[16,256,128]{2,1,0:T(8,128)(2,1)}, f32[1,320]{1,0:T(1,128)S(...) custom-call(s32[16,4]{1,0:T(8,128)S(1)} %copy.13.refs_0_.idx, ...), custom_call_target="tpu_custom_call" | custom-call | flops 1073741824 | bytes 4195584 | tf_op jit(solution)/shard_map/pallas_call | solution.py:288
  46.1 0.9 collective-permute-done.10.refs_5_.refs_15_
  46.9 1.2 %collective-permute-start.11 = (f32[1,320]{1,0:T(1,128)S(1)}, f32[1,320]{1,0:T(1,128)S(1)}, u32[]{:S(2)}, u32[]{:S(2)}) collective-permute-start(f32[1,320]{1,0:T(1,128)S(1)} %get-tuple-element.55), channel_id=1, source_target_pairs={{0,1},{1,0},{2,3},{3,2},{4,5},{5,4},{6,7},{7,6},{8,9},{9,8},{10,11... | collective-permute-start | bytes 3848 | tf_op jit(solution)/shard_map/ppermute | solution.py:320
  48.1 2.4 %collective-permute-done.11 = f32[1,320]{1,0:T(1,128)S(1)} collective-permute-done((f32[1,320]{1,0:T(1,128)S(1)}, f32[1,320]{1,0:T(1,128)S(1)}, u32[]{:S(2)}, u32[]{:S(2)}) %collective-permute-start.11) | collective-permute-done | bytes 1312 | tf_op jit(solution)/shard_map/ppermute | solution.py:320
  50.5 0.1 reshape.39
  50.6 0.1 reshape.40
  50.7 1.2 %collective-permute-start.12 = (bf16[64,2048]{1,0:T(8,128)(2,1)}, bf16[64,2048]{1,0:T(8,128)(2,1)S(1)}, u32[]{:S(2)}, u32[]{:S(2)}) collective-permute-start(bf16[64,2048]{1,0:T(8,128)(2,1)} %get-tuple-element.56), channel_id=1, source_target_pairs={{0,1},{1,0},{2,3},{3,2},{4,5},{5,4},{6,7},{7,6},{8,9},{9,8},{10,11... | collective-permute-start | bytes 786440 | tf_op jit(solution)/shard_map/ppermute | solution.py:320
  51.9 0.1 pad_maximum_fusion.1
  52.0 2.7 %collective-permute-start.14 = (f32[1,384]{1,0:T(1,128)S(1)}, f32[1,384]{1,0:T(1,128)S(1)}, u32[]{:S(2)}, u32[]{:S(2)}) collective-permute-start(f32[1,384]{1,0:T(1,128)S(1)} %pad_maximum_fusion.1), channel_id=1, source_target_pairs={{0,2},{1,3},{2,0},{3,1},{4,6},{5,7},{6,4},{7,5},{8,10},{9,11},{10,... | collective-permute-start | bytes 4616 | tf_op jit(solution)/shard_map/ppermute | solution.py:320
  54.7 4.7 %shard_map.123 = (bf16[16,256,128]{2,1,0:T(8,128)(2,1)}, f32[1,2048]{1,0:T(1,128)S(1)}) custom-call(s32[16,4]{1,0:T(8,128)S(1)} %copy.13.refs_0_.idx, s32[1]{0:T(128)} %bitcast.refs_1_, bf16[64,2048]{1,0:T(8,128)(2,1)} %upstream.1, bf16[64,2048]{1,0:T(8,128)(2,1)} %collective-permute-done.9.refs_3_.refs_13_, ...), custom_call_target="tpu_custom_call" | custom-call | flops 536870912 | bytes 1056768 | tf_op jit(solution)/shard_map/pallas_call | solution.py:288
  59.5 0.1 pad_maximum_fusion.refs_2_
  59.6 0.1 add_convert_fusion.4
  59.6 0.4 collective-permute-start.15
  60.1 1.6 %collective-permute-start.13 = (bf16[64,2048]{1,0:T(8,128)(2,1)S(1)}, bf16[64,2048]{1,0:T(8,128)(2,1)S(1)}, u32[]{:S(2)}, u32[]{:S(2)}) collective-permute-start(bf16[64,2048]{1,0:T(8,128)(2,1)S(1)} %copy-done.18), channel_id=1, source_target_pairs={{0,1},{1,0},{2,3},{3,2},{4,5},{5,4},{6,7},{7,6},{8,9},{9,8},{10,11... | collective-permute-start | bytes 786440 | tf_op jit(solution)/shard_map/ppermute | solution.py:320
  61.7 0.6 collective-permute-start.17
  62.3 2.7 %collective-permute-start.16 = (f32[1,512]{1,0:T(1,128)S(1)}, f32[1,512]{1,0:T(1,128)S(1)}, u32[]{:S(2)}, u32[]{:S(2)}) collective-permute-start(f32[1,512]{1,0:T(1,128)S(1)} %pad_maximum_fusion.refs_2_), channel_id=1, source_target_pairs={{0,4},{4,0},{8,12},{12,8},{16,20},{20,16},{24,28},{28,24},{1,5},{5... | collective-permute-start | bytes 6152 | tf_op jit(solution)/shard_map/ppermute | solution.py:320
  65.0 0.1 copy.16.refs_5_
  65.1 0.7 collective-permute-done.16.refs_3_
  65.8 6.3 %shard_map.124 = (f32[64,128]{1,0:T(8,128)S(1)}, bf16[16,256,128]{2,1,0:T(8,128)(2,1)S(1)}, bf16[512,2048]{1,0:T(8,128)(2,1)S(1)}, bf16[512,2048]{1,0:T(8,128)(2,1)S(1)}, bf16[512,2048]{1,0:T(8,128)(2,1)S(1)}) custom-call(s32[16,4]{1,0:T(8,128)S(1)} %copy.13.refs_0_.idx, s32[1]{0:T(128)} %bitcast.refs_1_, f32[1,512]{1,0:T(1,128)S(1)} %pad_maximum_fusion.refs_2_, ...), custom_call_target="tpu_custom_call" | custom-call | flops 1073741824 | bytes 7372800 | tf_op jit(solution)/shard_map/pallas_call | solution.py:288
  72.1 0.0 collective-permute-done.15
  72.2 0.7 collective-permute-start.21
  72.9 2.8 %shard_map.125 = (bf16[64,2048]{1,0:T(8,128)(2,1)S(1)}, bf16[64,2048]{1,0:T(8,128)(2,1)S(1)}, bf16[64,2048]{1,0:T(8,128)(2,1)S(1)}, bf16[64,2048]{1,0:T(8,128)(2,1)S(1)}) custom-call(s32[16,4]{1,0:T(8,128)S(1)} %copy.13.refs_0_.idx, bf16[16,256,128]{2,1,0:T(8,128)(2,1)S(1)} %get-tuple-element.69.pre_grad, bf16[512,2048]{1,0:T(8,128)(2,1)S(1)} %get-tuple-element.70.win), custom_call_target="tpu_custom_call" | custom-call | flops 536870912 | bytes 1048576 | tf_op jit(solution)/shard_map/pallas_call | solution.py:288
  75.7 1.0 collective-permute-done.21
  76.7 0.4 add_convert_fusion
  77.1 0.0 copy-start.1
  77.1 0.0 copy-start.11
  77.1 1.8 %collective-permute-start.22 = (bf16[256,2048]{1,0:T(8,128)(2,1)S(1)}, bf16[256,2048]{1,0:T(8,128)(2,1)S(1)}, u32[]{:S(2)}, u32[]{:S(2)}) collective-permute-start(bf16[256,2048]{1,0:T(8,128)(2,1)S(1)} %add_convert_fusion), channel_id=1, source_target_pairs={{0,8},{4,20},{8,0},{12,28},{16,24},{20,4},{24,16},{28,12},{1,9},{5... | collective-permute-start | bytes 3145736 | tf_op jit(solution)/shard_map/ppermute | solution.py:325
  78.9 0.6 collective-permute-start.18
  79.6 8.5 %collective-permute-done.18 = bf16[64,2048]{1,0:T(8,128)(2,1)S(1)} collective-permute-done((bf16[64,2048]{1,0:T(8,128)(2,1)S(1)}, bf16[64,2048]{1,0:T(8,128)(2,1)S(1)}, u32[]{:S(2)}, u32[]{:S(2)}) %collective-permute-start.18) | collective-permute-done | bytes 262176 | tf_op jit(solution)/shard_map/ppermute | solution.py:320
  88.1 0.5 collective-permute-start.19
  88.5 0.1 add_convert_fusion.2
  88.6 2.6 %collective-permute-start.20 = (bf16[64,2048]{1,0:T(8,128)(2,1)S(1)}, bf16[64,2048]{1,0:T(8,128)(2,1)S(1)}, u32[]{:S(2)}, u32[]{:S(2)}) collective-permute-start(bf16[64,2048]{1,0:T(8,128)(2,1)S(1)} %add_convert_fusion.2), channel_id=1, source_target_pairs={{0,2},{1,3},{2,0},{3,1},{4,6},{5,7},{6,4},{7,5},{8,10},{9,11},{10,... | collective-permute-start | bytes 786440 | tf_op jit(solution)/shard_map/ppermute | solution.py:320
  91.2 0.8 collective-permute-done.22
  92.0 0.2 add_convert_fusion.1
  92.2 2.9 %collective-permute-start.23 = (bf16[128,2048]{1,0:T(8,128)(2,1)S(1)}, bf16[128,2048]{1,0:T(8,128)(2,1)S(1)}, u32[]{:S(2)}, u32[]{:S(2)}) collective-permute-start(bf16[128,2048]{1,0:T(8,128)(2,1)S(1)} %add_convert_fusion.1), channel_id=1, source_target_pairs={{0,16},{4,12},{8,24},{12,4},{16,0},{20,28},{24,8},{28,20},{1,17},{... | collective-permute-start | bytes 1572872 | tf_op jit(solution)/shard_map/ppermute | solution.py:325
  95.2 0.8 add_convert_fusion.3
  96.0 5.7 %collective-permute-done.19 = bf16[64,2048]{1,0:T(8,128)(2,1)S(1)} collective-permute-done((bf16[64,2048]{1,0:T(8,128)(2,1)S(1)}, bf16[64,2048]{1,0:T(8,128)(2,1)S(1)}, u32[]{:S(2)}, u32[]{:S(2)}) %collective-permute-start.19) | collective-permute-done | bytes 262176 | tf_op jit(solution)/shard_map/ppermute | solution.py:320
  101.7 0.1 convert_add_fusion.1.own
  101.8 0.0 copy-start.3
  101.8 0.5 collective-permute-done.23
  102.3 0.3 convert_add_fusion
  102.6 1.0 fusion
  103.7 1.1 %shard_map.126 = bf16[64,2048]{1,0:T(8,128)(2,1)} custom-call(bf16[64,2048]{1,0:T(8,128)(2,1)S(1)} %copy-done.1, f32[1,2048]{1,0:T(1,128)S(1)} %bitcast.12, bf16[64,2048]{1,0:T(8,128)(2,1)S(1)} %copy-done.3, f32[1,2048]{1,0:T(1,128)S(1)} %bitcast.10, f32[64,128]{1,0:T(8,128)S(1)} %get-tuple-element.67.own_coeff, f32[64,2048]{1,0:T(8,128)S(1)} %convert_add_fusion.1.own, ...), custom_call_target="tpu_custom_call" | custom-call | flops 131072 | bytes 262144 | tf_op jit(solution)/shard_map/pallas_call | solution.py:288
  (52 shorter events, 0.2 us)
Async XLA Ops:
  0.6 18.6 %copy-start.2 = (bf16[64,2048]{1,0:T(8,128)(2,1)S(1)}, bf16[64,2048]{1,0:T(8,128)(2,1)}, u32[]{:S(2)}) copy-start(bf16[64,2048]{1,0:T(8,128)(2,1)} %upstream.1) | copy-start | bytes 786436
  0.6 16.3 %collective-permute-start.1 = (bf16[64,2048]{1,0:T(8,128)(2,1)}, bf16[64,2048]{1,0:T(8,128)(2,1)S(1)}, u32[]{:S(2)}, u32[]{:S(2)}) collective-permute-start(bf16[64,2048]{1,0:T(8,128)(2,1)} %x_ref.1), channel_id=1, source_target_pairs={{0,2},{1,3},{2,0},{3,1},{4,6},{5,7},{6,4},{7,5},{8,10},{9,11},{10,... | collective-permute-start | bytes 786440 | tf_op jit(solution)/shard_map/ppermute | solution.py:320
  4.7 12.4 %collective-permute-start = (bf16[64,2048]{1,0:T(8,128)(2,1)}, bf16[64,2048]{1,0:T(8,128)(2,1)S(1)}, u32[]{:S(2)}, u32[]{:S(2)}) collective-permute-start(bf16[64,2048]{1,0:T(8,128)(2,1)} %x_ref.1), channel_id=1, source_target_pairs={{0,1},{1,0},{2,3},{3,2},{4,5},{5,4},{6,7},{7,6},{8,9},{9,8},{10,11... | collective-permute-start | bytes 786440 | tf_op jit(solution)/shard_map/ppermute | solution.py:320
  6.3 0.9 copy-start.4
  7.3 0.9 copy-start.5
  8.2 26.7 %copy-start.16 = (s32[16,4]{0,1:T(4,128)S(1)}, s32[16,4]{0,1:T(4,128)}, u32[]{:S(2)}) copy-start(s32[16,4]{0,1:T(4,128)} %param.13) | copy-start | bytes 772
  8.2 28.4 %copy-start.6 = (f32[2048]{0:T(1024)S(1)}, f32[2048]{0:T(1024)}, u32[]{:S(2)}) copy-start(f32[2048]{0:T(1024)} %param.17) | copy-start | bytes 24580
  8.2 28.4 %copy-start.7 = (f32[2048]{0:T(1024)S(1)}, f32[2048]{0:T(1024)}, u32[]{:S(2)}) copy-start(f32[2048]{0:T(1024)} %param.10) | copy-start | bytes 24580
  8.2 28.4 %copy-start.8 = (s32[64]{0:T(128)S(1)}, s32[64]{0:T(128)}, u32[]{:S(2)}) copy-start(s32[64]{0:T(128)} %param.14) | copy-start | bytes 772
  8.3 8.9 %collective-permute-start.3 = (bf16[64,2048]{1,0:T(8,128)(2,1)S(1)}, bf16[64,2048]{1,0:T(8,128)(2,1)S(1)}, u32[]{:S(2)}, u32[]{:S(2)}) collective-permute-start(bf16[64,2048]{1,0:T(8,128)(2,1)S(1)} %copy-done.4), channel_id=1, source_target_pairs={{0,8},{4,20},{8,0},{12,28},{16,24},{20,4},{24,16},{28,12},{1,9},{5... | collective-permute-start | bytes 786440 | tf_op jit(solution)/shard_map/ppermute | solution.py:325
  9.8 7.7 %collective-permute-start.4 = (bf16[64,2048]{1,0:T(8,128)(2,1)S(1)}, bf16[64,2048]{1,0:T(8,128)(2,1)S(1)}, u32[]{:S(2)}, u32[]{:S(2)}) collective-permute-start(bf16[64,2048]{1,0:T(8,128)(2,1)S(1)} %copy-done.5), channel_id=1, source_target_pairs={{0,8},{4,20},{8,0},{12,28},{16,24},{20,4},{24,16},{28,12},{1,9},{5... | collective-permute-start | bytes 786440 | tf_op jit(solution)/shard_map/ppermute | solution.py:325
  17.0 16.6 %copy-start.12 = (bf16[64,2048]{1,0:T(8,128)(2,1)}, bf16[64,2048]{1,0:T(8,128)(2,1)S(1)}, u32[]{:S(2)}) copy-start(bf16[64,2048]{1,0:T(8,128)(2,1)S(1)} %collective-permute-done.1.refs_4_) | copy-start | bytes 786436
  17.2 17.7 %copy-start.13 = (bf16[64,2048]{1,0:T(8,128)(2,1)}, bf16[64,2048]{1,0:T(8,128)(2,1)S(1)}, u32[]{:S(2)}) copy-start(bf16[64,2048]{1,0:T(8,128)(2,1)S(1)} %collective-permute-done.refs_3_) | copy-start | bytes 786436
  17.6 19.0 %copy-start = (bf16[256,2048]{1,0:T(8,128)(2,1)}, bf16[256,2048]{1,0:T(8,128)(2,1)S(1)}, u32[]{:S(2)}) copy-start(bf16[256,2048]{1,0:T(8,128)(2,1)S(1)} %shard_map.121.refs_9_.refs_7_.refs_16_) | copy-start | bytes 3145732
  17.6 14.9 %collective-permute-start.5 = (bf16[256,2048]{1,0:T(8,128)(2,1)S(1)}, bf16[256,2048]{1,0:T(8,128)(2,1)S(1)}, u32[]{:S(2)}, u32[]{:S(2)}) collective-permute-start(bf16[256,2048]{1,0:T(8,128)(2,1)S(1)} %shard_map.121.refs_9_.refs_7_.refs_16_), channel_id=1, source_target_pairs={{0,16},{4,12},{8,24},{12,4},{16,0},{20,28},{24,8},{28,20},{1,17},{... | collective-permute-start | bytes 3145736 | tf_op jit(solution)/shard_map/ppermute | solution.py:325
  19.2 13.1 %collective-permute-start.6 = (bf16[64,2048]{1,0:T(8,128)(2,1)S(1)}, bf16[64,2048]{1,0:T(8,128)(2,1)}, u32[]{:S(2)}, u32[]{:S(2)}) collective-permute-start(bf16[64,2048]{1,0:T(8,128)(2,1)S(1)} %copy-done.2), channel_id=1, source_target_pairs={{0,2},{1,3},{2,0},{3,1},{4,6},{5,7},{6,4},{7,5},{8,10},{9,11},{10,... | collective-permute-start | bytes 786440 | tf_op jit(solution)/shard_map/ppermute | solution.py:320
  20.2 12.1 %collective-permute-start.2 = (bf16[64,2048]{1,0:T(8,128)(2,1)S(1)}, bf16[64,2048]{1,0:T(8,128)(2,1)S(1)}, u32[]{:S(2)}, u32[]{:S(2)}) collective-permute-start(bf16[64,2048]{1,0:T(8,128)(2,1)S(1)} %collective-permute-done.1.refs_4_), channel_id=1, source_target_pairs={{0,1},{1,0},{2,3},{3,2},{4,5},{5,4},{6,7},{7,6},{8,9},{9,8},{10,11... | collective-permute-start | bytes 786440 | tf_op jit(solution)/shard_map/ppermute | solution.py:320
  32.3 2.7 %collective-permute-start.7 = (bf16[256,2048]{1,0:T(8,128)(2,1)S(1)}, bf16[256,2048]{1,0:T(8,128)(2,1)S(1)}, u32[]{:S(2)}, u32[]{:S(2)}) collective-permute-start(bf16[256,2048]{1,0:T(8,128)(2,1)S(1)} %shard_map.121.refs_9_.refs_7_.refs_16_), channel_id=1, source_target_pairs={{0,4},{4,0},{8,12},{12,8},{16,20},{20,16},{24,28},{28,24},{1,5},{5... | collective-permute-start | bytes 3145736 | tf_op jit(solution)/shard_map/ppermute | solution.py:320
  32.3 2.6 %copy-start.15 = (bf16[64,2048]{1,0:T(8,128)(2,1)}, bf16[64,2048]{1,0:T(8,128)(2,1)S(1)}, u32[]{:S(2)}) copy-start(bf16[64,2048]{1,0:T(8,128)(2,1)S(1)} %collective-permute-done.2.refs_5_) | copy-start | bytes 786436
  32.5 4.1 %copy-start.9 = (bf16[256,2048]{1,0:T(8,128)(2,1)}, bf16[256,2048]{1,0:T(8,128)(2,1)S(1)}, u32[]{:S(2)}) copy-start(bf16[256,2048]{1,0:T(8,128)(2,1)S(1)} %collective-permute-done.5.refs_10_.refs_8_.refs_17_) | copy-start | bytes 3145732
  32.5 4.1 %collective-permute-start.8 = (bf16[256,2048]{1,0:T(8,128)(2,1)S(1)}, bf16[256,2048]{1,0:T(8,128)(2,1)}, u32[]{:S(2)}, u32[]{:S(2)}) collective-permute-start(bf16[256,2048]{1,0:T(8,128)(2,1)S(1)} %collective-permute-done.5.refs_10_.refs_8_.refs_17_), channel_id=1, source_target_pairs={{0,4},{4,0},{8,12},{12,8},{16,20},{20,16},{24,28},{28,24},{1,5},{5... | collective-permute-start | bytes 3145736 | tf_op jit(solution)/shard_map/ppermute | solution.py:320
  32.9 13.2 %collective-permute-start.9 = (bf16[64,2048]{1,0:T(8,128)(2,1)S(1)}, bf16[64,2048]{1,0:T(8,128)(2,1)}, u32[]{:S(2)}, u32[]{:S(2)}) collective-permute-start(bf16[64,2048]{1,0:T(8,128)(2,1)S(1)} %copy-done.2), channel_id=1, source_target_pairs={{0,1},{1,0},{2,3},{3,2},{4,5},{5,4},{6,7},{7,6},{8,9},{9,8},{10,11... | collective-permute-start | bytes 786440 | tf_op jit(solution)/shard_map/ppermute | solution.py:320
  33.6 13.3 %collective-permute-start.10 = (bf16[64,2048]{1,0:T(8,128)(2,1)}, bf16[64,2048]{1,0:T(8,128)(2,1)}, u32[]{:S(2)}, u32[]{:S(2)}) collective-permute-start(bf16[64,2048]{1,0:T(8,128)(2,1)} %collective-permute-done.6.refs_4_.refs_14_), channel_id=1, source_target_pairs={{0,1},{1,0},{2,3},{3,2},{4,5},{5,4},{6,7},{7,6},{8,9},{9,8},{10,11... | collective-permute-start | bytes 786440 | tf_op jit(solution)/shard_map/ppermute | solution.py:320
  35.0 1.6 %copy-start.10 = (bf16[256,2048]{1,0:T(8,128)(2,1)}, bf16[256,2048]{1,0:T(8,128)(2,1)S(1)}, u32[]{:S(2)}) copy-start(bf16[256,2048]{1,0:T(8,128)(2,1)S(1)} %collective-permute-done.7.refs_11_.refs_9_.refs_18_) | copy-start | bytes 3145732
  46.9 3.6 %collective-permute-start.11 = (f32[1,320]{1,0:T(1,128)S(1)}, f32[1,320]{1,0:T(1,128)S(1)}, u32[]{:S(2)}, u32[]{:S(2)}) collective-permute-start(f32[1,320]{1,0:T(1,128)S(1)} %get-tuple-element.55), channel_id=1, source_target_pairs={{0,1},{1,0},{2,3},{3,2},{4,5},{5,4},{6,7},{7,6},{8,9},{9,8},{10,11... | collective-permute-start | bytes 3848 | tf_op jit(solution)/shard_map/ppermute | solution.py:320
  50.7 8.8 %collective-permute-start.12 = (bf16[64,2048]{1,0:T(8,128)(2,1)}, bf16[64,2048]{1,0:T(8,128)(2,1)S(1)}, u32[]{:S(2)}, u32[]{:S(2)}) collective-permute-start(bf16[64,2048]{1,0:T(8,128)(2,1)} %get-tuple-element.56), channel_id=1, source_target_pairs={{0,1},{1,0},{2,3},{3,2},{4,5},{5,4},{6,7},{7,6},{8,9},{9,8},{10,11... | collective-permute-start | bytes 786440 | tf_op jit(solution)/shard_map/ppermute | solution.py:320
  52.0 7.6 %copy-start.14 = (bf16[64,2048]{1,0:T(8,128)(2,1)S(1)}, bf16[64,2048]{1,0:T(8,128)(2,1)}, u32[]{:S(2)}) copy-start(bf16[64,2048]{1,0:T(8,128)(2,1)} %get-tuple-element.60) | copy-start | bytes 786436
  52.0 8.1 %copy-start.18 = (bf16[64,2048]{1,0:T(8,128)(2,1)S(1)}, bf16[64,2048]{1,0:T(8,128)(2,1)}, u32[]{:S(2)}) copy-start(bf16[64,2048]{1,0:T(8,128)(2,1)} %get-tuple-element.59) | copy-start | bytes 786436
  52.0 13.0 %copy-start.17 = (f32[128]{0:T(128)S(1)}, f32[128]{0:T(128)}, u32[]{:S(2)}) copy-start(f32[128]{0:T(128)} %param.15) | copy-start | bytes 1540
  52.0 7.4 %collective-permute-start.14 = (f32[1,384]{1,0:T(1,128)S(1)}, f32[1,384]{1,0:T(1,128)S(1)}, u32[]{:S(2)}, u32[]{:S(2)}) collective-permute-start(f32[1,384]{1,0:T(1,128)S(1)} %pad_maximum_fusion.1), channel_id=1, source_target_pairs={{0,2},{1,3},{2,0},{3,1},{4,6},{5,7},{6,4},{7,5},{8,10},{9,11},{10,... | collective-permute-start | bytes 4616 | tf_op jit(solution)/shard_map/ppermute | solution.py:320
  59.6 12.5 %collective-permute-start.15 = (bf16[64,2048]{1,0:T(8,128)(2,1)S(1)}, bf16[64,2048]{1,0:T(8,128)(2,1)S(1)}, u32[]{:S(2)}, u32[]{:S(2)}) collective-permute-start(bf16[64,2048]{1,0:T(8,128)(2,1)S(1)} %add_convert_fusion.4), channel_id=1, source_target_pairs={{0,2},{1,3},{2,0},{3,1},{4,6},{5,7},{6,4},{7,5},{8,10},{9,11},{10,... | collective-permute-start | bytes 786440 | tf_op jit(solution)/shard_map/ppermute | solution.py:320
  60.1 12.1 %collective-permute-start.13 = (bf16[64,2048]{1,0:T(8,128)(2,1)S(1)}, bf16[64,2048]{1,0:T(8,128)(2,1)S(1)}, u32[]{:S(2)}, u32[]{:S(2)}) collective-permute-start(bf16[64,2048]{1,0:T(8,128)(2,1)S(1)} %copy-done.18), channel_id=1, source_target_pairs={{0,1},{1,0},{2,3},{3,2},{4,5},{5,4},{6,7},{7,6},{8,9},{9,8},{10,11... | collective-permute-start | bytes 786440 | tf_op jit(solution)/shard_map/ppermute | solution.py:320
  61.7 3.4 %collective-permute-start.17 = (f32[1,512]{1,0:T(1,128)S(1)}, f32[1,512]{1,0:T(1,128)S(1)}, u32[]{:S(2)}, u32[]{:S(2)}) collective-permute-start(f32[1,512]{1,0:T(1,128)S(1)} %pad_maximum_fusion.refs_2_), channel_id=1, source_target_pairs={{4,8},{12,16},{20,24},{8,4},{16,12},{24,20},{5,9},{13,17},{21,25},... | collective-permute-start | bytes 6152 | tf_op jit(solution)/shard_map/ppermute | solution.py:492
  62.3 3.5 %collective-permute-start.16 = (f32[1,512]{1,0:T(1,128)S(1)}, f32[1,512]{1,0:T(1,128)S(1)}, u32[]{:S(2)}, u32[]{:S(2)}) collective-permute-start(f32[1,512]{1,0:T(1,128)S(1)} %pad_maximum_fusion.refs_2_), channel_id=1, source_target_pairs={{0,4},{4,0},{8,12},{12,8},{16,20},{20,16},{24,28},{28,24},{1,5},{5... | collective-permute-start | bytes 6152 | tf_op jit(solution)/shard_map/ppermute | solution.py:320
  72.2 4.5 %collective-permute-start.21 = (bf16[512,2048]{1,0:T(8,128)(2,1)S(1)}, bf16[512,2048]{1,0:T(8,128)(2,1)S(1)}, u32[]{:S(2)}, u32[]{:S(2)}) collective-permute-start(bf16[512,2048]{1,0:T(8,128)(2,1)S(1)} %get-tuple-element.79), channel_id=1, source_target_pairs={{0,4},{4,0},{8,12},{12,8},{16,20},{20,16},{24,28},{28,24},{1,5},{5... | collective-permute-start | bytes 6291464 | tf_op jit(solution)/shard_map/ppermute | solution.py:320
  77.1 18.1 %copy-start.1 = (bf16[64,2048]{1,0:T(8,128)(2,1)S(1)}, bf16[64,2048]{1,0:T(8,128)(2,1)}, u32[]{:S(2)}) copy-start(bf16[64,2048]{1,0:T(8,128)(2,1)} %x_ref.1) | copy-start | bytes 786436
  77.1 18.1 %copy-start.11 = (bf16[64,2048]{1,0:T(8,128)(2,1)S(1)}, bf16[64,2048]{1,0:T(8,128)(2,1)}, u32[]{:S(2)}) copy-start(bf16[64,2048]{1,0:T(8,128)(2,1)} %get-tuple-element.49) | copy-start | bytes 786436
  77.1 14.9 %collective-permute-start.22 = (bf16[256,2048]{1,0:T(8,128)(2,1)S(1)}, bf16[256,2048]{1,0:T(8,128)(2,1)S(1)}, u32[]{:S(2)}, u32[]{:S(2)}) collective-permute-start(bf16[256,2048]{1,0:T(8,128)(2,1)S(1)} %add_convert_fusion), channel_id=1, source_target_pairs={{0,8},{4,20},{8,0},{12,28},{16,24},{20,4},{24,16},{28,12},{1,9},{5... | collective-permute-start | bytes 3145736 | tf_op jit(solution)/shard_map/ppermute | solution.py:325
  78.9 9.2 %collective-permute-start.18 = (bf16[64,2048]{1,0:T(8,128)(2,1)S(1)}, bf16[64,2048]{1,0:T(8,128)(2,1)S(1)}, u32[]{:S(2)}, u32[]{:S(2)}) collective-permute-start(bf16[64,2048]{1,0:T(8,128)(2,1)S(1)} %get-tuple-element.73), channel_id=1, source_target_pairs={{0,1},{1,0},{2,3},{3,2},{4,5},{5,4},{6,7},{7,6},{8,9},{9,8},{10,11... | collective-permute-start | bytes 786440 | tf_op jit(solution)/shard_map/ppermute | solution.py:320
  88.1 13.7 %collective-permute-start.19 = (bf16[64,2048]{1,0:T(8,128)(2,1)S(1)}, bf16[64,2048]{1,0:T(8,128)(2,1)S(1)}, u32[]{:S(2)}, u32[]{:S(2)}) collective-permute-start(bf16[64,2048]{1,0:T(8,128)(2,1)S(1)} %get-tuple-element.74), channel_id=1, source_target_pairs={{0,1},{1,0},{2,3},{3,2},{4,5},{5,4},{6,7},{7,6},{8,9},{9,8},{10,11... | collective-permute-start | bytes 786440 | tf_op jit(solution)/shard_map/ppermute | solution.py:320
  88.6 15.1 %collective-permute-start.20 = (bf16[64,2048]{1,0:T(8,128)(2,1)S(1)}, bf16[64,2048]{1,0:T(8,128)(2,1)S(1)}, u32[]{:S(2)}, u32[]{:S(2)}) collective-permute-start(bf16[64,2048]{1,0:T(8,128)(2,1)S(1)} %add_convert_fusion.2), channel_id=1, source_target_pairs={{0,2},{1,3},{2,0},{3,1},{4,6},{5,7},{6,4},{7,5},{8,10},{9,11},{10,... | collective-permute-start | bytes 786440 | tf_op jit(solution)/shard_map/ppermute | solution.py:320
  92.2 10.1 %collective-permute-start.23 = (bf16[128,2048]{1,0:T(8,128)(2,1)S(1)}, bf16[128,2048]{1,0:T(8,128)(2,1)S(1)}, u32[]{:S(2)}, u32[]{:S(2)}) collective-permute-start(bf16[128,2048]{1,0:T(8,128)(2,1)S(1)} %add_convert_fusion.1), channel_id=1, source_target_pairs={{0,16},{4,12},{8,24},{12,4},{16,0},{20,28},{24,8},{28,20},{1,17},{... | collective-permute-start | bytes 1572872 | tf_op jit(solution)/shard_map/ppermute | solution.py:325
  101.8 1.9 %copy-start.3 = (bf16[64,2048]{1,0:T(8,128)(2,1)S(1)}, bf16[64,2048]{1,0:T(8,128)(2,1)}, u32[]{:S(2)}) copy-start(bf16[64,2048]{1,0:T(8,128)(2,1)} %upstream.1) | copy-start | bytes 786436

commit v7 on v6

--- a/solution.py
+++ b/solution.py
@@ -160,7 +160,7 @@
 
     keep_at, send_at = slots(core), slots(1 - core)
 
-    @loop(nj, 4)
+    @loop(nj)
     def _(j):
         for which, (left, right) in enumerate(pairs):
             for k in range(kb):

time: 105 us -> 105 us (level)
  transfers between devices with their start and end apart: 24 -> 24, of which waited for: 14 -> 15; matrix products, arithmetic and copies ran while one was open for 3% -> 3% of each run, Pallas kernels for 22% -> 22%
where the time goes in v7:
time: 105 us
  waiting for transfers between devices  39.2 us (37%)
  starting transfers between devices  34.6 us (33%)
  Pallas kernels  24.2 us (23%)
  local copies, waits for them, and re-layouts  3.46 us (3%)
  other arithmetic  2.12 us (2%)
    ppermute x18, waiting for transfers between devices, swap(): return lax.ppermute(value, axis, [(i, i ^ mask) for i in range(n)])  37.4 us
    ppermute x18, starting transfers between devices, swap(): return lax.ppermute(value, axis, [(i, i ^ mask) for i in range(n)])  25.5 us
    pallas_call x7, Pallas kernels, call(): pl.pallas_call(body, out_shape=[pltpu.HBM(o.shape, o.dtype) if m is HBM e...  24.2 us
    ppermute x5, starting transfers between devices, swap_tok(): lax.ppermute(value, 'tok', [(i, i ^ (odd if i & 1 else even)) for i in ra...  8.42 us
  transfers between devices with their start and end apart: 24, of which 15 were waited for; matrix products, arithmetic and copies ran while one was open for 3% of the time, Pallas kernels for 22%

profile of v7, /device:TPU:0, one launch (start us, length us, event | category | flops | bytes accessed | tf_op | source)
XLA Modules:
  0.0 104.5 jit_solution(14645005030443196752)
XLA Ops:
  0.6 0.0 copy-start.2
  0.6 4.1 %collective-permute-start.1 = (bf16[64,2048]{1,0:T(8,128)(2,1)}, bf16[64,2048]{1,0:T(8,128)(2,1)S(1)}, u32[]{:S(2)}, u32[]{:S(2)}) collective-permute-start(bf16[64,2048]{1,0:T(8,128)(2,1)} %x_ref.1), channel_id=1, source_target_pairs={{0,2},{1,3},{2,0},{3,1},{4,6},{5,7},{6,4},{7,5},{8,10},{9,11},{10,... | collective-permute-start | bytes 786440 | tf_op jit(solution)/shard_map/ppermute | solution.py:320
  4.7 1.6 %collective-permute-start = (bf16[64,2048]{1,0:T(8,128)(2,1)}, bf16[64,2048]{1,0:T(8,128)(2,1)S(1)}, u32[]{:S(2)}, u32[]{:S(2)}) collective-permute-start(bf16[64,2048]{1,0:T(8,128)(2,1)} %x_ref.1), channel_id=1, source_target_pairs={{0,1},{1,0},{2,3},{3,2},{4,5},{5,4},{6,7},{7,6},{8,9},{9,8},{10,11... | collective-permute-start | bytes 786440 | tf_op jit(solution)/shard_map/ppermute | solution.py:320
  6.3 0.9 copy-done.4
  7.3 0.9 copy-done.5
  8.3 1.6 %collective-permute-start.3 = (bf16[64,2048]{1,0:T(8,128)(2,1)S(1)}, bf16[64,2048]{1,0:T(8,128)(2,1)S(1)}, u32[]{:S(2)}, u32[]{:S(2)}) collective-permute-start(bf16[64,2048]{1,0:T(8,128)(2,1)S(1)} %copy-done.4), channel_id=1, source_target_pairs={{0,8},{4,20},{8,0},{12,28},{16,24},{20,4},{24,16},{28,12},{1,9},{5... | collective-permute-start | bytes 786440 | tf_op jit(solution)/shard_map/ppermute | solution.py:325
  9.8 0.5 collective-permute-start.4
  10.4 6.6 %collective-permute-done.1.refs_4_ = bf16[64,2048]{1,0:T(8,128)(2,1)S(1)} collective-permute-done((bf16[64,2048]{1,0:T(8,128)(2,1)}, bf16[64,2048]{1,0:T(8,128)(2,1)S(1)}, u32[]{:S(2)}, u32[]{:S(2)}) %collective-permute-start.1) | collective-permute-done | bytes 262176 | tf_op jit(solution)/shard_map/ppermute | solution.py:320
  17.0 0.2 collective-permute-done.refs_3_
  17.2 0.3 collective-permute-done.4.refs_2_
  17.5 0.1 shard_map.121.refs_9_.refs_7_.refs_16_
  17.6 1.6 %collective-permute-start.5 = (bf16[256,2048]{1,0:T(8,128)(2,1)S(1)}, bf16[256,2048]{1,0:T(8,128)(2,1)S(1)}, u32[]{:S(2)}, u32[]{:S(2)}) collective-permute-start(bf16[256,2048]{1,0:T(8,128)(2,1)S(1)} %shard_map.121.refs_9_.refs_7_.refs_16_), channel_id=1, source_target_pairs={{0,16},{4,12},{8,24},{12,4},{16,0},{20,28},{24,8},{28,20},{1,17},{... | collective-permute-start | bytes 3145736 | tf_op jit(solution)/shard_map/ppermute | solution.py:325
  19.2 1.0 collective-permute-start.6
  20.2 2.4 %collective-permute-start.2 = (bf16[64,2048]{1,0:T(8,128)(2,1)S(1)}, bf16[64,2048]{1,0:T(8,128)(2,1)S(1)}, u32[]{:S(2)}, u32[]{:S(2)}) collective-permute-start(bf16[64,2048]{1,0:T(8,128)(2,1)S(1)} %collective-permute-done.1.refs_4_), channel_id=1, source_target_pairs={{0,1},{1,0},{2,3},{3,2},{4,5},{5,4},{6,7},{7,6},{8,9},{9,8},{10,11... | collective-permute-start | bytes 786440 | tf_op jit(solution)/shard_map/ppermute | solution.py:320
  22.7 9.6 %collective-permute-done.6.refs_4_.refs_14_ = bf16[64,2048]{1,0:T(8,128)(2,1)} collective-permute-done((bf16[64,2048]{1,0:T(8,128)(2,1)S(1)}, bf16[64,2048]{1,0:T(8,128)(2,1)}, u32[]{:S(2)}, u32[]{:S(2)}) %collective-permute-start.6) | collective-permute-done | bytes 262176 | tf_op jit(solution)/shard_map/ppermute | solution.py:320
  32.3 0.2 collective-permute-done.5.refs_10_.refs_8_.refs_17_
  32.5 0.4 collective-permute-start.8
  32.9 0.7 collective-permute-start.9
  33.6 1.3 %collective-permute-start.10 = (bf16[64,2048]{1,0:T(8,128)(2,1)}, bf16[64,2048]{1,0:T(8,128)(2,1)}, u32[]{:S(2)}, u32[]{:S(2)}) collective-permute-start(bf16[64,2048]{1,0:T(8,128)(2,1)} %collective-permute-done.6.refs_4_.refs_14_), channel_id=1, source_target_pairs={{0,1},{1,0},{2,3},{3,2},{4,5},{5,4},{6,7},{7,6},{8,9},{9,8},{10,11... | collective-permute-start | bytes 786440 | tf_op jit(solution)/shard_map/ppermute | solution.py:320
  34.9 0.1 copy.13.refs_0_.idx
  35.0 1.6 %collective-permute-done.8.refs_12_.refs_10_.refs_19_ = bf16[256,2048]{1,0:T(8,128)(2,1)} collective-permute-done((bf16[256,2048]{1,0:T(8,128)(2,1)S(1)}, bf16[256,2048]{1,0:T(8,128)(2,1)}, u32[]{:S(2)}, u32[]{:S(2)}) %collective-permute-start.8) | collective-permute-done | bytes 1048608 | tf_op jit(solution)/shard_map/ppermute | solution.py:320
  36.6 9.4 %shard_map.122 = (bf16[16,256,128]{2,1,0:T(8,128)(2,1)}, bf16[16,256,128]{2,1,0:T(8,128)(2,1)}, bf16[16,256,128]{2,1,0:T(8,128)(2,1)}, f32[1,320]{1,0:T(1,128)S(...) custom-call(s32[16,4]{1,0:T(8,128)S(1)} %copy.13.refs_0_.idx, ...), custom_call_target="tpu_custom_call" | custom-call | flops 1073741824 | bytes 4195584 | tf_op jit(solution)/shard_map/pallas_call | solution.py:288
  46.1 0.9 collective-permute-done.10.refs_5_.refs_15_
  46.9 1.2 %collective-permute-start.11 = (f32[1,320]{1,0:T(1,128)S(1)}, f32[1,320]{1,0:T(1,128)S(1)}, u32[]{:S(2)}, u32[]{:S(2)}) collective-permute-start(f32[1,320]{1,0:T(1,128)S(1)} %get-tuple-element.55), channel_id=1, source_target_pairs={{0,1},{1,0},{2,3},{3,2},{4,5},{5,4},{6,7},{7,6},{8,9},{9,8},{10,11... | collective-permute-start | bytes 3848 | tf_op jit(solution)/shard_map/ppermute | solution.py:320
  48.1 2.4 %collective-permute-done.11 = f32[1,320]{1,0:T(1,128)S(1)} collective-permute-done((f32[1,320]{1,0:T(1,128)S(1)}, f32[1,320]{1,0:T(1,128)S(1)}, u32[]{:S(2)}, u32[]{:S(2)}) %collective-permute-start.11) | collective-permute-done | bytes 1312 | tf_op jit(solution)/shard_map/ppermute | solution.py:320
  50.5 0.1 reshape.39
  50.6 0.1 reshape.40
  50.7 1.2 %collective-permute-start.12 = (bf16[64,2048]{1,0:T(8,128)(2,1)}, bf16[64,2048]{1,0:T(8,128)(2,1)S(1)}, u32[]{:S(2)}, u32[]{:S(2)}) collective-permute-start(bf16[64,2048]{1,0:T(8,128)(2,1)} %get-tuple-element.56), channel_id=1, source_target_pairs={{0,1},{1,0},{2,3},{3,2},{4,5},{5,4},{6,7},{7,6},{8,9},{9,8},{10,11... | collective-permute-start | bytes 786440 | tf_op jit(solution)/shard_map/ppermute | solution.py:320
  51.9 0.1 pad_maximum_fusion.1
  52.0 2.7 %collective-permute-start.14 = (f32[1,384]{1,0:T(1,128)S(1)}, f32[1,384]{1,0:T(1,128)S(1)}, u32[]{:S(2)}, u32[]{:S(2)}) collective-permute-start(f32[1,384]{1,0:T(1,128)S(1)} %pad_maximum_fusion.1), channel_id=1, source_target_pairs={{0,2},{1,3},{2,0},{3,1},{4,6},{5,7},{6,4},{7,5},{8,10},{9,11},{10,... | collective-permute-start | bytes 4616 | tf_op jit(solution)/shard_map/ppermute | solution.py:320
  54.7 4.7 %shard_map.123 = (bf16[16,256,128]{2,1,0:T(8,128)(2,1)}, f32[1,2048]{1,0:T(1,128)S(1)}) custom-call(s32[16,4]{1,0:T(8,128)S(1)} %copy.13.refs_0_.idx, s32[1]{0:T(128)} %bitcast.refs_1_, bf16[64,2048]{1,0:T(8,128)(2,1)} %upstream.1, bf16[64,2048]{1,0:T(8,128)(2,1)} %collective-permute-done.9.refs_3_.refs_13_, ...), custom_call_target="tpu_custom_call" | custom-call | flops 536870912 | bytes 1056768 | tf_op jit(solution)/shard_map/pallas_call | solution.py:288
  59.5 0.1 pad_maximum_fusion.refs_2_
  59.6 0.1 add_convert_fusion.4
  59.6 0.4 collective-permute-start.15
  60.1 1.6 %collective-permute-start.13 = (bf16[64,2048]{1,0:T(8,128)(2,1)S(1)}, bf16[64,2048]{1,0:T(8,128)(2,1)S(1)}, u32[]{:S(2)}, u32[]{:S(2)}) collective-permute-start(bf16[64,2048]{1,0:T(8,128)(2,1)S(1)} %copy-done.18), channel_id=1, source_target_pairs={{0,1},{1,0},{2,3},{3,2},{4,5},{5,4},{6,7},{7,6},{8,9},{9,8},{10,11... | collective-permute-start | bytes 786440 | tf_op jit(solution)/shard_map/ppermute | solution.py:320
  61.7 0.6 collective-permute-start.17
  62.3 2.7 %collective-permute-start.16 = (f32[1,512]{1,0:T(1,128)S(1)}, f32[1,512]{1,0:T(1,128)S(1)}, u32[]{:S(2)}, u32[]{:S(2)}) collective-permute-start(f32[1,512]{1,0:T(1,128)S(1)} %pad_maximum_fusion.refs_2_), channel_id=1, source_target_pairs={{0,4},{4,0},{8,12},{12,8},{16,20},{20,16},{24,28},{28,24},{1,5},{5... | collective-permute-start | bytes 6152 | tf_op jit(solution)/shard_map/ppermute | solution.py:320
  65.0 0.1 copy.16.refs_5_
  65.1 0.7 collective-permute-done.16.refs_3_
  65.8 6.1 %shard_map.124 = (f32[64,128]{1,0:T(8,128)S(1)}, bf16[16,256,128]{2,1,0:T(8,128)(2,1)S(1)}, bf16[512,2048]{1,0:T(8,128)(2,1)S(1)}, bf16[512,2048]{1,0:T(8,128)(2,1)S(1)}, bf16[512,2048]{1,0:T(8,128)(2,1)S(1)}) custom-call(s32[16,4]{1,0:T(8,128)S(1)} %copy.13.refs_0_.idx, s32[1]{0:T(128)} %bitcast.refs_1_, f32[1,512]{1,0:T(1,128)S(1)} %pad_maximum_fusion.refs_2_, ...), custom_call_target="tpu_custom_call" | custom-call | flops 1073741824 | bytes 7372800 | tf_op jit(solution)/shard_map/pallas_call | solution.py:288
  71.9 0.2 collective-permute-done.15
  72.2 0.5 collective-permute-start.21
  72.7 2.8 %shard_map.125 = (bf16[64,2048]{1,0:T(8,128)(2,1)S(1)}, bf16[64,2048]{1,0:T(8,128)(2,1)S(1)}, bf16[64,2048]{1,0:T(8,128)(2,1)S(1)}, bf16[64,2048]{1,0:T(8,128)(2,1)S(1)}) custom-call(s32[16,4]{1,0:T(8,128)S(1)} %copy.13.refs_0_.idx, bf16[16,256,128]{2,1,0:T(8,128)(2,1)S(1)} %get-tuple-element.69.pre_grad, bf16[512,2048]{1,0:T(8,128)(2,1)S(1)} %get-tuple-element.70.win), custom_call_target="tpu_custom_call" | custom-call | flops 536870912 | bytes 1048576 | tf_op jit(solution)/shard_map/pallas_call | solution.py:288
  75.5 1.0 collective-permute-done.21
  76.4 0.4 add_convert_fusion
  76.8 0.0 copy-start.1
  76.8 0.0 copy-start.11
  76.9 1.8 %collective-permute-start.22 = (bf16[256,2048]{1,0:T(8,128)(2,1)S(1)}, bf16[256,2048]{1,0:T(8,128)(2,1)S(1)}, u32[]{:S(2)}, u32[]{:S(2)}) collective-permute-start(bf16[256,2048]{1,0:T(8,128)(2,1)S(1)} %add_convert_fusion), channel_id=1, source_target_pairs={{0,8},{4,20},{8,0},{12,28},{16,24},{20,4},{24,16},{28,12},{1,9},{5... | collective-permute-start | bytes 3145736 | tf_op jit(solution)/shard_map/ppermute | solution.py:325
  78.7 0.6 collective-permute-start.18
  79.3 8.5 %collective-permute-done.18 = bf16[64,2048]{1,0:T(8,128)(2,1)S(1)} collective-permute-done((bf16[64,2048]{1,0:T(8,128)(2,1)S(1)}, bf16[64,2048]{1,0:T(8,128)(2,1)S(1)}, u32[]{:S(2)}, u32[]{:S(2)}) %collective-permute-start.18) | collective-permute-done | bytes 262176 | tf_op jit(solution)/shard_map/ppermute | solution.py:320
  87.8 0.5 collective-permute-start.19
  88.3 0.1 add_convert_fusion.2
  88.4 2.6 %collective-permute-start.20 = (bf16[64,2048]{1,0:T(8,128)(2,1)S(1)}, bf16[64,2048]{1,0:T(8,128)(2,1)S(1)}, u32[]{:S(2)}, u32[]{:S(2)}) collective-permute-start(bf16[64,2048]{1,0:T(8,128)(2,1)S(1)} %add_convert_fusion.2), channel_id=1, source_target_pairs={{0,2},{1,3},{2,0},{3,1},{4,6},{5,7},{6,4},{7,5},{8,10},{9,11},{10,... | collective-permute-start | bytes 786440 | tf_op jit(solution)/shard_map/ppermute | solution.py:320
  90.9 0.8 collective-permute-done.22
  91.7 0.2 add_convert_fusion.1
  92.0 2.9 %collective-permute-start.23 = (bf16[128,2048]{1,0:T(8,128)(2,1)S(1)}, bf16[128,2048]{1,0:T(8,128)(2,1)S(1)}, u32[]{:S(2)}, u32[]{:S(2)}) collective-permute-start(bf16[128,2048]{1,0:T(8,128)(2,1)S(1)} %add_convert_fusion.1), channel_id=1, source_target_pairs={{0,16},{4,12},{8,24},{12,4},{16,0},{20,28},{24,8},{28,20},{1,17},{... | collective-permute-start | bytes 1572872 | tf_op jit(solution)/shard_map/ppermute | solution.py:325
  94.9 0.8 add_convert_fusion.3
  95.7 5.7 %collective-permute-done.19 = bf16[64,2048]{1,0:T(8,128)(2,1)S(1)} collective-permute-done((bf16[64,2048]{1,0:T(8,128)(2,1)S(1)}, bf16[64,2048]{1,0:T(8,128)(2,1)S(1)}, u32[]{:S(2)}, u32[]{:S(2)}) %collective-permute-start.19) | collective-permute-done | bytes 262176 | tf_op jit(solution)/shard_map/ppermute | solution.py:320
  101.5 0.1 convert_add_fusion.1.own
  101.5 0.0 copy-start.3
  101.6 0.5 collective-permute-done.23
  102.1 0.3 convert_add_fusion
  102.4 1.0 fusion
  103.4 1.1 %shard_map.126 = bf16[64,2048]{1,0:T(8,128)(2,1)} custom-call(bf16[64,2048]{1,0:T(8,128)(2,1)S(1)} %copy-done.1, f32[1,2048]{1,0:T(1,128)S(1)} %bitcast.12, bf16[64,2048]{1,0:T(8,128)(2,1)S(1)} %copy-done.3, f32[1,2048]{1,0:T(1,128)S(1)} %bitcast.10, f32[64,128]{1,0:T(8,128)S(1)} %get-tuple-element.67.own_coeff, f32[64,2048]{1,0:T(8,128)S(1)} %convert_add_fusion.1.own, ...), custom_call_target="tpu_custom_call" | custom-call | flops 131072 | bytes 262144 | tf_op jit(solution)/shard_map/pallas_call | solution.py:288
  (52 shorter events, 0.2 us)
Async XLA Ops:
  0.6 18.6 %copy-start.2 = (bf16[64,2048]{1,0:T(8,128)(2,1)S(1)}, bf16[64,2048]{1,0:T(8,128)(2,1)}, u32[]{:S(2)}) copy-start(bf16[64,2048]{1,0:T(8,128)(2,1)} %upstream.1) | copy-start | bytes 786436
  0.6 16.3 %collective-permute-start.1 = (bf16[64,2048]{1,0:T(8,128)(2,1)}, bf16[64,2048]{1,0:T(8,128)(2,1)S(1)}, u32[]{:S(2)}, u32[]{:S(2)}) collective-permute-start(bf16[64,2048]{1,0:T(8,128)(2,1)} %x_ref.1), channel_id=1, source_target_pairs={{0,2},{1,3},{2,0},{3,1},{4,6},{5,7},{6,4},{7,5},{8,10},{9,11},{10,... | collective-permute-start | bytes 786440 | tf_op jit(solution)/shard_map/ppermute | solution.py:320
  4.7 12.4 %collective-permute-start = (bf16[64,2048]{1,0:T(8,128)(2,1)}, bf16[64,2048]{1,0:T(8,128)(2,1)S(1)}, u32[]{:S(2)}, u32[]{:S(2)}) collective-permute-start(bf16[64,2048]{1,0:T(8,128)(2,1)} %x_ref.1), channel_id=1, source_target_pairs={{0,1},{1,0},{2,3},{3,2},{4,5},{5,4},{6,7},{7,6},{8,9},{9,8},{10,11... | collective-permute-start | bytes 786440 | tf_op jit(solution)/shard_map/ppermute | solution.py:320
  6.3 0.9 copy-start.4
  7.3 0.9 copy-start.5
  8.2 26.7 %copy-start.16 = (s32[16,4]{0,1:T(4,128)S(1)}, s32[16,4]{0,1:T(4,128)}, u32[]{:S(2)}) copy-start(s32[16,4]{0,1:T(4,128)} %param.13) | copy-start | bytes 772
  8.2 28.4 %copy-start.6 = (f32[2048]{0:T(1024)S(1)}, f32[2048]{0:T(1024)}, u32[]{:S(2)}) copy-start(f32[2048]{0:T(1024)} %param.17) | copy-start | bytes 24580
  8.2 28.4 %copy-start.7 = (f32[2048]{0:T(1024)S(1)}, f32[2048]{0:T(1024)}, u32[]{:S(2)}) copy-start(f32[2048]{0:T(1024)} %param.10) | copy-start | bytes 24580
  8.2 28.4 %copy-start.8 = (s32[64]{0:T(128)S(1)}, s32[64]{0:T(128)}, u32[]{:S(2)}) copy-start(s32[64]{0:T(128)} %param.14) | copy-start | bytes 772
  8.3 8.9 %collective-permute-start.3 = (bf16[64,2048]{1,0:T(8,128)(2,1)S(1)}, bf16[64,2048]{1,0:T(8,128)(2,1)S(1)}, u32[]{:S(2)}, u32[]{:S(2)}) collective-permute-start(bf16[64,2048]{1,0:T(8,128)(2,1)S(1)} %copy-done.4), channel_id=1, source_target_pairs={{0,8},{4,20},{8,0},{12,28},{16,24},{20,4},{24,16},{28,12},{1,9},{5... | collective-permute-start | bytes 786440 | tf_op jit(solution)/shard_map/ppermute | solution.py:325
  9.8 7.7 %collective-permute-start.4 = (bf16[64,2048]{1,0:T(8,128)(2,1)S(1)}, bf16[64,2048]{1,0:T(8,128)(2,1)S(1)}, u32[]{:S(2)}, u32[]{:S(2)}) collective-permute-start(bf16[64,2048]{1,0:T(8,128)(2,1)S(1)} %copy-done.5), channel_id=1, source_target_pairs={{0,8},{4,20},{8,0},{12,28},{16,24},{20,4},{24,16},{28,12},{1,9},{5... | collective-permute-start | bytes 786440 | tf_op jit(solution)/shard_map/ppermute | solution.py:325
  17.0 16.6 %copy-start.12 = (bf16[64,2048]{1,0:T(8,128)(2,1)}, bf16[64,2048]{1,0:T(8,128)(2,1)S(1)}, u32[]{:S(2)}) copy-start(bf16[64,2048]{1,0:T(8,128)(2,1)S(1)} %collective-permute-done.1.refs_4_) | copy-start | bytes 786436
  17.2 17.7 %copy-start.13 = (bf16[64,2048]{1,0:T(8,128)(2,1)}, bf16[64,2048]{1,0:T(8,128)(2,1)S(1)}, u32[]{:S(2)}) copy-start(bf16[64,2048]{1,0:T(8,128)(2,1)S(1)} %collective-permute-done.refs_3_) | copy-start | bytes 786436
  17.6 19.0 %copy-start = (bf16[256,2048]{1,0:T(8,128)(2,1)}, bf16[256,2048]{1,0:T(8,128)(2,1)S(1)}, u32[]{:S(2)}) copy-start(bf16[256,2048]{1,0:T(8,128)(2,1)S(1)} %shard_map.121.refs_9_.refs_7_.refs_16_) | copy-start | bytes 3145732
  17.6 14.9 %collective-permute-start.5 = (bf16[256,2048]{1,0:T(8,128)(2,1)S(1)}, bf16[256,2048]{1,0:T(8,128)(2,1)S(1)}, u32[]{:S(2)}, u32[]{:S(2)}) collective-permute-start(bf16[256,2048]{1,0:T(8,128)(2,1)S(1)} %shard_map.121.refs_9_.refs_7_.refs_16_), channel_id=1, source_target_pairs={{0,16},{4,12},{8,24},{12,4},{16,0},{20,28},{24,8},{28,20},{1,17},{... | collective-permute-start | bytes 3145736 | tf_op jit(solution)/shard_map/ppermute | solution.py:325
  19.2 13.1 %collective-permute-start.6 = (bf16[64,2048]{1,0:T(8,128)(2,1)S(1)}, bf16[64,2048]{1,0:T(8,128)(2,1)}, u32[]{:S(2)}, u32[]{:S(2)}) collective-permute-start(bf16[64,2048]{1,0:T(8,128)(2,1)S(1)} %copy-done.2), channel_id=1, source_target_pairs={{0,2},{1,3},{2,0},{3,1},{4,6},{5,7},{6,4},{7,5},{8,10},{9,11},{10,... | collective-permute-start | bytes 786440 | tf_op jit(solution)/shard_map/ppermute | solution.py:320
  20.2 12.1 %collective-permute-start.2 = (bf16[64,2048]{1,0:T(8,128)(2,1)S(1)}, bf16[64,2048]{1,0:T(8,128)(2,1)S(1)}, u32[]{:S(2)}, u32[]{:S(2)}) collective-permute-start(bf16[64,2048]{1,0:T(8,128)(2,1)S(1)} %collective-permute-done.1.refs_4_), channel_id=1, source_target_pairs={{0,1},{1,0},{2,3},{3,2},{4,5},{5,4},{6,7},{7,6},{8,9},{9,8},{10,11... | collective-permute-start | bytes 786440 | tf_op jit(solution)/shard_map/ppermute | solution.py:320
  32.3 2.7 %collective-permute-start.7 = (bf16[256,2048]{1,0:T(8,128)(2,1)S(1)}, bf16[256,2048]{1,0:T(8,128)(2,1)S(1)}, u32[]{:S(2)}, u32[]{:S(2)}) collective-permute-start(bf16[256,2048]{1,0:T(8,128)(2,1)S(1)} %shard_map.121.refs_9_.refs_7_.refs_16_), channel_id=1, source_target_pairs={{0,4},{4,0},{8,12},{12,8},{16,20},{20,16},{24,28},{28,24},{1,5},{5... | collective-permute-start | bytes 3145736 | tf_op jit(solution)/shard_map/ppermute | solution.py:320
  32.3 2.6 %copy-start.15 = (bf16[64,2048]{1,0:T(8,128)(2,1)}, bf16[64,2048]{1,0:T(8,128)(2,1)S(1)}, u32[]{:S(2)}) copy-start(bf16[64,2048]{1,0:T(8,128)(2,1)S(1)} %collective-permute-done.2.refs_5_) | copy-start | bytes 786436
  32.5 4.1 %copy-start.9 = (bf16[256,2048]{1,0:T(8,128)(2,1)}, bf16[256,2048]{1,0:T(8,128)(2,1)S(1)}, u32[]{:S(2)}) copy-start(bf16[256,2048]{1,0:T(8,128)(2,1)S(1)} %collective-permute-done.5.refs_10_.refs_8_.refs_17_) | copy-start | bytes 3145732
  32.5 4.1 %collective-permute-start.8 = (bf16[256,2048]{1,0:T(8,128)(2,1)S(1)}, bf16[256,2048]{1,0:T(8,128)(2,1)}, u32[]{:S(2)}, u32[]{:S(2)}) collective-permute-start(bf16[256,2048]{1,0:T(8,128)(2,1)S(1)} %collective-permute-done.5.refs_10_.refs_8_.refs_17_), channel_id=1, source_target_pairs={{0,4},{4,0},{8,12},{12,8},{16,20},{20,16},{24,28},{28,24},{1,5},{5... | collective-permute-start | bytes 3145736 | tf_op jit(solution)/shard_map/ppermute | solution.py:320
  32.9 13.2 %collective-permute-start.9 = (bf16[64,2048]{1,0:T(8,128)(2,1)S(1)}, bf16[64,2048]{1,0:T(8,128)(2,1)}, u32[]{:S(2)}, u32[]{:S(2)}) collective-permute-start(bf16[64,2048]{1,0:T(8,128)(2,1)S(1)} %copy-done.2), channel_id=1, source_target_pairs={{0,1},{1,0},{2,3},{3,2},{4,5},{5,4},{6,7},{7,6},{8,9},{9,8},{10,11... | collective-permute-start | bytes 786440 | tf_op jit(solution)/shard_map/ppermute | solution.py:320
  33.6 13.3 %collective-permute-start.10 = (bf16[64,2048]{1,0:T(8,128)(2,1)}, bf16[64,2048]{1,0:T(8,128)(2,1)}, u32[]{:S(2)}, u32[]{:S(2)}) collective-permute-start(bf16[64,2048]{1,0:T(8,128)(2,1)} %collective-permute-done.6.refs_4_.refs_14_), channel_id=1, source_target_pairs={{0,1},{1,0},{2,3},{3,2},{4,5},{5,4},{6,7},{7,6},{8,9},{9,8},{10,11... | collective-permute-start | bytes 786440 | tf_op jit(solution)/shard_map/ppermute | solution.py:320
  35.0 1.6 %copy-start.10 = (bf16[256,2048]{1,0:T(8,128)(2,1)}, bf16[256,2048]{1,0:T(8,128)(2,1)S(1)}, u32[]{:S(2)}) copy-start(bf16[256,2048]{1,0:T(8,128)(2,1)S(1)} %collective-permute-done.7.refs_11_.refs_9_.refs_18_) | copy-start | bytes 3145732
  46.9 3.6 %collective-permute-start.11 = (f32[1,320]{1,0:T(1,128)S(1)}, f32[1,320]{1,0:T(1,128)S(1)}, u32[]{:S(2)}, u32[]{:S(2)}) collective-permute-start(f32[1,320]{1,0:T(1,128)S(1)} %get-tuple-element.55), channel_id=1, source_target_pairs={{0,1},{1,0},{2,3},{3,2},{4,5},{5,4},{6,7},{7,6},{8,9},{9,8},{10,11... | collective-permute-start | bytes 3848 | tf_op jit(solution)/shard_map/ppermute | solution.py:320
  50.7 8.8 %collective-permute-start.12 = (bf16[64,2048]{1,0:T(8,128)(2,1)}, bf16[64,2048]{1,0:T(8,128)(2,1)S(1)}, u32[]{:S(2)}, u32[]{:S(2)}) collective-permute-start(bf16[64,2048]{1,0:T(8,128)(2,1)} %get-tuple-element.56), channel_id=1, source_target_pairs={{0,1},{1,0},{2,3},{3,2},{4,5},{5,4},{6,7},{7,6},{8,9},{9,8},{10,11... | collective-permute-start | bytes 786440 | tf_op jit(solution)/shard_map/ppermute | solution.py:320
  52.0 7.6 %copy-start.14 = (bf16[64,2048]{1,0:T(8,128)(2,1)S(1)}, bf16[64,2048]{1,0:T(8,128)(2,1)}, u32[]{:S(2)}) copy-start(bf16[64,2048]{1,0:T(8,128)(2,1)} %get-tuple-element.60) | copy-start | bytes 786436
  52.0 8.1 %copy-start.18 = (bf16[64,2048]{1,0:T(8,128)(2,1)S(1)}, bf16[64,2048]{1,0:T(8,128)(2,1)}, u32[]{:S(2)}) copy-start(bf16[64,2048]{1,0:T(8,128)(2,1)} %get-tuple-element.59) | copy-start | bytes 786436
  52.0 13.0 %copy-start.17 = (f32[128]{0:T(128)S(1)}, f32[128]{0:T(128)}, u32[]{:S(2)}) copy-start(f32[128]{0:T(128)} %param.15) | copy-start | bytes 1540
  52.0 7.4 %collective-permute-start.14 = (f32[1,384]{1,0:T(1,128)S(1)}, f32[1,384]{1,0:T(1,128)S(1)}, u32[]{:S(2)}, u32[]{:S(2)}) collective-permute-start(f32[1,384]{1,0:T(1,128)S(1)} %pad_maximum_fusion.1), channel_id=1, source_target_pairs={{0,2},{1,3},{2,0},{3,1},{4,6},{5,7},{6,4},{7,5},{8,10},{9,11},{10,... | collective-permute-start | bytes 4616 | tf_op jit(solution)/shard_map/ppermute | solution.py:320
  59.6 12.5 %collective-permute-start.15 = (bf16[64,2048]{1,0:T(8,128)(2,1)S(1)}, bf16[64,2048]{1,0:T(8,128)(2,1)S(1)}, u32[]{:S(2)}, u32[]{:S(2)}) collective-permute-start(bf16[64,2048]{1,0:T(8,128)(2,1)S(1)} %add_convert_fusion.4), channel_id=1, source_target_pairs={{0,2},{1,3},{2,0},{3,1},{4,6},{5,7},{6,4},{7,5},{8,10},{9,11},{10,... | collective-permute-start | bytes 786440 | tf_op jit(solution)/shard_map/ppermute | solution.py:320
  60.1 12.1 %collective-permute-start.13 = (bf16[64,2048]{1,0:T(8,128)(2,1)S(1)}, bf16[64,2048]{1,0:T(8,128)(2,1)S(1)}, u32[]{:S(2)}, u32[]{:S(2)}) collective-permute-start(bf16[64,2048]{1,0:T(8,128)(2,1)S(1)} %copy-done.18), channel_id=1, source_target_pairs={{0,1},{1,0},{2,3},{3,2},{4,5},{5,4},{6,7},{7,6},{8,9},{9,8},{10,11... | collective-permute-start | bytes 786440 | tf_op jit(solution)/shard_map/ppermute | solution.py:320
  61.7 3.4 %collective-permute-start.17 = (f32[1,512]{1,0:T(1,128)S(1)}, f32[1,512]{1,0:T(1,128)S(1)}, u32[]{:S(2)}, u32[]{:S(2)}) collective-permute-start(f32[1,512]{1,0:T(1,128)S(1)} %pad_maximum_fusion.refs_2_), channel_id=1, source_target_pairs={{4,8},{12,16},{20,24},{8,4},{16,12},{24,20},{5,9},{13,17},{21,25},... | collective-permute-start | bytes 6152 | tf_op jit(solution)/shard_map/ppermute | solution.py:492
  62.3 3.5 %collective-permute-start.16 = (f32[1,512]{1,0:T(1,128)S(1)}, f32[1,512]{1,0:T(1,128)S(1)}, u32[]{:S(2)}, u32[]{:S(2)}) collective-permute-start(f32[1,512]{1,0:T(1,128)S(1)} %pad_maximum_fusion.refs_2_), channel_id=1, source_target_pairs={{0,4},{4,0},{8,12},{12,8},{16,20},{20,16},{24,28},{28,24},{1,5},{5... | collective-permute-start | bytes 6152 | tf_op jit(solution)/shard_map/ppermute | solution.py:320
  72.2 4.3 %collective-permute-start.21 = (bf16[512,2048]{1,0:T(8,128)(2,1)S(1)}, bf16[512,2048]{1,0:T(8,128)(2,1)S(1)}, u32[]{:S(2)}, u32[]{:S(2)}) collective-permute-start(bf16[512,2048]{1,0:T(8,128)(2,1)S(1)} %get-tuple-element.79), channel_id=1, source_target_pairs={{0,4},{4,0},{8,12},{12,8},{16,20},{20,16},{24,28},{28,24},{1,5},{5... | collective-permute-start | bytes 6291464 | tf_op jit(solution)/shard_map/ppermute | solution.py:320
  76.8 18.1 %copy-start.1 = (bf16[64,2048]{1,0:T(8,128)(2,1)S(1)}, bf16[64,2048]{1,0:T(8,128)(2,1)}, u32[]{:S(2)}) copy-start(bf16[64,2048]{1,0:T(8,128)(2,1)} %x_ref.1) | copy-start | bytes 786436
  76.8 18.1 %copy-start.11 = (bf16[64,2048]{1,0:T(8,128)(2,1)S(1)}, bf16[64,2048]{1,0:T(8,128)(2,1)}, u32[]{:S(2)}) copy-start(bf16[64,2048]{1,0:T(8,128)(2,1)} %get-tuple-element.49) | copy-start | bytes 786436
  76.9 14.9 %collective-permute-start.22 = (bf16[256,2048]{1,0:T(8,128)(2,1)S(1)}, bf16[256,2048]{1,0:T(8,128)(2,1)S(1)}, u32[]{:S(2)}, u32[]{:S(2)}) collective-permute-start(bf16[256,2048]{1,0:T(8,128)(2,1)S(1)} %add_convert_fusion), channel_id=1, source_target_pairs={{0,8},{4,20},{8,0},{12,28},{16,24},{20,4},{24,16},{28,12},{1,9},{5... | collective-permute-start | bytes 3145736 | tf_op jit(solution)/shard_map/ppermute | solution.py:325
  78.7 9.2 %collective-permute-start.18 = (bf16[64,2048]{1,0:T(8,128)(2,1)S(1)}, bf16[64,2048]{1,0:T(8,128)(2,1)S(1)}, u32[]{:S(2)}, u32[]{:S(2)}) collective-permute-start(bf16[64,2048]{1,0:T(8,128)(2,1)S(1)} %get-tuple-element.73), channel_id=1, source_target_pairs={{0,1},{1,0},{2,3},{3,2},{4,5},{5,4},{6,7},{7,6},{8,9},{9,8},{10,11... | collective-permute-start | bytes 786440 | tf_op jit(solution)/shard_map/ppermute | solution.py:320
  87.8 13.7 %collective-permute-start.19 = (bf16[64,2048]{1,0:T(8,128)(2,1)S(1)}, bf16[64,2048]{1,0:T(8,128)(2,1)S(1)}, u32[]{:S(2)}, u32[]{:S(2)}) collective-permute-start(bf16[64,2048]{1,0:T(8,128)(2,1)S(1)} %get-tuple-element.74), channel_id=1, source_target_pairs={{0,1},{1,0},{2,3},{3,2},{4,5},{5,4},{6,7},{7,6},{8,9},{9,8},{10,11... | collective-permute-start | bytes 786440 | tf_op jit(solution)/shard_map/ppermute | solution.py:320
  88.4 15.1 %collective-permute-start.20 = (bf16[64,2048]{1,0:T(8,128)(2,1)S(1)}, bf16[64,2048]{1,0:T(8,128)(2,1)S(1)}, u32[]{:S(2)}, u32[]{:S(2)}) collective-permute-start(bf16[64,2048]{1,0:T(8,128)(2,1)S(1)} %add_convert_fusion.2), channel_id=1, source_target_pairs={{0,2},{1,3},{2,0},{3,1},{4,6},{5,7},{6,4},{7,5},{8,10},{9,11},{10,... | collective-permute-start | bytes 786440 | tf_op jit(solution)/shard_map/ppermute | solution.py:320
  92.0 10.1 %collective-permute-start.23 = (bf16[128,2048]{1,0:T(8,128)(2,1)S(1)}, bf16[128,2048]{1,0:T(8,128)(2,1)S(1)}, u32[]{:S(2)}, u32[]{:S(2)}) collective-permute-start(bf16[128,2048]{1,0:T(8,128)(2,1)S(1)} %add_convert_fusion.1), channel_id=1, source_target_pairs={{0,16},{4,12},{8,24},{12,4},{16,0},{20,28},{24,8},{28,20},{1,17},{... | collective-permute-start | bytes 1572872 | tf_op jit(solution)/shard_map/ppermute | solution.py:325
  101.5 1.9 %copy-start.3 = (bf16[64,2048]{1,0:T(8,128)(2,1)S(1)}, bf16[64,2048]{1,0:T(8,128)(2,1)}, u32[]{:S(2)}) copy-start(bf16[64,2048]{1,0:T(8,128)(2,1)} %upstream.1) | copy-start | bytes 786436
